TPU v7x, 32 devices: a whole 2x2x4 slice. The times are simulated.
32 devices in a mesh: seq: 32 (over z, y, x, core).
Axes of the slice: x: 2, y: 2, z: 4, core: 2. Of those that a mesh axis runs over, the one named last changes fastest.
Arguments:
- tokens: bfloat16 [16384, 1024], P('seq'), may hold values from -128 to 128, as said below
- w_query: bfloat16 [1024, 1024], replicated, may hold values from -0.1875 to 0.1875
- w_key: bfloat16 [1024, 256], replicated, may hold values from -0.1875 to 0.1875
- w_value: bfloat16 [1024, 256], replicated, may hold values from -0.1875 to 0.1875
- w_out: bfloat16 [1024, 1024], replicated, may hold values from -0.1875 to 0.1875
Outputs:
- attended: bfloat16 [16384, 1024], P('seq')
Inputs may be any that keep to these rules, and one draw needn't show every extreme that they name: `tokens`: Real-valued activations.
All inputs are finite; a program needn't handle non-finite values.
Results may differ from a plain program's by a relative error of at most 0.007.
The roundings to bfloat16 on the way count: a program that leaves them out, or rounds other values in their place, can miss the bound.
Values may be sent and summed in bfloat16 or wider, within the bound.
No kernel may reach another device: no remote copies, remote signals or barrier semaphores. Data moves between devices by JAX's collectives and lax.ppermute only.
A program may use at most 128 MiB of HBM per device.

v0:
```python
import math

import jax
import jax.numpy as jnp
from jax import lax
from jax.sharding import PartitionSpec as P

HEADS = 16
KV_HEADS = 4
HEAD_DIM = 64
BLOCK = 256
POOL = 16
GROUP = 16


def extended(cells, sides, width):
    for axis, dim in sides:
        count = lax.axis_size(axis)
        ends = count - 1
        head = lax.slice_in_dim(cells, 0, width, axis=dim)
        tail = lax.slice_in_dim(cells, cells.shape[dim] - width, cells.shape[dim], axis=dim)
        cells = jnp.concatenate(
            [
                lax.ppermute(tail, axis, [(i, (i + 1) % count) for i in range(ends)]),
                cells,
                lax.ppermute(head, axis, [((i + 1) % count, i) for i in range(ends)]),
            ],
            axis=dim,
        )
    return cells


def from_partner(block, axis, apart):
    count = lax.axis_size(axis)
    route = []
    for low in range(count):
        high = low | 1 << apart
        if high != low and high < count:
            route += [(low, high), (high, low)]
    return lax.ppermute(block, axis, route)


def pool_rows(source, factor):
    width = source.shape[-1]
    grouped = source.astype(jnp.float32).reshape(-1, factor, width)
    return jnp.mean(grouped, axis=1).astype(jnp.bfloat16)


def usable_rows(block_index, my_group, all_blocks, group_tokens, group_summaries):
    near = block_index - 1 + jnp.arange(3 * BLOCK, dtype=jnp.int32) // BLOCK
    near_usable = (near >= 0) & (near < all_blocks)
    middle_blocks = (
        (my_group * group_summaries + jnp.arange(group_summaries, dtype=jnp.int32)) * POOL // BLOCK
    )
    middle_usable = jnp.abs(middle_blocks - block_index) > 1
    coarse_blocks = jnp.arange(all_blocks, dtype=jnp.int32)
    coarse_usable = (coarse_blocks * BLOCK // group_tokens != my_group) & (
        jnp.abs(coarse_blocks - block_index) > 1
    )
    return jnp.concatenate([near_usable, middle_usable, coarse_usable])


def attend_block(queries, pair_rows, usable):
    span_rows = pair_rows.shape[0]
    key_width = KV_HEADS * HEAD_DIM
    key_rows = pair_rows[:, :key_width].reshape(span_rows, KV_HEADS, HEAD_DIM)
    value_rows = pair_rows[:, key_width:].reshape(span_rows, KV_HEADS, HEAD_DIM)
    shaped = queries.reshape(-1, KV_HEADS, HEADS // KV_HEADS, HEAD_DIM)
    scores = jnp.einsum("qkgd,lkd->kgql", shaped, key_rows, preferred_element_type=jnp.float32) * (
        1.0 / math.sqrt(HEAD_DIM)
    )
    scores = jnp.where(usable, scores, -1e30)
    highest = jnp.max(scores, axis=-1, keepdims=True)
    weights = jnp.where(usable, jnp.exp(scores - highest), 0.0)
    totals = jnp.sum(weights, axis=-1)
    probabilities = weights.astype(jnp.bfloat16)
    weighted = jnp.einsum(
        "kgql,lkd->qkgd", probabilities, value_rows, preferred_element_type=jnp.float32
    )
    weighted = weighted / jnp.transpose(totals, (2, 0, 1))[..., None]
    return weighted.reshape(queries.shape[0], HEADS * HEAD_DIM).astype(jnp.bfloat16)


def body(tokens, w_query, w_key, w_value, w_out):
    devices = lax.axis_size("seq")
    my_index = lax.axis_index("seq")
    tok_rows = tokens.shape[0]
    block_count = tok_rows // BLOCK
    all_blocks = block_count * devices
    group_tokens = GROUP * tok_rows
    group_summaries = group_tokens // POOL
    queries = jnp.dot(tokens, w_query, preferred_element_type=jnp.float32).astype(jnp.bfloat16)
    key_rows = jnp.dot(tokens, w_key, preferred_element_type=jnp.float32).astype(jnp.bfloat16)
    value_rows = jnp.dot(tokens, w_value, preferred_element_type=jnp.float32).astype(jnp.bfloat16)
    pair_rows = jnp.concatenate([key_rows, value_rows], axis=1)
    padded = extended(pair_rows, (("seq", 0),), BLOCK)
    middle = pool_rows(pair_rows, POOL)
    coarse = pool_rows(pair_rows, BLOCK)
    my_group = my_index // GROUP
    group_mid = middle
    for level in range(GROUP.bit_length() - 1):
        partner = from_partner(group_mid, "seq", level)
        upper = my_index // 2**level % 2
        group_mid = jnp.where(
            upper == 1,
            jnp.concatenate([partner, group_mid], axis=0),
            jnp.concatenate([group_mid, partner], axis=0),
        )
    coarse_all = lax.all_gather(coarse, "seq", axis=0, tiled=True)

    def per_block(local_block):
        block_index = my_index * block_count + local_block
        near_rows = lax.dynamic_slice_in_dim(padded, local_block * BLOCK, 3 * BLOCK, 0)
        block_queries = lax.dynamic_slice_in_dim(queries, local_block * BLOCK, BLOCK, 0)
        gathered = jnp.concatenate([near_rows, group_mid, coarse_all], axis=0)
        usable = usable_rows(block_index, my_group, all_blocks, group_tokens, group_summaries)
        return attend_block(block_queries, gathered, usable)

    mixed = lax.map(per_block, jnp.arange(block_count, dtype=jnp.int32)).reshape(
        tok_rows, HEADS * HEAD_DIM
    )
    return jnp.dot(mixed, w_out, preferred_element_type=jnp.float32).astype(jnp.bfloat16)


def solution(mesh):
    placed = (P("seq", None), P(), P(), P(), P())
    return jax.shard_map(
        body, mesh=mesh, in_specs=placed, out_specs=P("seq", None), check_vma=False
    )
```

profile of v0, /device:TPU:0, one launch (start us, length us, event | category | flops | bytes accessed | tf_op | source)
XLA Modules:
  0.0 137.6 jit_solution(3340363011334243942)
XLA Ops:
  0.0 1.9 %convolution_convert_fusion.3 = bf16[512,256]{1,0:T(8,128)(2,1)S(1)} fusion(bf16[512,1024]{1,0:T(8,128)(2,1)} %param.7, bf16[1024,256]{1,0:T(8,128)(2,1)} %param.9), kind=kOutput, calls=%fused_computation.55 | convolution fusion | flops 268566528 | bytes 1835008 | tf_op jit(solution)/shard_map/dot_general | solution.py:93
  2.0 1.8 %convolution_convert_fusion.2 = bf16[512,256]{1,0:T(8,128)(2,1)S(1)} fusion(bf16[512,1024]{1,0:T(8,128)(2,1)} %param.7, bf16[1024,256]{1,0:T(8,128)(2,1)} %param.10), kind=kOutput, calls=%fused_computation.54 | convolution fusion | flops 268566528 | bytes 1835008 | tf_op jit(solution)/shard_map/dot_general | solution.py:94
  3.8 0.2 convert_reduce_fusion.1
  4.0 0.5 collective-permute-start.2
  4.5 0.9 collective-permute-done.2
  5.4 2.9 %collective-permute-start.3 = (bf16[64,512]{1,0:T(8,128)(2,1)S(1)}, bf16[64,512]{1,0:T(8,128)(2,1)S(1)}, u32[]{:S(2)}, u32[]{:S(2)}) collective-permute-start(bf16[64,512]{1,0:T(8,128)(2,1)S(1)} %maximum_select_fusion.3), channel_id=1, source_target_pairs={{0,2},{2,0},{1,3},{3,1},{4,6},{6,4},{5,7},{7,5},{8,10},{10,8},{9,1... | collective-permute-start | bytes 196616 | tf_op jit(solution)/shard_map/ppermute | solution.py:40
  8.3 0.7 fusion.41
  9.0 2.5 %collective-permute-start = (bf16[256,512]{1,0:T(8,128)(2,1)}, bf16[256,512]{1,0:T(8,128)(2,1)}, u32[]{:S(2)}, u32[]{:S(2)}) collective-permute-start(bf16[256,512]{1,0:T(8,128)(2,1)} %get-tuple-element.215), channel_id=1, source_target_pairs={{0,1},{1,2},{2,3},{3,4},{4,5},{5,6},{6,7},{7,8},{8,9},{9,10},{10,1... | collective-permute-start | bytes 786440 | tf_op jit(solution)/shard_map/ppermute | solution.py:24
  11.5 1.3 collective-permute-start.1
  12.8 0.0 collective-permute-done.3
  12.9 4.3 %collective-permute-start.4 = (bf16[128,512]{1,0:T(8,128)(2,1)S(1)}, bf16[128,512]{1,0:T(8,128)(2,1)S(1)}, u32[]{:S(2)}, u32[]{:S(2)}) collective-permute-start(bf16[128,512]{1,0:T(8,128)(2,1)S(1)} %maximum_select_fusion.2), channel_id=1, source_target_pairs={{0,4},{4,0},{1,5},{5,1},{2,6},{6,2},{3,7},{7,3},{8,12},{12,8},{9,1... | collective-permute-start | bytes 393224 | tf_op jit(solution)/shard_map/ppermute | solution.py:40
  17.1 3.5 %convolution_convert_fusion.1 = bf16[512,1024]{1,0:T(8,128)(2,1)} fusion(bf16[512,1024]{1,0:T(8,128)(2,1)} %param.7, bf16[1024,1024]{1,0:T(8,128)(2,1)S(1)} %copy-done), kind=kOutput, calls=%fused_computation.53 | convolution fusion | flops 1074266112 | bytes 4194304 | tf_op jit(solution)/shard_map/dot_general | solution.py:92
  20.6 0.1 convert_reduce_fusion
  20.7 0.0 collective-permute-done.4
  20.7 0.1 maximum_select_fusion.1
  20.8 2.4 %collective-permute-start.5 = (bf16[256,512]{1,0:T(8,128)(2,1)S(1)}, bf16[256,512]{1,0:T(8,128)(2,1)}, u32[]{:S(2)}, u32[]{:S(2)}) collective-permute-start(bf16[256,512]{1,0:T(8,128)(2,1)S(1)} %maximum_select_fusion.1), channel_id=1, source_target_pairs={{0,8},{8,0},{1,9},{9,1},{2,10},{10,2},{3,11},{11,3},{4,12},{12,4},... | collective-permute-start | bytes 786440 | tf_op jit(solution)/shard_map/ppermute | solution.py:40
  23.2 42.1 %all-gather = bf16[32,2,512]{2,1,0:T(2,128)(2,1)S(1)} all-gather(bf16[1,2,512]{2,1,0:T(2,128)(2,1)S(1)} %fusion.42), channel_id=1, replica_groups=mesh['seq'=32] {'seq'}, dimensions={0}, use_global_device_ids=true | all-gather | bytes 67584 | tf_op jit(solution)/shard_map/all_gather | solution.py:109
  65.3 0.1 copy.14
  65.5 0.0 collective-permute-done
  65.5 0.0 collective-permute-done.1
  65.5 2.1 %pad_maximum_fusion.1 = bf16[1024,512]{1,0:T(8,128)(2,1)} fusion(bf16[256,512]{1,0:T(8,128)(2,1)} %collective-permute-done.1, bf16[512,256]{1,0:T(8,128)(2,1)S(1)} %convolution_convert_fusion.2, bf16[512,256]{1,0:T(8,128)(2,1)S(1)} %convolution_convert_fusion.3, bf16[256,512]{1,0:T(8,128)(2,1)} %collective-permute-done), kind=kLoop, calls=%fused_computation.56 | loop fusion | flops 4194304 | bytes 2097152 | tf_op jit(solution)/shard_map/concatenate | solution.py:22
  67.6 0.0 collective-permute-done.5
  67.6 1.2 maximum_select_fusion
  68.7 0.2 copy.13
  69.0 64.5 %while.13 = (s32[]{:T(128)}, bf16[2,256,1024]{2,1,0:T(8,128)(2,1)}, s32[2]{0:T(128)S(1)}, bf16[1024,512]{1,0:T(8,128)(2,1)}, bf16[512,512]{0,1:T(8,128)(2,1)S(1)...) while((s32[]{:T(128)}, bf16[2,256,1024]{2,1,0:T(8,128)(2,1)}, ...), condition=%wide.region_5.6_spmd, body=%wide.region_2.5_spmd.sunk | while | flops 2173662720 | bytes 19275128 | solution.py:119
  69.2 0.6 dynamic_slice.29
  70.4 1.2 constant_dynamic-slice_fusion.4
  71.6 1.2 copy.26
  72.8 1.2 pad_maximum_fusion.4
  74.1 1.2 fusion.75
  75.3 1.1 constant_dynamic-slice_fusion.5
  76.3 1.0 copy.27
  78.0 9.7 %fusion.78 = f32[4,4,256]{2,1,0:T(4,128)S(1)} fusion(pred[1344]{0:T(1024)(128)(4,1)S(1)} %pad_add_fusion.2, bf16[1344,4,64,1]{0,2,3,1:T(8,128)(2,1)} %bitcast.78, bf16[256,4,4,64]{0,3,2,1:T(8,128)(2,1)} %bitcast.81), kind=kOutput, calls=%fused_computation.6.clone.1 | convolution fusion | flops 732169536 | bytes 1230144 | tf_op jit(solution)/shard_map/while/body/eval_jaxpr/sub | solution.py:74
  87.8 11.4 %divide_convert_fusion.2 = bf16[256,4,4,64]{0,3,2,1:T(8,128)(2,1)} fusion(bf16[1344,4,64,1]{0,2,3,1:T(8,128)(2,1)S(1)} %bitcast.80, pred[1344]{0:T(1024)(128)(4,1)S(1)} %pad_add_fusion.2, bf16[1344,4,64,1]{0,2,3,1:T(8,128)(2,1)} %bitcast.79, bf16[256,4,4,64]{0,3,2,1:T(8,128)(2,1)} %bitcast.82, f32[256,4,4]{0,2,1:T(4,128)S(1)} %bitcast.89), kind=kOutput, calls=%fused_computation.13.clone.1 | convolution fusion | flops 1437340928 | bytes 2442560 | tf_op jit(solution)/shard_map/while/body/eval_jaxpr/kgql,lkd->qkgd/dot_general | solution.py:77
  99.2 1.2 copy.28
  100.5 0.9 constant_dynamic-update-slice_fusion.2
  101.3 0.6 dynamic_slice.29
  102.6 1.2 constant_dynamic-slice_fusion.4
  103.8 1.2 copy.26
  105.0 1.2 pad_maximum_fusion.4
  106.2 1.2 fusion.75
  107.4 1.1 constant_dynamic-slice_fusion.5
  108.5 1.0 copy.27
  110.2 9.7 %fusion.78 = f32[4,4,256]{2,1,0:T(4,128)S(1)} fusion(pred[1344]{0:T(1024)(128)(4,1)S(1)} %pad_add_fusion.2, bf16[1344,4,64,1]{0,2,3,1:T(8,128)(2,1)} %bitcast.78, bf16[256,4,4,64]{0,3,2,1:T(8,128)(2,1)} %bitcast.81), kind=kOutput, calls=%fused_computation.6.clone.1 | convolution fusion | flops 732169536 | bytes 1230144 | tf_op jit(solution)/shard_map/while/body/eval_jaxpr/sub | solution.py:74
  119.9 11.4 %divide_convert_fusion.2 = bf16[256,4,4,64]{0,3,2,1:T(8,128)(2,1)} fusion(bf16[1344,4,64,1]{0,2,3,1:T(8,128)(2,1)S(1)} %bitcast.80, pred[1344]{0:T(1024)(128)(4,1)S(1)} %pad_add_fusion.2, bf16[1344,4,64,1]{0,2,3,1:T(8,128)(2,1)} %bitcast.79, bf16[256,4,4,64]{0,3,2,1:T(8,128)(2,1)} %bitcast.82, f32[256,4,4]{0,2,1:T(4,128)S(1)} %bitcast.89), kind=kOutput, calls=%fused_computation.13.clone.1 | convolution fusion | flops 1437340928 | bytes 2442560 | tf_op jit(solution)/shard_map/while/body/eval_jaxpr/kgql,lkd->qkgd/dot_general | solution.py:77
  131.4 1.2 copy.28
  132.6 0.9 constant_dynamic-update-slice_fusion.2
  133.5 4.1 %convolution_convert_fusion = bf16[512,1024]{1,0:T(8,128)(2,1)} fusion(bf16[512,1024]{1,0:T(8,128)(2,1)} %bitcast.88, bf16[1024,1024]{1,0:T(8,128)(2,1)} %param.11), kind=kOutput, calls=%fused_computation.52 | convolution fusion | flops 1074266112 | bytes 4194304 | tf_op jit(solution)/shard_map/dot_general | solution.py:122
  (21 shorter events, 0.2 us)
Async XLA Ops:
  0.0 17.1 %copy-start = (bf16[1024,1024]{1,0:T(8,128)(2,1)S(1)}, bf16[1024,1024]{1,0:T(8,128)(2,1)}, u32[]{:S(2)}) copy-start(bf16[1024,1024]{1,0:T(8,128)(2,1)} %param.8) | copy-start | bytes 6291460
  4.0 1.4 %collective-permute-start.2 = (bf16[32,512]{1,0:T(8,128)(2,1)S(1)}, bf16[32,512]{1,0:T(8,128)(2,1)S(1)}, u32[]{:S(2)}, u32[]{:S(2)}) collective-permute-start(bf16[32,512]{1,0:T(8,128)(2,1)S(1)} %multiply_convert_fusion), channel_id=1, source_target_pairs={{0,1},{1,0},{2,3},{3,2},{4,5},{5,4},{6,7},{7,6},{8,9},{9,8},{10,11... | collective-permute-start | bytes 98312 | tf_op jit(solution)/shard_map/ppermute | solution.py:40
  5.4 7.4 %collective-permute-start.3 = (bf16[64,512]{1,0:T(8,128)(2,1)S(1)}, bf16[64,512]{1,0:T(8,128)(2,1)S(1)}, u32[]{:S(2)}, u32[]{:S(2)}) collective-permute-start(bf16[64,512]{1,0:T(8,128)(2,1)S(1)} %maximum_select_fusion.3), channel_id=1, source_target_pairs={{0,2},{2,0},{1,3},{3,1},{4,6},{6,4},{5,7},{7,5},{8,10},{10,8},{9,1... | collective-permute-start | bytes 196616 | tf_op jit(solution)/shard_map/ppermute | solution.py:40
  9.0 56.5 %collective-permute-start = (bf16[256,512]{1,0:T(8,128)(2,1)}, bf16[256,512]{1,0:T(8,128)(2,1)}, u32[]{:S(2)}, u32[]{:S(2)}) collective-permute-start(bf16[256,512]{1,0:T(8,128)(2,1)} %get-tuple-element.215), channel_id=1, source_target_pairs={{0,1},{1,2},{2,3},{3,4},{4,5},{5,6},{6,7},{7,8},{8,9},{9,10},{10,1... | collective-permute-start | bytes 786440 | tf_op jit(solution)/shard_map/ppermute | solution.py:24
  11.5 54.0 %collective-permute-start.1 = (bf16[256,512]{1,0:T(8,128)(2,1)S(1)}, bf16[256,512]{1,0:T(8,128)(2,1)}, u32[]{:S(2)}, u32[]{:S(2)}) collective-permute-start(bf16[256,512]{1,0:T(8,128)(2,1)S(1)} %get-tuple-element.216), channel_id=1, source_target_pairs={{1,0},{2,1},{3,2},{4,3},{5,4},{6,5},{7,6},{8,7},{9,8},{10,9},{11,1... | collective-permute-start | bytes 786440 | tf_op jit(solution)/shard_map/ppermute | solution.py:26
  12.9 7.8 %collective-permute-start.4 = (bf16[128,512]{1,0:T(8,128)(2,1)S(1)}, bf16[128,512]{1,0:T(8,128)(2,1)S(1)}, u32[]{:S(2)}, u32[]{:S(2)}) collective-permute-start(bf16[128,512]{1,0:T(8,128)(2,1)S(1)} %maximum_select_fusion.2), channel_id=1, source_target_pairs={{0,4},{4,0},{1,5},{5,1},{2,6},{6,2},{3,7},{7,3},{8,12},{12,8},{9,1... | collective-permute-start | bytes 393224 | tf_op jit(solution)/shard_map/ppermute | solution.py:40
  20.8 46.8 %collective-permute-start.5 = (bf16[256,512]{1,0:T(8,128)(2,1)S(1)}, bf16[256,512]{1,0:T(8,128)(2,1)}, u32[]{:S(2)}, u32[]{:S(2)}) collective-permute-start(bf16[256,512]{1,0:T(8,128)(2,1)S(1)} %maximum_select_fusion.1), channel_id=1, source_target_pairs={{0,8},{8,0},{1,9},{9,1},{2,10},{10,2},{3,11},{11,3},{4,12},{12,4},... | collective-permute-start | bytes 786440 | tf_op jit(solution)/shard_map/ppermute | solution.py:40
  78.0 9.7 %copy-start.1 = (bf16[1344,256]{0,1:T(8,128)(2,1)S(1)}, bf16[1344,256]{0,1:T(8,128)(2,1)}, u32[]{:S(2)}) copy-start(bf16[1344,256]{0,1:T(8,128)(2,1)} %get-tuple-element.280) | copy-start | bytes 2064388 | tf_op jit(solution)/shard_map/while
  110.2 9.7 %copy-start.1 = (bf16[1344,256]{0,1:T(8,128)(2,1)S(1)}, bf16[1344,256]{0,1:T(8,128)(2,1)}, u32[]{:S(2)}) copy-start(bf16[1344,256]{0,1:T(8,128)(2,1)} %get-tuple-element.280) | copy-start | bytes 2064388 | tf_op jit(solution)/shard_map/while
where the time goes:
time: 138 us
  matrix products  53.7 us (39%)
  blocking collectives  42.1 us (31%)
  local copies, waits for them, and re-layouts  17.1 us (12%)
  starting transfers between devices  13.9 us (10%)
  other arithmetic  6.97 us (5%)
  loops' own time  2.85 us (2%)
    all_gather x1, blocking collectives, body(): coarse_all = lax.all_gather(coarse, 'seq', axis=0, tiled=True)  42.1 us
    dot_general x2, matrix products, attend_block(): jnp.einsum('kgql,lkd->qkgd', probabilities, value_rows, preferred_element...  22.9 us
    sub x2, matrix products, attend_block(): weights = jnp.where(usable, jnp.exp(scores - highest), 0.0)  19.4 us
    ppermute x4, starting transfers between devices, from_partner(): return lax.ppermute(block, axis, route)  10.1 us
    dynamic_slice x4, local copies, waits for them, and re-layouts, per_block(): lax.dynamic_slice_in_dim(padded, local_block * BLOCK, 3 * BLOCK, 0)  4.75 us
    dynamic_update_slice x4, local copies, waits for them, and re-layouts, body(): lax.map(per_block, jnp.arange(block_count, dtype=jnp.int32))  4.2 us
    dot_general x1, matrix products, body(): jnp.dot(mixed, w_out, preferred_element_type=jnp.float32)  4.14 us
    dynamic_slice x4, local copies, waits for them, and re-layouts, per_block(): lax.dynamic_slice_in_dim(queries, local_block * BLOCK, BLOCK, 0)  4.13 us
  transfers between devices with their start and end apart: 6, of which 1 were waited for; matrix products, arithmetic and copies ran while one was open for 5% of the time, Pallas kernels for 0%

commit v1 on v0

v1 whole, which is shorter than its diff:
```python
import functools
import math

import jax
import jax.numpy as jnp
from jax import lax
from jax.experimental import pallas as pl
from jax.experimental.pallas import tpu as pltpu
from jax.sharding import PartitionSpec as P

HEADS = 16
KV_HEADS = 4
HEAD_DIM = 64
BLOCK = 256
POOL = 16
GROUP = 16
SHARE = HEADS // KV_HEADS
WIDE = 128
VROWS = 80
BF16 = jnp.bfloat16
F32 = jnp.float32
NT = (((1,), (1,)), ((), ()))
TN = (((0,), (0,)), ((), ()))
MASKED = -1e30
HOPS = (2, 4, 8, 1)
VMEM = pl.BlockSpec(memory_space=pltpu.VMEM)


def swap(rows, apart):
    count = lax.axis_size("seq")
    return lax.ppermute(rows, "seq", [(i, i ^ apart) for i in range(count)])


def place(slot):
    return sum(hop for bit, hop in enumerate(HOPS) if slot >> bit & 1)


def project_pair(tokens_ref, wk_ref, wv_ref, pair_ref, mid_ref, coarse_ref):
    tokens = tokens_ref[...]
    rows = tokens.shape[0]
    width = wk_ref.shape[1]
    for part, weight in enumerate((wk_ref, wv_ref)):
        at = slice(part * width, (part + 1) * width)
        held = jnp.dot(tokens, weight[...], preferred_element_type=F32).astype(BF16)
        pair_ref[:, at] = held
        for factor, target in ((POOL, mid_ref), (BLOCK, coarse_ref)):
            kept = target.shape[0]
            first = lax.broadcasted_iota(jnp.int32, (kept, rows), 0) * factor
            inside = lax.broadcasted_iota(jnp.int32, (kept, rows), 1) - first
            share = jnp.where((inside >= 0) & (inside < factor), 1.0 / factor, 0.0)
            mean = jnp.dot(share.astype(BF16), held, preferred_element_type=F32)
            target[:, at] = mean.astype(BF16)


def put_keys(keys_ref, rows, at, count, bias):
    lane = lax.broadcasted_iota(jnp.int32, (count, HEAD_DIM), 1)
    extra = jnp.where(lane == 0, 0.0 if bias is None else bias, 0.0).astype(BF16)
    for head in range(KV_HEADS):
        keys_ref[head, at : at + count, :HEAD_DIM] = rows[:, head * HEAD_DIM : (head + 1) * HEAD_DIM]
        keys_ref[head, at : at + count, HEAD_DIM:] = extra


def put_values(values_ref, rows):
    width = KV_HEADS * HEAD_DIM
    count = rows.shape[0]
    tall = KV_HEADS * VROWS
    row = lax.broadcasted_iota(jnp.int32, (tall, width), 0)
    column = lax.broadcasted_iota(jnp.int32, (tall, width), 1)
    head, inner = column // HEAD_DIM, column % HEAD_DIM
    pick = jnp.where(row == head * VROWS + inner, 1.0, 0.0).astype(BF16)
    turned = lax.dot_general(pick, rows, NT, preferred_element_type=F32)
    counting = lax.broadcasted_iota(jnp.int32, (tall, count), 0) % VROWS == HEAD_DIM
    values_ref[...] = jnp.where(counting, 1.0, turned).astype(BF16).reshape(KV_HEADS, VROWS, count)


def run_units(units, scores, finish, values, even, odd):
    def first(unit, buffers):
        held, top = buffers
        x, floor = scores(unit)
        held[...] = x
        highest = jnp.max(x, axis=0, keepdims=True)
        top[...] = highest if floor is None else jnp.maximum(highest, floor)

    def second(unit, buffers):
        held, top = buffers
        highest = top[...]
        weights = jnp.exp(held[...] - highest).astype(BF16)
        finish(unit, highest, jnp.dot(values(unit), weights, preferred_element_type=F32))

    first(0, even)

    def step(i, carry):
        first(2 * i + 1, odd)
        second(2 * i, even)
        first(2 * i + 2, even)
        second(2 * i + 1, odd)
        return carry

    lax.fori_loop(0, units // 2 - 1, step, 0)
    first(units - 1, odd)
    second(units - 2, even)
    second(units - 1, odd)


def early(tokens_ref, wq_ref, pair_ref, q_ref, acc_ref, top_ref, keys_ref, values_ref, sa, ta, sb, tb):
    rows = tokens_ref.shape[0]
    blocks = rows // BLOCK
    width = KV_HEADS * HEAD_DIM
    put_keys(keys_ref, pair_ref[:, :width], 0, rows, None)
    put_values(values_ref, pair_ref[:, width:])
    lane = lax.broadcasted_iota(jnp.int32, (rows, HEAD_DIM), 1)
    extra = jnp.where(lane == 0, 1.0, 0.0).astype(BF16)
    for group in range(KV_HEADS):
        span = SHARE * HEAD_DIM
        part = jnp.dot(tokens_ref[...], wq_ref[:, group * span : (group + 1) * span], preferred_element_type=F32)
        part = part.astype(BF16) * (1.0 / math.sqrt(HEAD_DIM))
        for head in range(SHARE):
            for block in range(blocks):
                at = slice(head * BLOCK, (head + 1) * BLOCK)
                piece = part[block * BLOCK : (block + 1) * BLOCK, head * HEAD_DIM : (head + 1) * HEAD_DIM]
                q_ref[group * blocks + block, at, :HEAD_DIM] = piece
                q_ref[group * blocks + block, at, HEAD_DIM:] = extra[:BLOCK]

    def scores(unit):
        return lax.dot_general(keys_ref[unit // blocks], q_ref[unit], NT, preferred_element_type=F32), None

    def finish(unit, highest, total):
        acc_ref[unit] = total
        top_ref[unit] = highest

    run_units(KV_HEADS * blocks, scores, finish, lambda unit: values_ref[unit // blocks], (sa, ta), (sb, tb))


def late(q_ref, acc_ref, top_ref, prev_ref, next_ref, x_ref, y_ref, z_ref, c_ref, far_ref, wout_ref,
         out_ref, keys_ref, values_ref, mixed_ref, sa, ta, sb, tb):
    blocks = keys_ref.shape[0]
    width = KV_HEADS * HEAD_DIM
    me = lax.axis_index("seq")
    devices = lax.axis_size("seq")
    groups = devices // GROUP
    runs = BLOCK // POOL
    per_device = runs * blocks
    far_rows = far_ref.shape[0]
    pieces = [(far_ref, far_rows), (x_ref, per_device), (y_ref, 2 * per_device), (z_ref, 4 * per_device), (c_ref, 8 * per_device)]
    spread = blocks * (groups - 1)
    row = lax.broadcasted_iota(jnp.int32, (far_rows, HEAD_DIM), 0)
    slot = row // spread
    owner = jnp.zeros_like(row)
    for bit, hop in enumerate(HOPS):
        owner = owner + (slot // 2**bit % 2) * hop
    other = (row % spread) // blocks + 1
    far_block = (((me // GROUP) ^ other) * GROUP + ((me % GROUP) ^ owner)) * blocks + row % blocks
    mid_count = (GROUP - 1) * per_device
    row = lax.broadcasted_iota(jnp.int32, (mid_count, HEAD_DIM), 0) + per_device
    slot = row // per_device
    owner = jnp.zeros_like(row)
    for bit, hop in enumerate(HOPS):
        owner = owner + (slot // 2**bit % 2) * hop
    mid_block = (me ^ owner) * blocks + row % per_device // runs
    for block in range(blocks):
        index = me * blocks + block
        if block == 0:
            near_ref, exists = prev_ref, me > 0
        else:
            near_ref, exists = next_ref, me < devices - 1
        keys = keys_ref.at[block]
        put_keys(keys, near_ref[:, :width], 0, BLOCK, jnp.where(exists, 0.0, MASKED))
        put_keys(keys, far_ref[:, :width], BLOCK, far_rows, jnp.where(jnp.abs(far_block - index) > 1, 0.0, MASKED))
        bias = jnp.where(jnp.abs(mid_block - index) > 1, 0.0, MASKED)
        at = 0
        for piece, count in pieces[1:]:
            put_keys(keys, piece[:count, :width], BLOCK + far_rows + at, count, bias[at : at + count])
            at += count
        gathered = jnp.concatenate([near_ref[:, width:]] + [piece[:count, width:] for piece, count in pieces], axis=0)
        put_values(values_ref.at[block], gathered)

    def scores(unit):
        x = lax.dot_general(keys_ref[unit % blocks, unit // blocks], q_ref[unit], NT, preferred_element_type=F32)
        return x, top_ref[unit]

    def finish(unit, highest, total):
        total = total + acc_ref[unit] * jnp.exp(top_ref[unit] - highest)
        share = total[:HEAD_DIM] / total[HEAD_DIM : HEAD_DIM + 1]
        share = share.astype(BF16)
        for head in range(SHARE):
            at = pl.multiple_of((unit // blocks * SHARE + head) * HEAD_DIM, HEAD_DIM)
            mixed_ref[unit % blocks, pl.ds(at, HEAD_DIM), :] = share[:, head * BLOCK : (head + 1) * BLOCK]

    run_units(KV_HEADS * blocks, scores, finish, lambda unit: values_ref[unit % blocks, unit // blocks], (sa, ta), (sb, tb))
    for block in range(blocks):
        done = lax.dot_general(mixed_ref[block], wout_ref[...], TN, preferred_element_type=F32)
        out_ref[block * BLOCK : (block + 1) * BLOCK] = done.astype(BF16)


def body(tokens, w_query, w_key, w_value, w_out):
    devices = lax.axis_size("seq")
    me = lax.axis_index("seq")
    rows, model = tokens.shape
    blocks = rows // BLOCK
    pair_width = 2 * KV_HEADS * HEAD_DIM
    units = KV_HEADS * blocks
    stack = SHARE * BLOCK
    shape = jax.ShapeDtypeStruct
    params = lambda mib: pltpu.CompilerParams(vmem_limit_bytes=mib * 2**20)
    pair, mid, coarse = pl.pallas_call(
        project_pair,
        out_shape=[shape((rows, pair_width), BF16), shape((rows // POOL, pair_width), BF16), shape((blocks, pair_width), BF16)],
        in_specs=[VMEM] * 3,
        out_specs=[VMEM] * 3,
        compiler_params=params(16),
        cost_estimate=pl.CostEstimate(flops=2 * rows * model * pair_width, bytes_accessed=3 * 2**20, transcendentals=0),
        name="pair",
    )(tokens, w_key, w_value)

    groups = devices // GROUP
    before = lax.ppermute(pair[-BLOCK:], "seq", [(i, i + 1) for i in range(devices - 1)])
    after = lax.ppermute(pair[:BLOCK], "seq", [(i + 1, i) for i in range(devices - 1)])
    if groups == 2:
        spread = jnp.concatenate([swap(coarse, GROUP), swap(coarse, GROUP ^ HOPS[0])], axis=0)
    else:
        spread = coarse
        level = GROUP
        while level < devices:
            spread = jnp.concatenate([spread, swap(spread, level)], axis=0)
            level *= 2
        spread = spread[blocks:]
        spread = jnp.concatenate([spread, swap(spread, HOPS[0])], axis=0)
    held = mid
    arrived = swap(mid, HOPS[0])
    received = [arrived]
    for hop in HOPS[1:]:
        held = jnp.concatenate([held, arrived], axis=0)
        both = swap(jnp.concatenate([held, spread], axis=0), hop)
        arrived = both[: held.shape[0]]
        received.append(both)
        spread = jnp.concatenate([spread, both[held.shape[0] :]], axis=0)

    s_early = [pltpu.VMEM((rows, stack), F32), pltpu.VMEM((1, stack), F32)]
    q, acc, top = pl.pallas_call(
        early,
        out_shape=[shape((units, stack, WIDE), BF16), shape((units, VROWS, stack), F32), shape((units, 1, stack), F32)],
        in_specs=[VMEM] * 3,
        out_specs=[VMEM] * 3,
        scratch_shapes=[pltpu.VMEM((KV_HEADS, rows, WIDE), BF16), pltpu.VMEM((KV_HEADS, VROWS, rows), BF16)] + s_early + s_early,
        compiler_params=params(32),
        cost_estimate=pl.CostEstimate(flops=8 * 10**9, bytes_accessed=8 * 2**20, transcendentals=0),
        name="early",
    )(tokens, w_query, pair)

    keys = BLOCK + (GROUP - 1) * (rows // POOL) + spread.shape[0]
    s_late = [pltpu.VMEM((keys, stack), F32), pltpu.VMEM((1, stack), F32)]
    return pl.pallas_call(
        late,
        out_shape=shape((rows, w_out.shape[1]), BF16),
        in_specs=[VMEM] * 11,
        out_specs=VMEM,
        scratch_shapes=[
            pltpu.VMEM((blocks, KV_HEADS, keys, WIDE), BF16),
            pltpu.VMEM((blocks, KV_HEADS, VROWS, keys), BF16),
            pltpu.VMEM((blocks, HEADS * HEAD_DIM, BLOCK), BF16),
        ]
        + s_late
        + s_late,
        compiler_params=params(40),
        cost_estimate=pl.CostEstimate(flops=12 * 10**9, bytes_accessed=8 * 2**20, transcendentals=0),
        name="late",
    )(q, acc, top, before, after, *received, spread, w_out)


def solution(mesh):
    placed = (P("seq", None), P(), P(), P(), P())
    return jax.shard_map(body, mesh=mesh, in_specs=placed, out_specs=P("seq", None), check_vma=False)
```

time: 138 us -> 53.9 us (0.39)
  matrix products: 53.7 us -> 0 us
  blocking collectives: 42.1 us -> 0 us
  Pallas kernels: 0 us -> 19 us
  other arithmetic: 6.97 us -> 0.01 us
  waiting for transfers between devices: 0.87 us -> 7.3 us
  local copies, waits for them, and re-layouts: 17.1 us -> 12.8 us
  loops' own time: 2.85 us -> 0 us
    all_gather x1 -> x0, blocking collectives: 42.1 us -> none  [body(): coarse_all = lax.all_gather(coarse, 'seq', axis=0, tiled=True)]
    dot_general x6 -> x0, matrix products: 34.2 us -> none  [the longest x2 22.9 us: attend_block(): jnp.einsum('kgql,lkd->qkgd', probabilities, value_rows, preferred_element...]
    sub x2 -> x0, matrix products: 19.4 us -> none  [attend_block(): weights = jnp.where(usable, jnp.exp(scores - highest), 0.0)]
    pallas_call x0 -> x3, Pallas kernels: none -> 19 us  [the longest x1 10.9 us: body(): pl.pallas_call(late, out_shape=shape((rows, w_out.shape[1]), BF16), in_sp...]
    unnamed x2 -> x20, local copies, waits for them, and re-layouts: 0.01 us -> 12.6 us
    dynamic_slice x10 -> x0, local copies, waits for them, and re-layouts: 10.1 us -> none  [the longest x4 4.75 us: per_block(): lax.dynamic_slice_in_dim(padded, local_block * BLOCK, 3 * BLOCK, 0)]
    ppermute x6 -> x8, waiting for transfers between devices: 0.87 us -> 7.3 us  [the longest x6 7.29 us: swap(): return lax.ppermute(rows, 'seq', [(i, i ^ apart) for i in range(count)])]
    concatenate x6 -> x1, other arithmetic: 5.31 us -> 0.01 us  [body(): both = swap(jnp.concatenate([held, spread], axis=0), hop)]
  transfers between devices with their start and end apart: 6 -> 8, of which waited for: 1 -> 3; matrix products, arithmetic and copies ran while one was open for 5% -> 0% of each run, Pallas kernels for 0% -> 12%
where the time goes in v1:
time: 53.9 us; the launch traced here: 53.5 us
  Pallas kernels  19 us (35%)
  starting transfers between devices  14.3 us (27%)
  local copies, waits for them, and re-layouts  12.8 us (24%)
  waiting for transfers between devices  7.3 us (14%)
    unnamed x20, local copies, waits for them, and re-layouts  12.6 us
    pallas_call x1, Pallas kernels, body(): pl.pallas_call(late, out_shape=shape((rows, w_out.shape[1]), BF16), in_sp...  10.9 us
    ppermute x6, starting transfers between devices, swap(): return lax.ppermute(rows, 'seq', [(i, i ^ apart) for i in range(count)])  9.93 us
    ppermute x6, waiting for transfers between devices, swap(): return lax.ppermute(rows, 'seq', [(i, i ^ apart) for i in range(count)])  7.29 us
    pallas_call x1, Pallas kernels, body(): pl.pallas_call(early, out_shape=[shape((units, stack, WIDE), BF16), shape...  6.47 us
    ppermute x1, starting transfers between devices, body(): lax.ppermute(pair[-BLOCK:], 'seq', [(i, i + 1) for i in range(devices - 1)])  3.05 us
    pallas_call x1, Pallas kernels, body(): pl.pallas_call(project_pair, out_shape=[shape((rows, pair_width), BF16),...  1.62 us
    ppermute x1, starting transfers between devices, body(): lax.ppermute(pair[:BLOCK], 'seq', [(i + 1, i) for i in range(devices - 1)])  1.29 us
  transfers between devices with their start and end apart: 8, of which 3 were waited for; matrix products, arithmetic and copies ran while one was open for 0% of the time, Pallas kernels for 12%

profile of v1, /device:TPU:0, one launch (start us, length us, event | category | flops | bytes accessed | tf_op | source)
XLA Modules:
  0.0 53.5 jit_solution(3897173866055194948)
XLA Ops:
  0.0 0.0 copy-start
  0.0 1.2 %copy-done = bf16[512,1024]{1,0:T(8,128)(2,1)S(1)} copy-done((bf16[512,1024]{1,0:T(8,128)(2,1)S(1)}, bf16[512,1024]{1,0:T(8,128)(2,1)}, u32[]{:S(2)}) %copy-start) | copy-done | bytes 1048600
  1.2 0.0 copy-start.2
  1.2 1.0 %copy-done.2 = bf16[1024,256]{1,0:T(8,128)(2,1)S(1)} copy-done((bf16[1024,256]{1,0:T(8,128)(2,1)S(1)}, bf16[1024,256]{1,0:T(8,128)(2,1)}, u32[]{:S(2)}) %copy-start.2) | copy-done | bytes 524312
  2.3 0.0 copy-start.3
  2.3 1.0 %copy-done.3 = bf16[1024,256]{1,0:T(8,128)(2,1)S(1)} copy-done((bf16[1024,256]{1,0:T(8,128)(2,1)S(1)}, bf16[1024,256]{1,0:T(8,128)(2,1)}, u32[]{:S(2)}) %copy-start.3) | copy-done | bytes 524312
  3.3 0.0 copy-start.1
  3.3 1.6 %pair.1 = (bf16[512,512]{1,0:T(8,128)(2,1)S(1)}, bf16[32,512]{1,0:T(8,128)(2,1)S(1)}, bf16[2,512]{1,0:T(2,128)(2,1)S(1)}) custom-call(bf16[512,1024]{1,0:T(8,128)(2,1)S(1)} %copy-done, bf16[1024,256]{1,0:T(8,128)(2,1)S(1)} %copy-done.2, bf16[1024,256]{1,0:T(8,128)(2,1)S(1)} %copy-done.3), custom_call_target="tpu_custom_call" | custom-call | flops 536870912 | bytes 3145728 | tf_op jit(solution)/shard_map/pair/pallas_call | solution.py:205
  4.9 3.0 %collective-permute-start.2 = (bf16[32,512]{1,0:T(8,128)(2,1)S(1)}, bf16[32,512]{1,0:T(8,128)(2,1)S(1)}, u32[]{:S(2)}, u32[]{:S(2)}) collective-permute-start(bf16[32,512]{1,0:T(8,128)(2,1)S(1)} %get-tuple-element.15), channel_id=1, source_target_pairs={{0,2},{1,3},{2,0},{3,1},{4,6},{5,7},{6,4},{7,5},{8,10},{9,11},{10,... | collective-permute-start | bytes 98312 | tf_op jit(solution)/shard_map/ppermute | solution.py:31
  7.9 2.6 %collective-permute-start.4 = (bf16[2,512]{1,0:T(2,128)(2,1)S(1)}, bf16[2,512]{1,0:T(2,128)(2,1)S(1)}, u32[]{:S(2)}, u32[]{:S(2)}) collective-permute-start(bf16[2,512]{1,0:T(2,128)(2,1)S(1)} %get-tuple-element.16), channel_id=1, source_target_pairs={{0,18},{1,19},{2,16},{3,17},{4,22},{5,23},{6,20},{7,21},{8,26},{9,... | collective-permute-start | bytes 6152 | tf_op jit(solution)/shard_map/ppermute | solution.py:31
  10.5 0.0 collective-permute-start.3
  10.5 2.8 %collective-permute-done.4 = bf16[2,512]{1,0:T(2,128)(2,1)S(1)} collective-permute-done((bf16[2,512]{1,0:T(2,128)(2,1)S(1)}, bf16[2,512]{1,0:T(2,128)(2,1)S(1)}, u32[]{:S(2)}, u32[]{:S(2)}) %collective-permute-start.4) | collective-permute-done | bytes 2080 | tf_op jit(solution)/shard_map/ppermute | solution.py:31
  13.3 1.7 %collective-permute-done.3 = bf16[2,512]{1,0:T(2,128)(2,1)S(1)} collective-permute-done((bf16[2,512]{1,0:T(2,128)(2,1)S(1)}, bf16[2,512]{1,0:T(2,128)(2,1)S(1)}, u32[]{:S(2)}, u32[]{:S(2)}) %collective-permute-start.3) | collective-permute-done | bytes 2080 | tf_op jit(solution)/shard_map/ppermute | solution.py:31
  14.9 0.0 collective-permute-done.2.x_ref
  15.0 1.6 %collective-permute-start.5 = (bf16[68,512]{1,0:T(8,128)(2,1)S(1)}, bf16[68,512]{1,0:T(8,128)(2,1)S(1)}, u32[]{:S(2)}, u32[]{:S(2)}) collective-permute-start(bf16[68,512]{1,0:T(8,128)(2,1)S(1)} %pad_maximum_fusion), channel_id=1, source_target_pairs={{0,4},{1,5},{2,6},{3,7},{4,0},{5,1},{6,2},{7,3},{8,12},{9,13},{10,... | collective-permute-start | bytes 208904 | tf_op jit(solution)/shard_map/ppermute | solution.py:31
  16.5 2.8 %collective-permute-done.5.y_ref = bf16[68,512]{1,0:T(8,128)(2,1)S(1)} collective-permute-done((bf16[68,512]{1,0:T(8,128)(2,1)S(1)}, bf16[68,512]{1,0:T(8,128)(2,1)S(1)}, u32[]{:S(2)}, u32[]{:S(2)}) %collective-permute-start.5) | collective-permute-done | bytes 69664 | tf_op jit(solution)/shard_map/ppermute | solution.py:31
  19.4 1.6 %collective-permute-start.6 = (bf16[136,512]{1,0:T(8,128)(2,1)S(1)}, bf16[136,512]{1,0:T(8,128)(2,1)S(1)}, u32[]{:S(2)}, u32[]{:S(2)}) collective-permute-start(bf16[136,512]{1,0:T(8,128)(2,1)S(1)} %concatenate.25), channel_id=1, source_target_pairs={{0,8},{1,9},{2,10},{3,11},{4,12},{5,13},{6,14},{7,15},{8,0},{9,1},... | collective-permute-start | bytes 417800 | tf_op jit(solution)/shard_map/ppermute | solution.py:31
  21.1 1.3 %collective-permute-start.1 = (bf16[256,512]{1,0:T(8,128)(2,1)S(1)}, bf16[256,512]{1,0:T(8,128)(2,1)S(1)}, u32[]{:S(2)}, u32[]{:S(2)}) collective-permute-start(bf16[256,512]{1,0:T(8,128)(2,1)S(1)} %get-tuple-element.17), channel_id=1, source_target_pairs={{1,0},{2,1},{3,2},{4,3},{5,4},{6,5},{7,6},{8,7},{9,8},{10,9},{11,1... | collective-permute-start | bytes 786440 | tf_op jit(solution)/shard_map/ppermute | solution.py:217
  22.4 3.0 %collective-permute-start = (bf16[256,512]{1,0:T(8,128)(2,1)S(1)}, bf16[256,512]{1,0:T(8,128)(2,1)S(1)}, u32[]{:S(2)}, u32[]{:S(2)}) collective-permute-start(bf16[256,512]{1,0:T(8,128)(2,1)S(1)} %get-tuple-element.18), channel_id=1, source_target_pairs={{0,1},{1,2},{2,3},{3,4},{4,5},{5,6},{6,7},{7,8},{8,9},{9,10},{10,1... | collective-permute-start | bytes 786440 | tf_op jit(solution)/shard_map/ppermute | solution.py:216
  25.5 0.0 collective-permute-done.6.z_ref
  25.5 1.2 %collective-permute-start.7 = (bf16[272,512]{1,0:T(8,128)(2,1)S(1)}, bf16[272,512]{1,0:T(8,128)(2,1)S(1)}, u32[]{:S(2)}, u32[]{:S(2)}) collective-permute-start(bf16[272,512]{1,0:T(8,128)(2,1)S(1)} %concatenate.26), channel_id=1, source_target_pairs={{0,1},{1,0},{2,3},{3,2},{4,5},{5,4},{6,7},{7,6},{8,9},{9,8},{10,11... | collective-permute-start | bytes 835592 | tf_op jit(solution)/shard_map/ppermute | solution.py:31
  26.7 0.0 copy-done.1
  26.7 0.0 copy-start.4
  26.7 1.6 %copy-done.4 = bf16[1024,1024]{1,0:T(8,128)(2,1)S(1)} copy-done((bf16[1024,1024]{1,0:T(8,128)(2,1)S(1)}, bf16[1024,1024]{1,0:T(8,128)(2,1)}, u32[]{:S(2)}) %copy-start.4) | copy-done | bytes 2097176
  28.3 6.5 %early.1 = (bf16[8,1024,128]{2,1,0:T(8,128)(2,1)S(1)}, f32[8,80,1024]{2,1,0:T(8,128)S(1)}, f32[8,1,1024]{2,1,0:T(1,128)S(1)}) custom-call(bf16[512,1024]{1,0:T(8,128)(2,1)S(1)} %copy-done.1, bf16[1024,1024]{1,0:T(8,128)(2,1)S(1)} %copy-done.4, bf16[512,512]{1,0:T(8,128)(2,1)S(1)} %get-tuple-element.11.pair_ref), custom_call_target="tpu_custom_call" | custom-call | flops 8000000000 | bytes 8388608 | tf_op jit(solution)/shard_map/early/pallas_call | solution.py:239
  34.8 0.0 copy-start.6
  34.8 1.5 %copy-done.6 = f32[8,80,1024]{2,1,0:T(8,128)} copy-done((f32[8,80,1024]{2,1,0:T(8,128)}, f32[8,80,1024]{2,1,0:T(8,128)S(1)}, u32[]{:S(2)}) %copy-start.6) | copy-done | bytes 2621464
  36.3 0.0 copy-start.8
  36.3 1.3 %copy-done.8 = bf16[8,1024,128]{2,1,0:T(8,128)(2,1)} copy-done((bf16[8,1024,128]{2,1,0:T(8,128)(2,1)}, bf16[8,1024,128]{2,1,0:T(8,128)(2,1)S(1)}, u32[]{:S(2)}) %copy-start.8) | copy-done | bytes 2097176
  37.6 0.0 collective-permute-done.7.c_ref
  37.6 0.0 collective-permute-done.1.next_ref
  37.6 0.0 collective-permute-done.prev_ref
  37.7 0.0 copy-start.5
  37.7 1.6 %copy-done.5 = bf16[1024,1024]{1,0:T(8,128)(2,1)S(1)} copy-done((bf16[1024,1024]{1,0:T(8,128)(2,1)S(1)}, bf16[1024,1024]{1,0:T(8,128)(2,1)}, u32[]{:S(2)}) %copy-start.5) | copy-done | bytes 2097176
  39.3 0.0 copy-start.7
  39.3 1.7 %copy-done.7 = f32[8,80,1024]{2,1,0:T(8,128)S(1)} copy-done((f32[8,80,1024]{2,1,0:T(8,128)S(1)}, f32[8,80,1024]{2,1,0:T(8,128)}, u32[]{:S(2)}) %copy-start.7) | copy-done | bytes 2621464
  41.0 0.0 copy-start.9
  41.0 1.6 %copy-done.9 = bf16[8,1024,128]{2,1,0:T(8,128)(2,1)S(1)} copy-done((bf16[8,1024,128]{2,1,0:T(8,128)(2,1)S(1)}, bf16[8,1024,128]{2,1,0:T(8,128)(2,1)}, u32[]{:S(2)}) %copy-start.9) | copy-done | bytes 2097176
  42.6 10.9 %late.1 = bf16[512,1024]{1,0:T(8,128)(2,1)} custom-call(bf16[8,1024,128]{2,1,0:T(8,128)(2,1)S(1)} %copy-done.9, f32[8,80,1024]{2,1,0:T(8,128)S(1)} %copy-done.7, f32[8,1,1024]{2,1,0:T(1,128)S(1)} %get-tuple-element.14.top_ref, bf16[256,512]{1,0:T(8,128)(2,1)S(1)} %collective-permute-done.prev_ref, bf16[256,512]{1,0:T(8,128)(2,1)S(1)} %collective-permute-done.1.next_ref, ...), custom_call_target="tpu_custom_call" | custom-call | flops 12000000000 | bytes 8388608 | tf_op jit(solution)/shard_map/late/pallas_call | solution.py:252
  (10 shorter events, 0.2 us)
Async XLA Ops:
  0.0 1.2 %copy-start = (bf16[512,1024]{1,0:T(8,128)(2,1)S(1)}, bf16[512,1024]{1,0:T(8,128)(2,1)}, u32[]{:S(2)}) copy-start(bf16[512,1024]{1,0:T(8,128)(2,1)} %tokens_ref.3) | copy-start | bytes 3145732
  1.2 1.0 %copy-start.2 = (bf16[1024,256]{1,0:T(8,128)(2,1)S(1)}, bf16[1024,256]{1,0:T(8,128)(2,1)}, u32[]{:S(2)}) copy-start(bf16[1024,256]{1,0:T(8,128)(2,1)} %wk_ref.1) | copy-start | bytes 1572868
  2.3 1.0 %copy-start.3 = (bf16[1024,256]{1,0:T(8,128)(2,1)S(1)}, bf16[1024,256]{1,0:T(8,128)(2,1)}, u32[]{:S(2)}) copy-start(bf16[1024,256]{1,0:T(8,128)(2,1)} %wv_ref.1) | copy-start | bytes 1572868
  3.3 23.4 %copy-start.1 = (bf16[512,1024]{1,0:T(8,128)(2,1)S(1)}, bf16[512,1024]{1,0:T(8,128)(2,1)}, u32[]{:S(2)}) copy-start(bf16[512,1024]{1,0:T(8,128)(2,1)} %tokens_ref.3) | copy-start | bytes 3145732
  4.9 10.0 %collective-permute-start.2 = (bf16[32,512]{1,0:T(8,128)(2,1)S(1)}, bf16[32,512]{1,0:T(8,128)(2,1)S(1)}, u32[]{:S(2)}, u32[]{:S(2)}) collective-permute-start(bf16[32,512]{1,0:T(8,128)(2,1)S(1)} %get-tuple-element.15), channel_id=1, source_target_pairs={{0,2},{1,3},{2,0},{3,1},{4,6},{5,7},{6,4},{7,5},{8,10},{9,11},{10,... | collective-permute-start | bytes 98312 | tf_op jit(solution)/shard_map/ppermute | solution.py:31
  7.9 5.4 %collective-permute-start.4 = (bf16[2,512]{1,0:T(2,128)(2,1)S(1)}, bf16[2,512]{1,0:T(2,128)(2,1)S(1)}, u32[]{:S(2)}, u32[]{:S(2)}) collective-permute-start(bf16[2,512]{1,0:T(2,128)(2,1)S(1)} %get-tuple-element.16), channel_id=1, source_target_pairs={{0,18},{1,19},{2,16},{3,17},{4,22},{5,23},{6,20},{7,21},{8,26},{9,... | collective-permute-start | bytes 6152 | tf_op jit(solution)/shard_map/ppermute | solution.py:31
  10.5 4.5 %collective-permute-start.3 = (bf16[2,512]{1,0:T(2,128)(2,1)S(1)}, bf16[2,512]{1,0:T(2,128)(2,1)S(1)}, u32[]{:S(2)}, u32[]{:S(2)}) collective-permute-start(bf16[2,512]{1,0:T(2,128)(2,1)S(1)} %get-tuple-element.16), channel_id=1, source_target_pairs={{0,16},{1,17},{2,18},{3,19},{4,20},{5,21},{6,22},{7,23},{8,24},{9,... | collective-permute-start | bytes 6152 | tf_op jit(solution)/shard_map/ppermute | solution.py:31
  15.0 4.4 %collective-permute-start.5 = (bf16[68,512]{1,0:T(8,128)(2,1)S(1)}, bf16[68,512]{1,0:T(8,128)(2,1)S(1)}, u32[]{:S(2)}, u32[]{:S(2)}) collective-permute-start(bf16[68,512]{1,0:T(8,128)(2,1)S(1)} %pad_maximum_fusion), channel_id=1, source_target_pairs={{0,4},{1,5},{2,6},{3,7},{4,0},{5,1},{6,2},{7,3},{8,12},{9,13},{10,... | collective-permute-start | bytes 208904 | tf_op jit(solution)/shard_map/ppermute | solution.py:31
  19.4 6.0 %collective-permute-start.6 = (bf16[136,512]{1,0:T(8,128)(2,1)S(1)}, bf16[136,512]{1,0:T(8,128)(2,1)S(1)}, u32[]{:S(2)}, u32[]{:S(2)}) collective-permute-start(bf16[136,512]{1,0:T(8,128)(2,1)S(1)} %concatenate.25), channel_id=1, source_target_pairs={{0,8},{1,9},{2,10},{3,11},{4,12},{5,13},{6,14},{7,15},{8,0},{9,1},... | collective-permute-start | bytes 417800 | tf_op jit(solution)/shard_map/ppermute | solution.py:31
  21.1 16.5 %collective-permute-start.1 = (bf16[256,512]{1,0:T(8,128)(2,1)S(1)}, bf16[256,512]{1,0:T(8,128)(2,1)S(1)}, u32[]{:S(2)}, u32[]{:S(2)}) collective-permute-start(bf16[256,512]{1,0:T(8,128)(2,1)S(1)} %get-tuple-element.17), channel_id=1, source_target_pairs={{1,0},{2,1},{3,2},{4,3},{5,4},{6,5},{7,6},{8,7},{9,8},{10,9},{11,1... | collective-permute-start | bytes 786440 | tf_op jit(solution)/shard_map/ppermute | solution.py:217
  22.4 15.2 %collective-permute-start = (bf16[256,512]{1,0:T(8,128)(2,1)S(1)}, bf16[256,512]{1,0:T(8,128)(2,1)S(1)}, u32[]{:S(2)}, u32[]{:S(2)}) collective-permute-start(bf16[256,512]{1,0:T(8,128)(2,1)S(1)} %get-tuple-element.18), channel_id=1, source_target_pairs={{0,1},{1,2},{2,3},{3,4},{4,5},{5,6},{6,7},{7,8},{8,9},{9,10},{10,1... | collective-permute-start | bytes 786440 | tf_op jit(solution)/shard_map/ppermute | solution.py:216
  25.5 12.1 %collective-permute-start.7 = (bf16[272,512]{1,0:T(8,128)(2,1)S(1)}, bf16[272,512]{1,0:T(8,128)(2,1)S(1)}, u32[]{:S(2)}, u32[]{:S(2)}) collective-permute-start(bf16[272,512]{1,0:T(8,128)(2,1)S(1)} %concatenate.26), channel_id=1, source_target_pairs={{0,1},{1,0},{2,3},{3,2},{4,5},{5,4},{6,7},{7,6},{8,9},{9,8},{10,11... | collective-permute-start | bytes 835592 | tf_op jit(solution)/shard_map/ppermute | solution.py:31
  26.7 1.6 %copy-start.4 = (bf16[1024,1024]{1,0:T(8,128)(2,1)S(1)}, bf16[1024,1024]{1,0:T(8,128)(2,1)}, u32[]{:S(2)}) copy-start(bf16[1024,1024]{1,0:T(8,128)(2,1)} %wq_ref.1) | copy-start | bytes 6291460
  34.8 1.5 %copy-start.6 = (f32[8,80,1024]{2,1,0:T(8,128)}, f32[8,80,1024]{2,1,0:T(8,128)S(1)}, u32[]{:S(2)}) copy-start(f32[8,80,1024]{2,1,0:T(8,128)S(1)} %get-tuple-element.13.acc_ref) | copy-start | bytes 7864324
  36.3 1.3 %copy-start.8 = (bf16[8,1024,128]{2,1,0:T(8,128)(2,1)}, bf16[8,1024,128]{2,1,0:T(8,128)(2,1)S(1)}, u32[]{:S(2)}) copy-start(bf16[8,1024,128]{2,1,0:T(8,128)(2,1)S(1)} %get-tuple-element.12.q_ref) | copy-start | bytes 6291460
  37.7 1.6 %copy-start.5 = (bf16[1024,1024]{1,0:T(8,128)(2,1)S(1)}, bf16[1024,1024]{1,0:T(8,128)(2,1)}, u32[]{:S(2)}) copy-start(bf16[1024,1024]{1,0:T(8,128)(2,1)} %wout_ref.1) | copy-start | bytes 6291460
  39.3 1.7 %copy-start.7 = (f32[8,80,1024]{2,1,0:T(8,128)S(1)}, f32[8,80,1024]{2,1,0:T(8,128)}, u32[]{:S(2)}) copy-start(f32[8,80,1024]{2,1,0:T(8,128)} %copy-done.6) | copy-start | bytes 7864324
  41.0 1.6 %copy-start.9 = (bf16[8,1024,128]{2,1,0:T(8,128)(2,1)S(1)}, bf16[8,1024,128]{2,1,0:T(8,128)(2,1)}, u32[]{:S(2)}) copy-start(bf16[8,1024,128]{2,1,0:T(8,128)(2,1)} %copy-done.8) | copy-start | bytes 6291460

commit v2 on v1

v2 whole, which is shorter than its diff:
```python
import functools
import math

import jax
import jax.numpy as jnp
from jax import lax
from jax.experimental import pallas as pl
from jax.experimental.pallas import tpu as pltpu
from jax.sharding import PartitionSpec as P

HEADS = 16
KV_HEADS = 4
HEAD_DIM = 64
BLOCK = 256
POOL = 16
GROUP = 16
SHARE = HEADS // KV_HEADS
WIDE = 128
VROWS = 80
BF16 = jnp.bfloat16
F32 = jnp.float32
NT = (((1,), (1,)), ((), ()))
TN = (((0,), (0,)), ((), ()))
MASKED = -1e30
HOPS = (2, 4, 8, 1)
VMEM = pl.BlockSpec(memory_space=pltpu.VMEM)
HBM = pl.BlockSpec(memory_space=pl.ANY)


def swap(rows, apart):
    count = lax.axis_size("seq")
    return lax.ppermute(rows, "seq", [(i, i ^ apart) for i in range(count)])


def place(slot):
    return sum(hop for bit, hop in enumerate(HOPS) if slot >> bit & 1)


def tied(rows, *others):
    return lax.optimization_barrier((rows, *others))[0]


def project_pair(tokens_hbm, wk_hbm, wv_hbm, tokens_ref, pair_ref, mid_ref, coarse_ref, inner_ref, outer_ref, wk_ref, wv_ref, sems):
    copies = [
        pltpu.make_async_copy(source, target, sems.at[at])
        for at, (source, target) in enumerate(((wk_hbm, wk_ref), (tokens_hbm, tokens_ref), (wv_hbm, wv_ref)))
    ]
    for copy in copies:
        copy.start()
    copies[0].wait()
    copies[1].wait()
    tokens = tokens_ref[...]
    rows = tokens.shape[0]
    width = wk_ref.shape[1]
    for part, weight in enumerate((wk_ref, wv_ref)):
        if part == 1:
            copies[2].wait()
        at = slice(part * width, (part + 1) * width)
        held = jnp.dot(tokens, weight[...], preferred_element_type=F32).astype(BF16)
        pair_ref[:, at] = held
        for factor, target in ((POOL, mid_ref), (BLOCK, coarse_ref)):
            kept = target.shape[0]
            first = lax.broadcasted_iota(jnp.int32, (kept, rows), 0) * factor
            inside = lax.broadcasted_iota(jnp.int32, (kept, rows), 1) - first
            share = jnp.where((inside >= 0) & (inside < factor), 1.0 / factor, 0.0)
            mean = jnp.dot(share.astype(BF16), held, preferred_element_type=F32)
            target[:, at] = mean.astype(BF16)
    even = lax.axis_index("seq") % 2 == 0
    inner_ref[...] = jnp.where(even, pair_ref[rows - BLOCK :], pair_ref[:BLOCK])
    outer_ref[...] = jnp.where(even, pair_ref[:BLOCK], pair_ref[rows - BLOCK :])


def put_keys(keys_ref, rows, at, count, biases):
    lane = lax.broadcasted_iota(jnp.int32, (count, HEAD_DIM), 1)
    extra = jnp.zeros((count, HEAD_DIM), F32)
    for place_, bias in enumerate(biases):
        extra = jnp.where(lane == place_, bias, extra)
    extra = extra.astype(BF16)
    for head in range(KV_HEADS):
        keys_ref[head, at : at + count, :HEAD_DIM] = rows[:, head * HEAD_DIM : (head + 1) * HEAD_DIM]
        keys_ref[head, at : at + count, HEAD_DIM:] = extra


def put_values(values_ref, rows):
    width = KV_HEADS * HEAD_DIM
    count = rows.shape[0]
    tall = KV_HEADS * VROWS
    row = lax.broadcasted_iota(jnp.int32, (tall, width), 0)
    column = lax.broadcasted_iota(jnp.int32, (tall, width), 1)
    head, inner = column // HEAD_DIM, column % HEAD_DIM
    pick = jnp.where(row == head * VROWS + inner, 1.0, 0.0).astype(BF16)
    turned = lax.dot_general(pick, rows, NT, preferred_element_type=F32)
    counting = lax.broadcasted_iota(jnp.int32, (tall, count), 0) % VROWS == HEAD_DIM
    values_ref[...] = jnp.where(counting, 1.0, turned).astype(BF16).reshape(KV_HEADS, VROWS, count)


def run_units(units, scores, finish, values, even, odd):
    def first(unit, buffers):
        held, top = buffers
        x, floor = scores(unit)
        held[...] = x
        highest = jnp.max(x, axis=0, keepdims=True)
        top[...] = highest if floor is None else jnp.maximum(highest, floor)

    def second(unit, buffers):
        held, top = buffers
        highest = top[...]
        weights = jnp.exp(held[...] - highest).astype(BF16)
        finish(unit, highest, jnp.dot(values(unit), weights, preferred_element_type=F32))

    first(0, even)

    def step(i, carry):
        first(2 * i + 1, odd)
        second(2 * i, even)
        first(2 * i + 2, even)
        second(2 * i + 1, odd)
        return carry

    lax.fori_loop(0, units // 2 - 1, step, 0)
    first(units - 1, odd)
    second(units - 2, even)
    second(units - 1, odd)


def own(groups, tokens_ref, wq_hbm, pair_ref, *rest):
    q_ref, acc_ref, top_ref, wq_ref, sems, keys_ref, values_ref, sa, ta, sb, tb = rest[-11:]
    rows = tokens_ref.shape[0]
    blocks = rows // BLOCK
    width = KV_HEADS * HEAD_DIM
    span = SHARE * HEAD_DIM
    copies = []
    for at, group in enumerate(groups):
        copy = pltpu.make_async_copy(wq_hbm.at[:, pl.ds(group * span, span)], wq_ref.at[at], sems.at[at])
        copy.start()
        copies.append(copy)
    put_keys(keys_ref, pair_ref[:, :width], 0, rows, ())
    put_values(values_ref, pair_ref[:, width:])
    lane = lax.broadcasted_iota(jnp.int32, (BLOCK, HEAD_DIM), 1)
    for at, group in enumerate(groups):
        copies[at].wait()
        part = jnp.dot(tokens_ref[...], wq_ref[at], preferred_element_type=F32)
        part = part.astype(BF16) * (1.0 / math.sqrt(HEAD_DIM))
        for block in range(blocks):
            extra = jnp.where(lane == block, 1.0, 0.0).astype(BF16)
            for head in range(SHARE):
                to = slice(head * BLOCK, (head + 1) * BLOCK)
                piece = part[block * BLOCK : (block + 1) * BLOCK, head * HEAD_DIM : (head + 1) * HEAD_DIM]
                q_ref[group * blocks + block, to, :HEAD_DIM] = piece
                q_ref[group * blocks + block, to, HEAD_DIM:] = extra
    start = groups[0] * blocks

    def scores(unit):
        unit = unit + start
        return lax.dot_general(keys_ref[unit // blocks], q_ref[unit], NT, preferred_element_type=F32), None

    def finish(unit, highest, total):
        acc_ref[unit + start] = total
        top_ref[unit + start] = highest

    run_units(len(groups) * blocks, scores, finish, lambda unit: values_ref[(unit + start) // blocks], (sa, ta), (sb, tb))


def halo(q_ref, acc_in, top_in, inner_ref, outer_ref, acc_ref, top_ref, keys_ref, values_ref, sa, ta, sb, tb):
    blocks = keys_ref.shape[0]
    width = KV_HEADS * HEAD_DIM
    me = lax.axis_index("seq")
    devices = lax.axis_size("seq")
    even = me % 2 == 0
    for block in range(blocks):
        exists = me > 0 if block == 0 else me < devices - 1
        rows = jnp.where(even == (block == 0), outer_ref[...], inner_ref[...])
        bias = jnp.where(exists, 0.0, MASKED)
        put_keys(keys_ref.at[block], rows[:, :width], 0, BLOCK, [bias] * blocks)
        put_values(values_ref.at[block], rows[:, width:])

    def scores(unit):
        x = lax.dot_general(keys_ref[unit % blocks, unit // blocks], q_ref[unit], NT, preferred_element_type=F32)
        return x, top_in[unit]

    def finish(unit, highest, total):
        acc_ref[unit] = total + acc_in[unit] * jnp.exp(top_in[unit] - highest)
        top_ref[unit] = highest

    run_units(KV_HEADS * blocks, scores, finish, lambda unit: values_ref[unit % blocks, unit // blocks], (sa, ta), (sb, tb))


def slot_owner(slot):
    owner = jnp.zeros_like(slot)
    for bit, hop in enumerate(HOPS):
        owner = owner + (slot // 2**bit % 2) * hop
    return owner


def far(q_ref, acc_ref, top_ref, x_ref, y_ref, z_ref, c_ref, far_ref, wout_hbm,
        out_hbm, wout_ref, out_ref, sems, keys_ref, values_ref, mixed_ref, sa, ta, sb, tb):
    fetch = pltpu.make_async_copy(wout_hbm, wout_ref, sems.at[0])
    fetch.start()
    blocks = mixed_ref.shape[0]
    width = KV_HEADS * HEAD_DIM
    me = lax.axis_index("seq")
    groups = lax.axis_size("seq") // GROUP
    runs = BLOCK // POOL
    per_device = runs * blocks
    far_rows = far_ref.shape[0]
    pieces = [(far_ref, far_rows), (x_ref, per_device), (y_ref, 2 * per_device), (z_ref, 4 * per_device), (c_ref, 8 * per_device)]
    spread = blocks * (groups - 1)
    row = lax.broadcasted_iota(jnp.int32, (far_rows, HEAD_DIM), 0)
    other = (row % spread) // blocks + 1
    far_block = (((me // GROUP) ^ other) * GROUP + ((me % GROUP) ^ slot_owner(row // spread))) * blocks + row % blocks
    row = lax.broadcasted_iota(jnp.int32, ((GROUP - 1) * per_device, HEAD_DIM), 0) + per_device
    mid_block = (me ^ slot_owner(row // per_device)) * blocks + row % per_device // runs
    indices = [me * blocks + block for block in range(blocks)]
    far_bias = [jnp.where(jnp.abs(far_block - index) > 1, 0.0, MASKED) for index in indices]
    mid_bias = [jnp.where(jnp.abs(mid_block - index) > 1, 0.0, MASKED) for index in indices]
    put_keys(keys_ref, far_ref[:, :width], 0, far_rows, far_bias)
    at = 0
    for piece, count in pieces[1:]:
        put_keys(keys_ref, piece[:count, :width], far_rows + at, count, [bias[at : at + count] for bias in mid_bias])
        at += count
    put_values(values_ref, jnp.concatenate([piece[:count, width:] for piece, count in pieces], axis=0))

    def scores(unit):
        return lax.dot_general(keys_ref[unit // blocks], q_ref[unit], NT, preferred_element_type=F32), top_ref[unit]

    def finish(unit, highest, total):
        total = total + acc_ref[unit] * jnp.exp(top_ref[unit] - highest)
        share = total[:HEAD_DIM] / total[HEAD_DIM : HEAD_DIM + 1]
        share = share.astype(BF16)
        for head in range(SHARE):
            to = pl.multiple_of((unit // blocks * SHARE + head) * HEAD_DIM, HEAD_DIM)
            mixed_ref[unit % blocks, pl.ds(to, HEAD_DIM), :] = share[:, head * BLOCK : (head + 1) * BLOCK]

    run_units(KV_HEADS * blocks, scores, finish, lambda unit: values_ref[unit // blocks], (sa, ta), (sb, tb))
    fetch.wait()
    stores = []
    for block in range(blocks):
        at = pl.ds(block * BLOCK, BLOCK)
        out_ref[at] = lax.dot_general(mixed_ref[block], wout_ref[...], TN, preferred_element_type=F32).astype(BF16)
        store = pltpu.make_async_copy(out_ref.at[at], out_hbm.at[at], sems.at[1 + block])
        store.start()
        stores.append(store)
    for store in stores:
        store.wait()


def body(tokens, w_query, w_key, w_value, w_out):
    devices = lax.axis_size("seq")
    rows, model = tokens.shape
    blocks = rows // BLOCK
    width = KV_HEADS * HEAD_DIM
    units = KV_HEADS * blocks
    stack = SHARE * BLOCK
    shape = jax.ShapeDtypeStruct
    dma = pltpu.SemaphoreType.DMA

    def call(kernel, out_shape, in_specs, out_specs, scratch, flops, name, aliases={}, mib=20):
        return pl.pallas_call(
            kernel,
            out_shape=out_shape,
            in_specs=in_specs,
            out_specs=out_specs,
            scratch_shapes=scratch,
            input_output_aliases=aliases,
            compiler_params=pltpu.CompilerParams(vmem_limit_bytes=mib * 2**20),
            cost_estimate=pl.CostEstimate(flops=flops, bytes_accessed=2**20, transcendentals=0),
            name=name,
        )

    def slots(keys):
        return [pltpu.VMEM((keys, stack), F32), pltpu.VMEM((1, stack), F32)] * 2

    half = shape((BLOCK, 2 * width), BF16)
    held_tokens, pair, mid, coarse, inner, outer = call(
        project_pair,
        [shape((rows, model), BF16), shape((rows, 2 * width), BF16), shape((rows // POOL, 2 * width), BF16), shape((blocks, 2 * width), BF16), half, half],
        [HBM] * 3,
        [VMEM] * 6,
        [pltpu.VMEM((model, width), BF16)] * 2 + [dma((3,))],
        2 * 10**9,
        "pair",
    )(tokens, w_key, w_value)

    spread = coarse
    level = GROUP
    while level < devices:
        spread = jnp.concatenate([spread, swap(spread, level)], axis=0)
        level *= 2
    spread = spread[blocks:]
    inner = swap(inner, 1)
    pairs = [(i, i + 1) for i in range(1, devices - 1, 2)]
    outer = lax.ppermute(outer, "seq", pairs + [(b, a) for a, b in pairs])
    held = mid
    payload = jnp.concatenate([held, spread], axis=0)
    first = swap(payload, HOPS[0])
    received = [first]

    state = [shape((units, stack, WIDE), BF16), shape((units, VROWS, stack), F32), shape((units, 1, stack), F32)]
    share = KV_HEADS // 2
    scratch = [
        pltpu.VMEM((share, model, SHARE * HEAD_DIM), BF16),
        dma((share,)),
        pltpu.VMEM((KV_HEADS, rows, WIDE), BF16),
        pltpu.VMEM((KV_HEADS, VROWS, rows), BF16),
    ] + slots(rows)
    attend = lambda part, extra: call(
        functools.partial(own, list(range(part * share, (part + 1) * share))),
        state,
        [VMEM, HBM, VMEM] + [VMEM] * extra,
        [VMEM] * 3,
        scratch,
        5 * 10**9,
        "own%d" % part,
        {3 + i: i for i in range(extra)},
    )
    q, acc, top = attend(0, 0)(tied(held_tokens, payload), w_query, pair)

    def grow(held, spread, both, hop, top):
        held = jnp.concatenate([held, both[: held.shape[0]]], axis=0)
        spread = jnp.concatenate([spread, both[held.shape[0] // 2 :]], axis=0)
        payload = tied(jnp.concatenate([held, spread], axis=0), top)
        both = swap(payload, hop)
        received.append(both)
        return held, spread, payload, both

    held, spread, payload, both = grow(held, spread, first, HOPS[1], top)
    q, acc, top = attend(1, 3)(tied(held_tokens, payload), w_query, pair, q, acc, top)
    held, spread, payload, both = grow(held, spread, both, HOPS[2], top)
    acc, top = call(
        halo,
        state[1:],
        [VMEM] * 5,
        [VMEM] * 2,
        [pltpu.VMEM((blocks, KV_HEADS, BLOCK, WIDE), BF16), pltpu.VMEM((blocks, KV_HEADS, VROWS, BLOCK), BF16)] + slots(BLOCK),
        4 * 10**9,
        "halo",
        {1: 0, 2: 1},
    )(tied(q, payload), acc, top, inner, outer)
    held, spread, payload, both = grow(held, spread, both, HOPS[3], top)
    spread = jnp.concatenate([spread, both[held.shape[0] :]], axis=0)
    keys = (GROUP - 1) * (rows // POOL) + spread.shape[0]
    return call(
        far,
        shape((rows, w_out.shape[1]), BF16),
        [VMEM] * 8 + [HBM],
        HBM,
        [
            pltpu.VMEM(w_out.shape, BF16),
            pltpu.VMEM((rows, w_out.shape[1]), BF16),
            dma((1 + blocks,)),
            pltpu.VMEM((KV_HEADS, keys, WIDE), BF16),
            pltpu.VMEM((KV_HEADS, VROWS, keys), BF16),
            pltpu.VMEM((blocks, HEADS * HEAD_DIM, BLOCK), BF16),
        ]
        + slots(keys),
        8 * 10**9,
        "far",
        mib=30,
    )(q, acc, top, *received, spread, w_out)


def solution(mesh):
    placed = (P("seq", None), P(), P(), P(), P())
    return jax.shard_map(body, mesh=mesh, in_specs=placed, out_specs=P("seq", None), check_vma=False)
```

time: 53.9 us -> 56.9 us (1.056)
  Pallas kernels: 19 us -> 22.7 us
  starting transfers between devices: 14.3 us -> 10.8 us
  local copies, waits for them, and re-layouts: 12.8 us -> 14.6 us
  waiting for transfers between devices: 7.3 us -> 8.36 us
    pallas_call x3 -> x5, Pallas kernels: 19 us -> 22.7 us  [the longest x1 7.99 us: body(): call(far, shape((rows, w_out.shape[1]), BF16), [VMEM] * 8 + [HBM], HBM, [...]
    ppermute x2 -> x1, starting transfers between devices: 4.34 us -> 0.67 us  [body(): outer = lax.ppermute(outer, 'seq', pairs + [(b, a) for a, b in pairs])]
    unnamed x20 -> x25, local copies, waits for them, and re-layouts: 12.6 us -> 14.5 us
    ppermute x6, waiting for transfers between devices: 7.29 us -> 8.36 us  [swap(): return lax.ppermute(rows, 'seq', [(i, i ^ apart) for i in range(count)])]
  transfers between devices with their start and end apart: 8 -> 7, of which waited for: 3 -> 4; matrix products, arithmetic and copies ran while one was open for 0% -> 0% of each run, Pallas kernels for 12% -> 17%
where the time goes in v2:
time: 56.9 us; the launch traced here: 56.6 us
  Pallas kernels  22.7 us (40%)
  local copies, waits for them, and re-layouts  14.6 us (26%)
  starting transfers between devices  10.8 us (19%)
  waiting for transfers between devices  8.36 us (15%)
    unnamed x25, local copies, waits for them, and re-layouts  14.5 us
    ppermute x6, starting transfers between devices, swap(): return lax.ppermute(rows, 'seq', [(i, i ^ apart) for i in range(count)])  10.2 us
    ppermute x6, waiting for transfers between devices, swap(): return lax.ppermute(rows, 'seq', [(i, i ^ apart) for i in range(count)])  8.36 us
    pallas_call x1, Pallas kernels, body(): call(far, shape((rows, w_out.shape[1]), BF16), [VMEM] * 8 + [HBM], HBM, [...  7.99 us
    pallas_call x1, Pallas kernels, body(): attend(1, 3)(tied(held_tokens, payload), w_query, pair, q, acc, top)  4.74 us
    pallas_call x1, Pallas kernels, body(): q, acc, top = attend(0, 0)(tied(held_tokens, payload), w_query, pair)  4.74 us
    pallas_call x1, Pallas kernels, body(): call(halo, state[1:], [VMEM] * 5, [VMEM] * 2, [pltpu.VMEM((blocks, KV_HEA...  3.24 us
    pallas_call x1, Pallas kernels, body(): call(project_pair, [shape((rows, model), BF16), shape((rows, 2 * width),...  1.94 us
  transfers between devices with their start and end apart: 7, of which 4 were waited for; matrix products, arithmetic and copies ran while one was open for 0% of the time, Pallas kernels for 17%

profile of v2, /device:TPU:0, one launch (start us, length us, event | category | flops | bytes accessed | tf_op | source)
XLA Modules:
  0.0 56.6 jit_solution(12055306834950972603)
XLA Ops:
  0.0 0.0 copy-start
  0.0 0.0 copy-start.2
  0.0 1.4 %copy-done.2 = bf16[512,1024]{1,0:T(8,128)(2,1)S(1)} copy-done((bf16[512,1024]{1,0:T(8,128)(2,1)S(1)}, bf16[512,1024]{1,0:T(8,128)(2,1)}, u32[]{:S(2)}) %copy-start.2) | copy-done | bytes 1048600
  1.4 0.0 copy-start.3
  1.4 1.0 %copy-done.3 = bf16[1024,256]{1,0:T(8,128)(2,1)S(1)} copy-done((bf16[1024,256]{1,0:T(8,128)(2,1)S(1)}, bf16[1024,256]{1,0:T(8,128)(2,1)}, u32[]{:S(2)}) %copy-start.3) | copy-done | bytes 524312
  2.4 0.0 copy-start.4
  2.4 1.0 %copy-done.4 = bf16[1024,256]{1,0:T(8,128)(2,1)S(1)} copy-done((bf16[1024,256]{1,0:T(8,128)(2,1)S(1)}, bf16[1024,256]{1,0:T(8,128)(2,1)}, u32[]{:S(2)}) %copy-start.4) | copy-done | bytes 524312
  3.5 1.9 %pair.1 = (bf16[512,1024]{1,0:T(8,128)(2,1)S(1)}, bf16[512,512]{1,0:T(8,128)(2,1)S(1)}, bf16[32,512]{1,0:T(8,128)(2,1)S(1)}, bf16[2,512]{1,0:T(2,128)(2,1)S(1)},...) custom-call(bf16[512,1024]{1,0:T(8,128)(2,1)S(1)} %copy-done.2, bf16[1024,256]{1,0:T(8,128)(2,1)S(1)} %copy-done.3, ...), custom_call_target="tpu_custom_call" | custom-call | flops 2000000000 | bytes 1048576 | tf_op jit(solution)/shard_map/pair/pallas_call | solution.py:274
  5.4 4.1 %collective-permute-start = (bf16[2,512]{1,0:T(2,128)(2,1)S(1)}, bf16[2,512]{1,0:T(2,128)(2,1)S(1)}, u32[]{:S(2)}, u32[]{:S(2)}) collective-permute-start(bf16[2,512]{1,0:T(2,128)(2,1)S(1)} %get-tuple-element.27), channel_id=1, source_target_pairs={{0,16},{1,17},{2,18},{3,19},{4,20},{5,21},{6,22},{7,23},{8,24},{9,... | collective-permute-start | bytes 6152 | tf_op jit(solution)/shard_map/ppermute | solution.py:32
  9.5 0.0 collective-permute-start.3
  9.5 0.7 %collective-permute-start.4 = (bf16[256,512]{1,0:T(8,128)(2,1)S(1)}, bf16[256,512]{1,0:T(8,128)(2,1)S(1)}, u32[]{:S(2)}, u32[]{:S(2)}) collective-permute-start(bf16[256,512]{1,0:T(8,128)(2,1)S(1)} %get-tuple-element.41), channel_id=1, source_target_pairs={{1,2},{3,4},{5,6},{7,8},{9,10},{11,12},{13,14},{15,16},{17,18},{19... | collective-permute-start | bytes 786440 | tf_op jit(solution)/shard_map/ppermute | solution.py:292
  10.2 0.9 %collective-permute-done = bf16[2,512]{1,0:T(2,128)(2,1)S(1)} collective-permute-done((bf16[2,512]{1,0:T(2,128)(2,1)S(1)}, bf16[2,512]{1,0:T(2,128)(2,1)S(1)}, u32[]{:S(2)}, u32[]{:S(2)}) %collective-permute-start) | collective-permute-done | bytes 2080 | tf_op jit(solution)/shard_map/ppermute | solution.py:32
  11.1 2.6 %collective-permute-start.1 = (bf16[34,512]{1,0:T(8,128)(2,1)S(1)}, bf16[34,512]{1,0:T(8,128)(2,1)S(1)}, u32[]{:S(2)}, u32[]{:S(2)}) collective-permute-start(bf16[34,512]{1,0:T(8,128)(2,1)S(1)} %constant_dynamic-update-slice_fusion), channel_id=1, source_target_pairs={{0,2},{1,3},{2,0},{3,1},{4,6},{5,7},{6,4},{7,5},{8,10},{9,11},{10,... | collective-permute-start | bytes 104456 | tf_op jit(solution)/shard_map/ppermute | solution.py:32
  13.7 0.0 copy-done
  13.7 4.7 %own0.1 = (bf16[8,1024,128]{2,1,0:T(8,128)(2,1)S(1)}, f32[8,80,1024]{2,1,0:T(8,128)S(1)}, f32[8,1,1024]{2,1,0:T(1,128)S(1)}) custom-call(bf16[512,1024]{1,0:T(8,128)(2,1)S(1)} %get-tuple-element.32.tokens_ref, bf16[1024,1024]{1,0:T(8,128)(2,1)S(1)} %copy-done, bf16[512,512]{1,0:T(8,128)(2,1)S(1)} %get-tuple-element.29.pair_ref), custom_call_target="tpu_custom_call" | custom-call | flops 5000000000 | bytes 1048576 | tf_op jit(solution)/shard_map/own0/pallas_call | solution.py:316
  18.4 2.9 %collective-permute-done.1.x_ref = bf16[34,512]{1,0:T(8,128)(2,1)S(1)} collective-permute-done((bf16[34,512]{1,0:T(8,128)(2,1)S(1)}, bf16[34,512]{1,0:T(8,128)(2,1)S(1)}, u32[]{:S(2)}, u32[]{:S(2)}) %collective-permute-start.1) | collective-permute-done | bytes 34848 | tf_op jit(solution)/shard_map/ppermute | solution.py:32
  21.3 0.2 collective-permute-start.2
  21.5 4.7 %own1.1 = (bf16[8,1024,128]{2,1,0:T(8,128)(2,1)S(1)}, f32[8,80,1024]{2,1,0:T(8,128)S(1)}, f32[8,1,1024]{2,1,0:T(1,128)S(1)}) custom-call(bf16[512,1024]{1,0:T(8,128)(2,1)S(1)} %get-tuple-element.32.tokens_ref, bf16[1024,1024]{1,0:T(8,128)(2,1)S(1)} %copy-done, ...), custom_call_target="tpu_custom_call", output_to_operand_aliasing={{0}: (3, {}), {1}: (4, {}), {2}: (5, {})} | custom-call | flops 5000000000 | bytes 1048576 | tf_op jit(solution)/shard_map/own1/pallas_call | solution.py:327
  26.3 0.0 copy-start.5
  26.3 1.5 %copy-done.5 = f32[8,80,1024]{2,1,0:T(8,128)} copy-done((f32[8,80,1024]{2,1,0:T(8,128)}, f32[8,80,1024]{2,1,0:T(8,128)S(1)}, u32[]{:S(2)}) %copy-start.5) | copy-done | bytes 2621464
  27.8 0.0 copy-start.9
  27.8 1.4 %copy-done.9 = bf16[8,1024,128]{2,1,0:T(8,128)(2,1)} copy-done((bf16[8,1024,128]{2,1,0:T(8,128)(2,1)}, bf16[8,1024,128]{2,1,0:T(8,128)(2,1)S(1)}, u32[]{:S(2)}) %copy-start.9) | copy-done | bytes 2097176
  29.1 0.0 collective-permute-done.2.y_ref
  29.2 3.3 %collective-permute-start.5 = (bf16[136,512]{1,0:T(8,128)(2,1)S(1)}, bf16[136,512]{1,0:T(8,128)(2,1)S(1)}, u32[]{:S(2)}, u32[]{:S(2)}) collective-permute-start(bf16[136,512]{1,0:T(8,128)(2,1)S(1)} %concatenate.29), channel_id=1, source_target_pairs={{0,8},{1,9},{2,10},{3,11},{4,12},{5,13},{6,14},{7,15},{8,0},{9,1},... | collective-permute-start | bytes 417800 | tf_op jit(solution)/shard_map/ppermute | solution.py:32
  32.5 3.0 %collective-permute-done.5.z_ref = bf16[136,512]{1,0:T(8,128)(2,1)S(1)} collective-permute-done((bf16[136,512]{1,0:T(8,128)(2,1)S(1)}, bf16[136,512]{1,0:T(8,128)(2,1)S(1)}, u32[]{:S(2)}, u32[]{:S(2)}) %collective-permute-start.5) | collective-permute-done | bytes 139296 | tf_op jit(solution)/shard_map/ppermute | solution.py:32
  35.6 0.0 collective-permute-done.3.inner_ref
  35.6 0.0 collective-permute-done.4.outer_ref
  35.6 0.0 copy-start.6
  35.6 1.7 %copy-done.6 = f32[8,80,1024]{2,1,0:T(8,128)S(1)} copy-done((f32[8,80,1024]{2,1,0:T(8,128)S(1)}, f32[8,80,1024]{2,1,0:T(8,128)}, u32[]{:S(2)}) %copy-start.6) | copy-done | bytes 2621464
  37.4 0.0 copy-start.10
  37.4 1.6 %copy-done.10 = bf16[8,1024,128]{2,1,0:T(8,128)(2,1)S(1)} copy-done((bf16[8,1024,128]{2,1,0:T(8,128)(2,1)S(1)}, bf16[8,1024,128]{2,1,0:T(8,128)(2,1)}, u32[]{:S(2)}) %copy-start.10) | copy-done | bytes 2097176
  38.9 0.0 copy-start.1
  38.9 3.2 %halo.1 = (f32[8,80,1024]{2,1,0:T(8,128)S(1)}, f32[8,1,1024]{2,1,0:T(1,128)S(1)}) custom-call(bf16[8,1024,128]{2,1,0:T(8,128)(2,1)S(1)} %copy-done.10, f32[8,80,1024]{2,1,0:T(8,128)S(1)} %copy-done.6, f32[8,1,1024]{2,1,0:T(1,128)S(1)} %get-tuple-element.36.top_in, ...), custom_call_target="tpu_custom_call", output_to_operand_aliasing={{0}: (1, {}), {1}: (2, {})} | custom-call | flops 4000000000 | bytes 1048576 | tf_op jit(solution)/shard_map/halo/pallas_call | solution.py:329
  42.2 0.0 copy-start.7
  42.2 1.5 %copy-done.7 = f32[8,80,1024]{2,1,0:T(8,128)} copy-done((f32[8,80,1024]{2,1,0:T(8,128)}, f32[8,80,1024]{2,1,0:T(8,128)S(1)}, u32[]{:S(2)}) %copy-start.7) | copy-done | bytes 2621464
  43.7 0.0 collective-permute-start.6
  43.7 1.6 %collective-permute-done.6.c_ref = bf16[272,512]{1,0:T(8,128)(2,1)S(1)} collective-permute-done((bf16[272,512]{1,0:T(8,128)(2,1)S(1)}, bf16[272,512]{1,0:T(8,128)(2,1)S(1)}, u32[]{:S(2)}, u32[]{:S(2)}) %collective-permute-start.6) | collective-permute-done | bytes 278560 | tf_op jit(solution)/shard_map/ppermute | solution.py:32
  45.3 0.0 copy-done.1
  45.3 0.0 copy-start.8
  45.3 1.7 %copy-done.8 = f32[8,80,1024]{2,1,0:T(8,128)S(1)} copy-done((f32[8,80,1024]{2,1,0:T(8,128)S(1)}, f32[8,80,1024]{2,1,0:T(8,128)}, u32[]{:S(2)}) %copy-start.8) | copy-done | bytes 2621464
  47.0 0.0 copy-start.11
  47.0 1.6 %copy-done.11 = bf16[8,1024,128]{2,1,0:T(8,128)(2,1)S(1)} copy-done((bf16[8,1024,128]{2,1,0:T(8,128)(2,1)S(1)}, bf16[8,1024,128]{2,1,0:T(8,128)(2,1)}, u32[]{:S(2)}) %copy-start.11) | copy-done | bytes 2097176
  48.6 8.0 %far.1 = bf16[512,1024]{1,0:T(8,128)(2,1)} custom-call(bf16[8,1024,128]{2,1,0:T(8,128)(2,1)S(1)} %copy-done.11, f32[8,80,1024]{2,1,0:T(8,128)S(1)} %copy-done.8, f32[8,1,1024]{2,1,0:T(1,128)S(1)} %get-tuple-element.43.top_ref, bf16[34,512]{1,0:T(8,128)(2,1)S(1)} %collective-permute-done.1.x_ref, bf16[68,512]{1,0:T(8,128)(2,1)S(1)} %collective-permute-done.2.y_ref, ...), custom_call_target="tpu_custom_call" | custom-call | flops 8000000000 | bytes 1048576 | tf_op jit(solution)/shard_map/far/pallas_call | solution.py:342
  (13 shorter events, 0.2 us)
Async XLA Ops:
  0.0 13.7 %copy-start = (bf16[1024,1024]{1,0:T(8,128)(2,1)S(1)}, bf16[1024,1024]{1,0:T(8,128)(2,1)}, u32[]{:S(2)}) copy-start(bf16[1024,1024]{1,0:T(8,128)(2,1)} %wq_hbm.3) | copy-start | bytes 6291460
  0.0 1.4 %copy-start.2 = (bf16[512,1024]{1,0:T(8,128)(2,1)S(1)}, bf16[512,1024]{1,0:T(8,128)(2,1)}, u32[]{:S(2)}) copy-start(bf16[512,1024]{1,0:T(8,128)(2,1)} %tokens_hbm.1) | copy-start | bytes 3145732
  1.4 1.0 %copy-start.3 = (bf16[1024,256]{1,0:T(8,128)(2,1)S(1)}, bf16[1024,256]{1,0:T(8,128)(2,1)}, u32[]{:S(2)}) copy-start(bf16[1024,256]{1,0:T(8,128)(2,1)} %wk_hbm.1) | copy-start | bytes 1572868
  2.4 1.0 %copy-start.4 = (bf16[1024,256]{1,0:T(8,128)(2,1)S(1)}, bf16[1024,256]{1,0:T(8,128)(2,1)}, u32[]{:S(2)}) copy-start(bf16[1024,256]{1,0:T(8,128)(2,1)} %wv_hbm.1) | copy-start | bytes 1572868
  5.4 5.7 %collective-permute-start = (bf16[2,512]{1,0:T(2,128)(2,1)S(1)}, bf16[2,512]{1,0:T(2,128)(2,1)S(1)}, u32[]{:S(2)}, u32[]{:S(2)}) collective-permute-start(bf16[2,512]{1,0:T(2,128)(2,1)S(1)} %get-tuple-element.27), channel_id=1, source_target_pairs={{0,16},{1,17},{2,18},{3,19},{4,20},{5,21},{6,22},{7,23},{8,24},{9,... | collective-permute-start | bytes 6152 | tf_op jit(solution)/shard_map/ppermute | solution.py:32
  9.5 26.1 %collective-permute-start.3 = (bf16[256,512]{1,0:T(8,128)(2,1)S(1)}, bf16[256,512]{1,0:T(8,128)(2,1)S(1)}, u32[]{:S(2)}, u32[]{:S(2)}) collective-permute-start(bf16[256,512]{1,0:T(8,128)(2,1)S(1)} %get-tuple-element.40), channel_id=1, source_target_pairs={{0,1},{1,0},{2,3},{3,2},{4,5},{5,4},{6,7},{7,6},{8,9},{9,8},{10,11... | collective-permute-start | bytes 786440 | tf_op jit(solution)/shard_map/ppermute | solution.py:32
  9.5 26.1 %collective-permute-start.4 = (bf16[256,512]{1,0:T(8,128)(2,1)S(1)}, bf16[256,512]{1,0:T(8,128)(2,1)S(1)}, u32[]{:S(2)}, u32[]{:S(2)}) collective-permute-start(bf16[256,512]{1,0:T(8,128)(2,1)S(1)} %get-tuple-element.41), channel_id=1, source_target_pairs={{1,2},{3,4},{5,6},{7,8},{9,10},{11,12},{13,14},{15,16},{17,18},{19... | collective-permute-start | bytes 786440 | tf_op jit(solution)/shard_map/ppermute | solution.py:292
  11.1 10.2 %collective-permute-start.1 = (bf16[34,512]{1,0:T(8,128)(2,1)S(1)}, bf16[34,512]{1,0:T(8,128)(2,1)S(1)}, u32[]{:S(2)}, u32[]{:S(2)}) collective-permute-start(bf16[34,512]{1,0:T(8,128)(2,1)S(1)} %constant_dynamic-update-slice_fusion), channel_id=1, source_target_pairs={{0,2},{1,3},{2,0},{3,1},{4,6},{5,7},{6,4},{7,5},{8,10},{9,11},{10,... | collective-permute-start | bytes 104456 | tf_op jit(solution)/shard_map/ppermute | solution.py:32
  21.3 7.8 %collective-permute-start.2 = (bf16[68,512]{1,0:T(8,128)(2,1)S(1)}, bf16[68,512]{1,0:T(8,128)(2,1)S(1)}, u32[]{:S(2)}, u32[]{:S(2)}) collective-permute-start(bf16[68,512]{1,0:T(8,128)(2,1)S(1)} %pad_maximum_fusion), channel_id=1, source_target_pairs={{0,4},{1,5},{2,6},{3,7},{4,0},{5,1},{6,2},{7,3},{8,12},{9,13},{10,... | collective-permute-start | bytes 208904 | tf_op jit(solution)/shard_map/ppermute | solution.py:32
  26.3 1.5 %copy-start.5 = (f32[8,80,1024]{2,1,0:T(8,128)}, f32[8,80,1024]{2,1,0:T(8,128)S(1)}, u32[]{:S(2)}) copy-start(f32[8,80,1024]{2,1,0:T(8,128)S(1)} %get-tuple-element.39.acc_in) | copy-start | bytes 7864324
  27.8 1.4 %copy-start.9 = (bf16[8,1024,128]{2,1,0:T(8,128)(2,1)}, bf16[8,1024,128]{2,1,0:T(8,128)(2,1)S(1)}, u32[]{:S(2)}) copy-start(bf16[8,1024,128]{2,1,0:T(8,128)(2,1)S(1)} %get-tuple-element.38.q_ref) | copy-start | bytes 6291460
  29.2 6.4 %collective-permute-start.5 = (bf16[136,512]{1,0:T(8,128)(2,1)S(1)}, bf16[136,512]{1,0:T(8,128)(2,1)S(1)}, u32[]{:S(2)}, u32[]{:S(2)}) collective-permute-start(bf16[136,512]{1,0:T(8,128)(2,1)S(1)} %concatenate.29), channel_id=1, source_target_pairs={{0,8},{1,9},{2,10},{3,11},{4,12},{5,13},{6,14},{7,15},{8,0},{9,1},... | collective-permute-start | bytes 417800 | tf_op jit(solution)/shard_map/ppermute | solution.py:32
  35.6 1.7 %copy-start.6 = (f32[8,80,1024]{2,1,0:T(8,128)S(1)}, f32[8,80,1024]{2,1,0:T(8,128)}, u32[]{:S(2)}) copy-start(f32[8,80,1024]{2,1,0:T(8,128)} %copy-done.5) | copy-start | bytes 7864324
  37.4 1.6 %copy-start.10 = (bf16[8,1024,128]{2,1,0:T(8,128)(2,1)S(1)}, bf16[8,1024,128]{2,1,0:T(8,128)(2,1)}, u32[]{:S(2)}) copy-start(bf16[8,1024,128]{2,1,0:T(8,128)(2,1)} %copy-done.9) | copy-start | bytes 6291460
  38.9 6.3 %copy-start.1 = (bf16[1024,1024]{1,0:T(8,128)(2,1)S(1)}, bf16[1024,1024]{1,0:T(8,128)(2,1)}, u32[]{:S(2)}) copy-start(bf16[1024,1024]{1,0:T(8,128)(2,1)} %wout_hbm.1) | copy-start | bytes 6291460
  42.2 1.5 %copy-start.7 = (f32[8,80,1024]{2,1,0:T(8,128)}, f32[8,80,1024]{2,1,0:T(8,128)S(1)}, u32[]{:S(2)}) copy-start(f32[8,80,1024]{2,1,0:T(8,128)S(1)} %get-tuple-element.42.acc_ref) | copy-start | bytes 7864324
  43.7 1.6 %collective-permute-start.6 = (bf16[272,512]{1,0:T(8,128)(2,1)S(1)}, bf16[272,512]{1,0:T(8,128)(2,1)S(1)}, u32[]{:S(2)}, u32[]{:S(2)}) collective-permute-start(bf16[272,512]{1,0:T(8,128)(2,1)S(1)} %concatenate.30), channel_id=1, source_target_pairs={{0,1},{1,0},{2,3},{3,2},{4,5},{5,4},{6,7},{7,6},{8,9},{9,8},{10,11... | collective-permute-start | bytes 835592 | tf_op jit(solution)/shard_map/ppermute | solution.py:32
  45.3 1.7 %copy-start.8 = (f32[8,80,1024]{2,1,0:T(8,128)S(1)}, f32[8,80,1024]{2,1,0:T(8,128)}, u32[]{:S(2)}) copy-start(f32[8,80,1024]{2,1,0:T(8,128)} %copy-done.7) | copy-start | bytes 7864324
  47.0 1.6 %copy-start.11 = (bf16[8,1024,128]{2,1,0:T(8,128)(2,1)S(1)}, bf16[8,1024,128]{2,1,0:T(8,128)(2,1)}, u32[]{:S(2)}) copy-start(bf16[8,1024,128]{2,1,0:T(8,128)(2,1)} %copy-done.9) | copy-start | bytes 6291460

commit v3 on v2

v3 whole, which is shorter than its diff:
```python
import math

import jax
import jax.numpy as jnp
from jax import lax
from jax.experimental import pallas as pl
from jax.experimental.pallas import tpu as pltpu
from jax.sharding import PartitionSpec as P

HEADS = 16
KV_HEADS = 4
HEAD_DIM = 64
BLOCK = 256
POOL = 16
GROUP = 16
SHARE = HEADS // KV_HEADS
WIDE = 128
VROWS = 80
BF16 = jnp.bfloat16
F32 = jnp.float32
NT = (((1,), (1,)), ((), ()))
TN = (((0,), (0,)), ((), ()))
MASKED = -1e30
VMEM = pl.BlockSpec(memory_space=pltpu.VMEM)
HBM = pl.BlockSpec(memory_space=pltpu.HBM)


def swap(rows, apart):
    count = lax.axis_size("seq")
    return lax.ppermute(rows, "seq", [(i, i ^ apart) for i in range(count)])


def tied(rows, *others):
    return lax.optimization_barrier((rows, *others))[0]


def project_pair(tokens_hbm, wk_hbm, wv_hbm, pair_ref, mid_ref, coarse_ref, inner_ref, outer_ref, tokens_ref, wk_ref, wv_ref, sems):
    copies = [
        pltpu.make_async_copy(source, target, sems.at[at])
        for at, (source, target) in enumerate(((wk_hbm, wk_ref), (tokens_hbm, tokens_ref), (wv_hbm, wv_ref)))
    ]
    for copy in copies:
        copy.start()
    copies[0].wait()
    copies[1].wait()
    tokens = tokens_ref[...]
    rows = tokens.shape[0]
    width = wk_ref.shape[1]
    for part, weight in enumerate((wk_ref, wv_ref)):
        if part == 1:
            copies[2].wait()
        at = slice(part * width, (part + 1) * width)
        held = jnp.dot(tokens, weight[...], preferred_element_type=F32).astype(BF16)
        pair_ref[:, at] = held
        for factor, target in ((POOL, mid_ref), (BLOCK, coarse_ref)):
            kept = target.shape[0]
            first = lax.broadcasted_iota(jnp.int32, (kept, rows), 0) * factor
            inside = lax.broadcasted_iota(jnp.int32, (kept, rows), 1) - first
            share = jnp.where((inside >= 0) & (inside < factor), 1.0 / factor, 0.0)
            mean = jnp.dot(share.astype(BF16), held, preferred_element_type=F32)
            target[:, at] = mean.astype(BF16)
    even = lax.axis_index("seq") % 2 == 0
    inner_ref[...] = jnp.where(even, pair_ref[rows - BLOCK :], pair_ref[:BLOCK])
    outer_ref[...] = jnp.where(even, pair_ref[:BLOCK], pair_ref[rows - BLOCK :])


def put_keys(keys_ref, rows, at, biases):
    count = rows.shape[0]
    lane = lax.broadcasted_iota(jnp.int32, (count, HEAD_DIM), 1)
    extra = jnp.zeros((count, HEAD_DIM), F32)
    for order, bias in enumerate(biases):
        extra = jnp.where(lane == order, bias, extra)
    extra = extra.astype(BF16)
    for head in range(KV_HEADS):
        keys_ref[head, pl.ds(at, count), :HEAD_DIM] = rows[:, head * HEAD_DIM : (head + 1) * HEAD_DIM]
        keys_ref[head, pl.ds(at, count), HEAD_DIM:] = extra


def put_values(values_ref, rows):
    width = KV_HEADS * HEAD_DIM
    count = rows.shape[0]
    tall = KV_HEADS * VROWS
    row = lax.broadcasted_iota(jnp.int32, (tall, width), 0)
    column = lax.broadcasted_iota(jnp.int32, (tall, width), 1)
    head, inner = column // HEAD_DIM, column % HEAD_DIM
    pick = jnp.where(row == head * VROWS + inner, 1.0, 0.0).astype(BF16)
    turned = lax.dot_general(pick, rows, NT, preferred_element_type=F32)
    counting = lax.broadcasted_iota(jnp.int32, (tall, count), 0) % VROWS == HEAD_DIM
    values_ref[...] = jnp.where(counting, 1.0, turned).astype(BF16).reshape(KV_HEADS, VROWS, count)


def run_units(scores, finish, values, buffers):
    def first(group, block):
        held, top = buffers[block]
        x, floor = scores(group, block)
        held[...] = x
        highest = jnp.max(x, axis=0, keepdims=True)
        top[...] = highest if floor is None else jnp.maximum(highest, floor)

    def second(group, block):
        held, top = buffers[block]
        highest = top[...]
        weights = jnp.exp(held[...] - highest).astype(BF16)
        finish(group, block, highest, jnp.dot(values(group, block), weights, preferred_element_type=F32))

    first(0, 0)

    def step(group, carry):
        first(group, 1)
        second(group, 0)
        first(group + 1, 0)
        second(group, 1)
        return carry

    lax.fori_loop(0, KV_HEADS - 1, step, 0)
    last = KV_HEADS - 1
    first(last, 1)
    second(last, 0)
    second(last, 1)


def near(tokens_hbm, wq_hbm, pair_ref, inner_ref, outer_ref, q_hbm, acc_hbm, top_hbm,
         tokens_ref, wq_ref, q_ref, acc_ref, top_ref, sems, keys_ref, values_ref, sa, ta, sb, tb):
    rows = tokens_ref.shape[0]
    blocks = rows // BLOCK
    width = KV_HEADS * HEAD_DIM
    span = SHARE * HEAD_DIM
    me = lax.axis_index("seq")
    devices = lax.axis_size("seq")
    even = me % 2 == 0
    fetches = [pltpu.make_async_copy(tokens_hbm, tokens_ref, sems.at[KV_HEADS])]
    for group in range(KV_HEADS):
        fetches.append(pltpu.make_async_copy(wq_hbm.at[:, pl.ds(group * span, span)], wq_ref.at[group], sems.at[group]))
    for fetch in fetches:
        fetch.start()
    prev = jnp.where(even, outer_ref[...], inner_ref[...])
    follow = jnp.where(even, inner_ref[...], outer_ref[...])
    put_keys(keys_ref, prev[:, :width], 0, [jnp.where(me > 0, 0.0, MASKED)] * blocks)
    put_keys(keys_ref, pair_ref[:, :width], BLOCK, ())
    put_keys(keys_ref, follow[:, :width], BLOCK + rows, [jnp.where(me < devices - 1, 0.0, MASKED)] * blocks)
    put_values(values_ref, jnp.concatenate([prev[:, width:], pair_ref[:, width:], follow[:, width:]], axis=0))
    fetches[0].wait()
    lane = lax.broadcasted_iota(jnp.int32, (BLOCK, HEAD_DIM), 1)
    for group in range(KV_HEADS):
        fetches[1 + group].wait()
        part = jnp.dot(tokens_ref[...], wq_ref[group], preferred_element_type=F32)
        part = part.astype(BF16) * (1.0 / math.sqrt(HEAD_DIM))
        for block in range(blocks):
            extra = jnp.where(lane == block, 1.0, 0.0).astype(BF16)
            for head in range(SHARE):
                to = slice(head * BLOCK, (head + 1) * BLOCK)
                piece = part[block * BLOCK : (block + 1) * BLOCK, head * HEAD_DIM : (head + 1) * HEAD_DIM]
                q_ref[group, block, to, :HEAD_DIM] = piece
                q_ref[group, block, to, HEAD_DIM:] = extra
    keep = pltpu.make_async_copy(q_ref, q_hbm, sems.at[KV_HEADS + 1])
    keep.start()

    def scores(group, block):
        at = slice(block * BLOCK, block * BLOCK + BLOCK + rows)
        return lax.dot_general(keys_ref[group, at], q_ref[group, block], NT, preferred_element_type=F32), None

    def kept(group):
        return pltpu.make_async_copy(acc_ref.at[group], acc_hbm.at[group], sems.at[KV_HEADS + 2])

    def finish(group, block, highest, total):
        acc_ref[group, block] = total
        top_ref[group, block] = highest
        if block == blocks - 1:
            kept(group).start()

    def values(group, block):
        return values_ref[group, :, block * BLOCK : block * BLOCK + BLOCK + rows]

    run_units(scores, finish, values, ((sa, ta), (sb, tb)))
    keep_top = pltpu.make_async_copy(top_ref, top_hbm, sems.at[0])
    keep_top.start()
    keep.wait()
    pltpu.make_async_copy(acc_ref, acc_hbm, sems.at[KV_HEADS + 2]).wait()
    keep_top.wait()


def far(q_hbm, acc_hbm, top_hbm, mids_ref, coarse_ref, wout_hbm, out_hbm,
        q_ref, acc_ref, top_ref, wout_ref, out_ref, sems, rows_ref, keys_ref, values_ref, mixed_ref, sa, ta, sb, tb):
    fetches = [
        pltpu.make_async_copy(source, target, sems.at[at])
        for at, (source, target) in enumerate(
            ((q_hbm, q_ref), (top_hbm, top_ref), (acc_hbm, acc_ref), (wout_hbm, wout_ref))
        )
    ]
    for fetch in fetches:
        fetch.start()
    blocks = mixed_ref.shape[0]
    width = KV_HEADS * HEAD_DIM
    me = lax.axis_index("seq")
    groups = lax.axis_size("seq") // GROUP
    mine = me % GROUP
    runs = BLOCK // POOL
    per_device = runs * blocks
    mid_rows = GROUP * per_device
    spread = blocks * (groups - 1)
    swapped = pl.multiple_of(mine * per_device, per_device)
    for member in range(GROUP):
        rows_ref[member * per_device : (member + 1) * per_device] = mids_ref[member, :per_device]
    rows_ref[pl.ds(swapped, per_device)] = coarse_ref[:per_device]
    if coarse_ref.shape[0] > per_device:
        rows_ref[mid_rows:] = coarse_ref[per_device:]
    indices = [me * blocks + block for block in range(blocks)]
    row = lax.broadcasted_iota(jnp.int32, (mid_rows, HEAD_DIM), 0)
    mid_block = (me - mine + row // per_device) * blocks + row % per_device // runs
    put_keys(keys_ref, rows_ref[:mid_rows, :width], 0, [jnp.where(jnp.abs(mid_block - index) > 1, 0.0, MASKED) for index in indices])
    for start in range(0, coarse_ref.shape[0], per_device):
        row = lax.broadcasted_iota(jnp.int32, (per_device, HEAD_DIM), 0) + start
        other = (row % spread) // blocks + 1
        far_block = (((me // GROUP) ^ other) * GROUP + row // spread) * blocks + row % blocks
        bias = [jnp.where(jnp.abs(far_block - index) > 1, 0.0, MASKED) for index in indices]
        at = swapped if start == 0 else mid_rows + start - per_device
        put_keys(keys_ref, coarse_ref[start : start + per_device, :width], at, bias)
    put_values(values_ref, rows_ref[:, width:])
    fetches[0].wait()
    fetches[1].wait()
    fetches[2].wait()

    def scores(group, block):
        return lax.dot_general(keys_ref[group], q_ref[group, block], NT, preferred_element_type=F32), top_ref[group, block]

    def finish(group, block, highest, total):
        total = total + acc_ref[group, block] * jnp.exp(top_ref[group, block] - highest)
        share = total[:HEAD_DIM] / total[HEAD_DIM : HEAD_DIM + 1]
        share = share.astype(BF16)
        for head in range(SHARE):
            to = pl.multiple_of((group * SHARE + head) * HEAD_DIM, HEAD_DIM)
            mixed_ref[block, pl.ds(to, HEAD_DIM), :] = share[:, head * BLOCK : (head + 1) * BLOCK]

    run_units(scores, finish, lambda group, block: values_ref[group], ((sa, ta), (sb, tb)))
    fetches[3].wait()
    stores = []
    for block in range(blocks):
        at = pl.ds(block * BLOCK, BLOCK)
        out_ref[at] = lax.dot_general(mixed_ref[block], wout_ref[...], TN, preferred_element_type=F32).astype(BF16)
        store = pltpu.make_async_copy(out_ref.at[at], out_hbm.at[at], sems.at[4 + block])
        store.start()
        stores.append(store)
    for store in stores:
        store.wait()


def body(tokens, w_query, w_key, w_value, w_out):
    devices = lax.axis_size("seq")
    rows, model = tokens.shape
    blocks = rows // BLOCK
    width = KV_HEADS * HEAD_DIM
    stack = SHARE * BLOCK
    per_device = rows // POOL
    shape = jax.ShapeDtypeStruct
    dma = pltpu.SemaphoreType.DMA

    def call(kernel, out_shape, in_specs, out_specs, scratch, flops, name, kib=53000):
        return pl.pallas_call(
            kernel,
            out_shape=out_shape,
            in_specs=in_specs,
            out_specs=out_specs,
            scratch_shapes=scratch,
            compiler_params=pltpu.CompilerParams(vmem_limit_bytes=kib * 2**10),
            cost_estimate=pl.CostEstimate(flops=flops, bytes_accessed=2**20, transcendentals=0),
            name=name,
        )

    def slots(keys):
        return [pltpu.VMEM((keys, stack), F32), pltpu.VMEM((1, stack), F32)] * 2

    half = shape((BLOCK, 2 * width), BF16)
    pair, mid, coarse, inner, outer = call(
        project_pair,
        [shape((rows, 2 * width), BF16), shape((per_device, 2 * width), BF16), shape((blocks, 2 * width), BF16), half, half],
        [HBM] * 3,
        [VMEM] * 5,
        [pltpu.VMEM((rows, model), BF16)] + [pltpu.VMEM((model, width), BF16)] * 2 + [dma((3,))],
        2 * 10**9,
        "pair",
        54000,
    )(tokens, w_key, w_value)

    spread = coarse
    level = GROUP
    while level < devices:
        spread = jnp.concatenate([spread, swap(spread, level)], axis=0)
        level *= 2
    spread = spread[blocks:]
    inner = swap(inner, 1)
    links = [(i, i + 1) for i in range(1, devices - 1, 2)]
    outer = lax.ppermute(outer, "seq", links + [(b, a) for a, b in links])
    payload = jnp.concatenate([mid, spread], axis=0)
    payload = jnp.broadcast_to(payload[None], (GROUP, *payload.shape))
    members = [list(range(at, at + GROUP)) for at in range(0, devices, GROUP)]
    arrived = lax.all_to_all(payload, "seq", 0, 0, axis_index_groups=members)

    state = [shape((KV_HEADS, blocks, stack, WIDE), BF16), shape((KV_HEADS, blocks, VROWS, stack), F32), shape((KV_HEADS, blocks, 1, stack), F32)]
    held = [pltpu.VMEM(part.shape, part.dtype) for part in state]
    q, acc, top = call(
        near,
        state,
        [HBM, HBM, VMEM, VMEM, VMEM],
        [HBM] * 3,
        [pltpu.VMEM((rows, model), BF16), pltpu.VMEM((KV_HEADS, model, SHARE * HEAD_DIM), BF16)]
        + held
        + [dma((KV_HEADS + 3,)), pltpu.VMEM((KV_HEADS, rows + 2 * BLOCK, WIDE), BF16), pltpu.VMEM((KV_HEADS, VROWS, rows + 2 * BLOCK), BF16)]
        + slots(rows + BLOCK),
        10**10,
        "near",
    )(tokens, w_query, tied(pair, payload), inner, outer)

    coarse_far = arrived[:, per_device:].reshape(-1, 2 * width)
    keys = (GROUP - 1) * per_device + coarse_far.shape[0]
    return call(
        far,
        shape((rows, w_out.shape[1]), BF16),
        [HBM] * 3 + [VMEM, VMEM, HBM],
        HBM,
        held
        + [
            pltpu.VMEM(w_out.shape, BF16),
            pltpu.VMEM((rows, w_out.shape[1]), BF16),
            dma((4 + blocks,)),
            pltpu.VMEM((keys, 2 * width), BF16),
            pltpu.VMEM((KV_HEADS, keys, WIDE), BF16),
            pltpu.VMEM((KV_HEADS, VROWS, keys), BF16),
            pltpu.VMEM((blocks, HEADS * HEAD_DIM, BLOCK), BF16),
        ]
        + slots(keys),
        8 * 10**9,
        "far",
    )(q, acc, top, arrived, coarse_far, w_out)


def solution(mesh):
    placed = (P("seq", None), P(), P(), P(), P())
    return jax.shard_map(body, mesh=mesh, in_specs=placed, out_specs=P("seq", None), check_vma=False)
```

time: 56.9 us -> 43.8 us (0.77)
  local copies, waits for them, and re-layouts: 14.6 us -> 0.92 us
  waiting for transfers between devices: 8.36 us -> 4.34 us
  Pallas kernels: 22.7 us -> 26.1 us
  starting transfers between devices: 10.8 us -> 12.1 us
    unnamed x25 -> x2, local copies, waits for them, and re-layouts: 14.5 us -> 0.01 us
    ppermute x6 -> x2, waiting for transfers between devices: 8.36 us -> 4.33 us  [swap(): return lax.ppermute(rows, 'seq', [(i, i ^ apart) for i in range(count)])]
    all_to_all x0 -> x1, starting transfers between devices: none -> 3.59 us  [body(): arrived = lax.all_to_all(payload, 'seq', 0, 0, axis_index_groups=members)]
    pallas_call x5 -> x3, Pallas kernels: 22.7 us -> 26.1 us  [the longest x1 13.1 us: body(): call(near, state, [HBM, HBM, VMEM, VMEM, VMEM], [HBM] * 3, [pltpu.VMEM((r...]
    ppermute x6 -> x2, starting transfers between devices: 10.2 us -> 7.85 us  [swap(): return lax.ppermute(rows, 'seq', [(i, i ^ apart) for i in range(count)])]
    broadcast_in_dim x0 -> x1, local copies, waits for them, and re-layouts: none -> 0.88 us  [body(): payload = jnp.broadcast_to(payload[None], (GROUP, *payload.shape))]
  transfers between devices with their start and end apart: 7 -> 4, of which waited for: 4 -> 1; matrix products, arithmetic and copies ran while one was open for 0% -> 2% of each run, Pallas kernels for 17% -> 30%
where the time goes in v3:
time: 43.8 us; the launch traced here: 43.5 us
  Pallas kernels  26.1 us (60%)
  starting transfers between devices  12.1 us (28%)
  waiting for transfers between devices  4.34 us (10%)
  local copies, waits for them, and re-layouts  0.92 us (2%)
    pallas_call x1, Pallas kernels, body(): call(near, state, [HBM, HBM, VMEM, VMEM, VMEM], [HBM] * 3, [pltpu.VMEM((r...  13.1 us
    pallas_call x1, Pallas kernels, body(): call(far, shape((rows, w_out.shape[1]), BF16), [HBM] * 3 + [VMEM, VMEM, H...  9.7 us
    ppermute x2, starting transfers between devices, swap(): return lax.ppermute(rows, 'seq', [(i, i ^ apart) for i in range(count)])  7.85 us
    ppermute x2, waiting for transfers between devices, swap(): return lax.ppermute(rows, 'seq', [(i, i ^ apart) for i in range(count)])  4.33 us
    all_to_all x1, starting transfers between devices, body(): arrived = lax.all_to_all(payload, 'seq', 0, 0, axis_index_groups=members)  3.59 us
    pallas_call x1, Pallas kernels, body(): call(project_pair, [shape((rows, 2 * width), BF16), shape((per_device, 2...  3.28 us
    broadcast_in_dim x1, local copies, waits for them, and re-layouts, body(): payload = jnp.broadcast_to(payload[None], (GROUP, *payload.shape))  0.88 us
  transfers between devices with their start and end apart: 4, of which 1 were waited for; matrix products, arithmetic and copies ran while one was open for 2% of the time, Pallas kernels for 30%

profile of v3, /device:TPU:0, one launch (start us, length us, event | category | flops | bytes accessed | tf_op | source)
XLA Modules:
  0.0 43.5 jit_solution(1848065864534765128)
XLA Ops:
  0.0 0.0 copy-start
  0.0 3.3 %pair.1 = (bf16[512,512]{1,0:T(8,128)(2,1)S(1)}, bf16[32,512]{1,0:T(8,128)(2,1)S(1)}, bf16[2,512]{1,0:T(2,128)(2,1)S(1)}, bf16[256,512]{1,0:T(8,128)(2,1)S(1)}, bf16[256,512]{1,0:T(8,128)(2,1)S(1)}) custom-call(bf16[512,1024]{1,0:T(8,128)(2,1)} %tokens_hbm.3, bf16[1024,256]{1,0:T(8,128)(2,1)} %wk_hbm.1, bf16[1024,256]{1,0:T(8,128)(2,1)} %wv_hbm.1), custom_call_target="tpu_custom_call" | custom-call | flops 2000000000 | bytes 1048576 | tf_op jit(solution)/shard_map/pair/pallas_call | solution.py:273
  3.3 0.5 %collective-permute-start.1 = (bf16[256,512]{1,0:T(8,128)(2,1)S(1)}, bf16[256,512]{1,0:T(8,128)(2,1)S(1)}, u32[]{:S(2)}, u32[]{:S(2)}) collective-permute-start(bf16[256,512]{1,0:T(8,128)(2,1)S(1)} %get-tuple-element.18), channel_id=1, source_target_pairs={{0,1},{1,0},{2,3},{3,2},{4,5},{5,4},{6,7},{7,6},{8,9},{9,8},{10,11... | collective-permute-start | bytes 786440 | tf_op jit(solution)/shard_map/ppermute | solution.py:30
  3.8 0.7 %collective-permute-start.2 = (bf16[256,512]{1,0:T(8,128)(2,1)S(1)}, bf16[256,512]{1,0:T(8,128)(2,1)S(1)}, u32[]{:S(2)}, u32[]{:S(2)}) collective-permute-start(bf16[256,512]{1,0:T(8,128)(2,1)S(1)} %get-tuple-element.19), channel_id=1, source_target_pairs={{1,2},{3,4},{5,6},{7,8},{9,10},{11,12},{13,14},{15,16},{17,18},{19... | collective-permute-start | bytes 786440 | tf_op jit(solution)/shard_map/ppermute | solution.py:292
  4.5 7.3 %collective-permute-start = (bf16[2,512]{1,0:T(2,128)(2,1)S(1)}, bf16[2,512]{1,0:T(2,128)(2,1)S(1)}, u32[]{:S(2)}, u32[]{:S(2)}) collective-permute-start(bf16[2,512]{1,0:T(2,128)(2,1)S(1)} %get-tuple-element.16), channel_id=1, source_target_pairs={{0,16},{1,17},{2,18},{3,19},{4,20},{5,21},{6,22},{7,23},{8,24},{9,... | collective-permute-start | bytes 6152 | tf_op jit(solution)/shard_map/ppermute | solution.py:30
  11.8 4.3 %collective-permute-done = bf16[2,512]{1,0:T(2,128)(2,1)S(1)} collective-permute-done((bf16[2,512]{1,0:T(2,128)(2,1)S(1)}, bf16[2,512]{1,0:T(2,128)(2,1)S(1)}, u32[]{:S(2)}, u32[]{:S(2)}) %collective-permute-start) | collective-permute-done | bytes 2080 | tf_op jit(solution)/shard_map/ppermute | solution.py:30
  16.1 0.9 %broadcast_in_dim.2 = bf16[16,34,512]{2,1,0:T(8,128)(2,1)} broadcast(bf16[34,512]{1,0:T(8,128)(2,1)S(1)} %pad_maximum_fusion), dimensions={1,2} | broadcast | bytes 591872 | tf_op jit(solution)/shard_map/broadcast_in_dim | solution.py:294
  17.0 3.6 %all-to-all-start = ((bf16[16,34,512]{2,1,0:T(8,128)(2,1)}), bf16[16,34,512]{2,1,0:T(8,128)(2,1)S(1)}, u32[]{:S(2)}, u32[]{:S(2)}) async-start(bf16[16,34,512]{2,1,0:T(8,128)(2,1)} %broadcast_in_dim.2), calls=%async_computation | async-start | bytes 1310720 | tf_op jit(solution)/shard_map/all_to_all | solution.py:296
  20.6 0.0 collective-permute-done.1.inner_ref
  20.6 0.0 collective-permute-done.2.outer_ref
  20.6 0.0 copy-done
  20.7 13.1 %near.1 = (bf16[4,2,1024,128]{3,2,1,0:T(8,128)(2,1)}, f32[4,2,80,1024]{3,2,1,0:T(8,128)}, f32[4,2,1,1024]{3,2,1,0:T(1,128)S(1)}) custom-call(bf16[512,1024]{1,0:T(8,128)(2,1)S(1)} %copy-done, bf16[1024,1024]{1,0:T(8,128)(2,1)} %wq_hbm.1, bf16[512,512]{1,0:T(8,128)(2,1)S(1)} %get-tuple-element.17.pair_ref, ...), custom_call_target="tpu_custom_call" | custom-call | flops 10000000000 | bytes 1048576 | tf_op jit(solution)/shard_map/near/pallas_call | solution.py:300
  33.8 0.0 all-to-all-done.mids_ref
  33.8 9.7 %far.1 = bf16[512,1024]{1,0:T(8,128)(2,1)} custom-call(bf16[4,2,1024,128]{3,2,1,0:T(8,128)(2,1)} %get-tuple-element.20.q_hbm, f32[4,2,80,1024]{3,2,1,0:T(8,128)} %get-tuple-element.21.acc_hbm, f32[4,2,1,1024]{3,2,1,0:T(1,128)S(1)} %get-tuple-element.22.top_hbm, bf16[16,34,512]{2,1,0:T(8,128)(2,1)S(1)} %all-to-all-done.mids_ref, ...), custom_call_target="tpu_custom_call" | custom-call | flops 8000000000 | bytes 1048576 | tf_op jit(solution)/shard_map/far/pallas_call | solution.py:315
  (3 shorter events, 0.0 us)
Async XLA Ops:
  0.0 20.6 %copy-start = (bf16[512,1024]{1,0:T(8,128)(2,1)S(1)}, bf16[512,1024]{1,0:T(8,128)(2,1)}, u32[]{:S(2)}) copy-start(bf16[512,1024]{1,0:T(8,128)(2,1)} %tokens_hbm.3) | copy-start | bytes 3145732
  3.3 17.3 %collective-permute-start.1 = (bf16[256,512]{1,0:T(8,128)(2,1)S(1)}, bf16[256,512]{1,0:T(8,128)(2,1)S(1)}, u32[]{:S(2)}, u32[]{:S(2)}) collective-permute-start(bf16[256,512]{1,0:T(8,128)(2,1)S(1)} %get-tuple-element.18), channel_id=1, source_target_pairs={{0,1},{1,0},{2,3},{3,2},{4,5},{5,4},{6,7},{7,6},{8,9},{9,8},{10,11... | collective-permute-start | bytes 786440 | tf_op jit(solution)/shard_map/ppermute | solution.py:30
  3.8 16.8 %collective-permute-start.2 = (bf16[256,512]{1,0:T(8,128)(2,1)S(1)}, bf16[256,512]{1,0:T(8,128)(2,1)S(1)}, u32[]{:S(2)}, u32[]{:S(2)}) collective-permute-start(bf16[256,512]{1,0:T(8,128)(2,1)S(1)} %get-tuple-element.19), channel_id=1, source_target_pairs={{1,2},{3,4},{5,6},{7,8},{9,10},{11,12},{13,14},{15,16},{17,18},{19... | collective-permute-start | bytes 786440 | tf_op jit(solution)/shard_map/ppermute | solution.py:292
  4.5 11.7 %collective-permute-start = (bf16[2,512]{1,0:T(2,128)(2,1)S(1)}, bf16[2,512]{1,0:T(2,128)(2,1)S(1)}, u32[]{:S(2)}, u32[]{:S(2)}) collective-permute-start(bf16[2,512]{1,0:T(2,128)(2,1)S(1)} %get-tuple-element.16), channel_id=1, source_target_pairs={{0,16},{1,17},{2,18},{3,19},{4,20},{5,21},{6,22},{7,23},{8,24},{9,... | collective-permute-start | bytes 6152 | tf_op jit(solution)/shard_map/ppermute | solution.py:30
  17.0 16.7 %all-to-all-start = ((bf16[16,34,512]{2,1,0:T(8,128)(2,1)}), bf16[16,34,512]{2,1,0:T(8,128)(2,1)S(1)}, u32[]{:S(2)}, u32[]{:S(2)}) async-start(bf16[16,34,512]{2,1,0:T(8,128)(2,1)} %broadcast_in_dim.2), calls=%async_computation | async-start | bytes 1310720 | tf_op jit(solution)/shard_map/all_to_all | solution.py:296

commit v4 on v3

--- a/solution.py
+++ b/solution.py
@@ -34,34 +34,67 @@
     return lax.optimization_barrier((rows, *others))[0]
 
 
-def project_pair(tokens_hbm, wk_hbm, wv_hbm, pair_ref, mid_ref, coarse_ref, inner_ref, outer_ref, tokens_ref, wk_ref, wv_ref, sems):
-    copies = [
-        pltpu.make_async_copy(source, target, sems.at[at])
-        for at, (source, target) in enumerate(((wk_hbm, wk_ref), (tokens_hbm, tokens_ref), (wv_hbm, wv_ref)))
-    ]
-    for copy in copies:
-        copy.start()
-    copies[0].wait()
-    copies[1].wait()
-    tokens = tokens_ref[...]
-    rows = tokens.shape[0]
-    width = wk_ref.shape[1]
-    for part, weight in enumerate((wk_ref, wv_ref)):
-        if part == 1:
-            copies[2].wait()
-        at = slice(part * width, (part + 1) * width)
-        held = jnp.dot(tokens, weight[...], preferred_element_type=F32).astype(BF16)
-        pair_ref[:, at] = held
-        for factor, target in ((POOL, mid_ref), (BLOCK, coarse_ref)):
-            kept = target.shape[0]
-            first = lax.broadcasted_iota(jnp.int32, (kept, rows), 0) * factor
-            inside = lax.broadcasted_iota(jnp.int32, (kept, rows), 1) - first
-            share = jnp.where((inside >= 0) & (inside < factor), 1.0 / factor, 0.0)
-            mean = jnp.dot(share.astype(BF16), held, preferred_element_type=F32)
-            target[:, at] = mean.astype(BF16)
+def project_pair(tokens_hbm, wk_hbm, wv_hbm, pair_ref, mid_ref, coarse_ref, inner_ref, outer_ref, tokens_ref, weight_ref, sems):
+    rows = tokens_ref.shape[0]
+    width = wk_hbm.shape[1]
+    blocks = rows // BLOCK
+    fetches = [pltpu.make_async_copy(wk_hbm, weight_ref.at[:, pl.ds(0, width)], sems.at[0])]
+    fetches.append(pltpu.make_async_copy(wv_hbm, weight_ref.at[:, pl.ds(width, width)], sems.at[1]))
+    for block in range(blocks):
+        at = pl.ds(block * BLOCK, BLOCK)
+        fetches.append(pltpu.make_async_copy(tokens_hbm.at[at], tokens_ref.at[at], sems.at[2 + block]))
+    for fetch in fetches:
+        fetch.start()
     even = lax.axis_index("seq") % 2 == 0
-    inner_ref[...] = jnp.where(even, pair_ref[rows - BLOCK :], pair_ref[:BLOCK])
-    outer_ref[...] = jnp.where(even, pair_ref[:BLOCK], pair_ref[rows - BLOCK :])
+    runs = BLOCK // POOL
+    tall = 3 * runs // 2
+    row = lax.broadcasted_iota(jnp.int32, (tall, BLOCK), 0)
+    column = lax.broadcasted_iota(jnp.int32, (tall, BLOCK), 1)
+    share = jnp.where(row < runs, jnp.where(column // POOL == row, 1.0 / POOL, 0.0), jnp.where(row == runs, 1.0 / BLOCK, 0.0))
+    share = share.astype(BF16)
+    fetches[0].wait()
+    fetches[1].wait()
+    kept = []
+    for block in range(blocks):
+        at = slice(block * BLOCK, (block + 1) * BLOCK)
+        fetches[2 + block].wait()
+        held = jnp.dot(tokens_ref[at], weight_ref[...], preferred_element_type=F32).astype(BF16)
+        pair_ref[at] = held
+        kept.append(held)
+        mean = jnp.dot(share, held, preferred_element_type=F32)
+        mid_ref[block * runs : (block + 1) * runs] = mean[:runs].astype(BF16)
+        coarse_ref[block : block + 1] = mean[runs : runs + 1].astype(BF16)
+    inner_ref[...] = jnp.where(even, kept[-1], kept[0])
+    outer_ref[...] = jnp.where(even, kept[0], kept[-1])
+
+
+def query(tokens_hbm, wq_hbm, order_ref, q_hbm, tokens_ref, wq_ref, q_ref, sems):
+    rows = tokens_ref.shape[0]
+    blocks = rows // BLOCK
+    span = SHARE * HEAD_DIM
+    fetches = [pltpu.make_async_copy(tokens_hbm, tokens_ref, sems.at[KV_HEADS])]
+    for group in range(KV_HEADS):
+        fetches.append(pltpu.make_async_copy(wq_hbm.at[:, pl.ds(group * span, span)], wq_ref.at[group], sems.at[group]))
+    for fetch in fetches:
+        fetch.start()
+    lane = lax.broadcasted_iota(jnp.int32, (BLOCK, HEAD_DIM), 1)
+    fetches[0].wait()
+    keeps = []
+    for group in range(KV_HEADS):
+        fetches[1 + group].wait()
+        part = jnp.dot(tokens_ref[...], wq_ref[group], preferred_element_type=F32)
+        part = part.astype(BF16) * (1.0 / math.sqrt(HEAD_DIM))
+        for block in range(blocks):
+            extra = jnp.where(lane == block, 1.0, 0.0).astype(BF16)
+            for head in range(SHARE):
+                to = slice(head * BLOCK, (head + 1) * BLOCK)
+                piece = part[block * BLOCK : (block + 1) * BLOCK, head * HEAD_DIM : (head + 1) * HEAD_DIM]
+                q_ref[group, block, to, :HEAD_DIM] = piece
+                q_ref[group, block, to, HEAD_DIM:] = extra
+        keeps.append(pltpu.make_async_copy(q_ref.at[group], q_hbm.at[group], sems.at[KV_HEADS + 1 + group]))
+        keeps[-1].start()
+    for keep in keeps:
+        keep.wait()
 
 
 def put_keys(keys_ref, rows, at, biases):
@@ -119,48 +152,30 @@
     second(last, 1)
 
 
-def near(tokens_hbm, wq_hbm, pair_ref, inner_ref, outer_ref, q_hbm, acc_hbm, top_hbm,
-         tokens_ref, wq_ref, q_ref, acc_ref, top_ref, sems, keys_ref, values_ref, sa, ta, sb, tb):
-    rows = tokens_ref.shape[0]
+def near(q_hbm, pair_ref, inner_ref, outer_ref, acc_hbm, top_hbm,
+         q_ref, acc_ref, top_ref, sems, keys_ref, values_ref, sa, ta, sb, tb):
+    fetch = pltpu.make_async_copy(q_hbm, q_ref, sems.at[0])
+    fetch.start()
+    rows = pair_ref.shape[0]
     blocks = rows // BLOCK
     width = KV_HEADS * HEAD_DIM
-    span = SHARE * HEAD_DIM
     me = lax.axis_index("seq")
     devices = lax.axis_size("seq")
     even = me % 2 == 0
-    fetches = [pltpu.make_async_copy(tokens_hbm, tokens_ref, sems.at[KV_HEADS])]
-    for group in range(KV_HEADS):
-        fetches.append(pltpu.make_async_copy(wq_hbm.at[:, pl.ds(group * span, span)], wq_ref.at[group], sems.at[group]))
-    for fetch in fetches:
-        fetch.start()
     prev = jnp.where(even, outer_ref[...], inner_ref[...])
     follow = jnp.where(even, inner_ref[...], outer_ref[...])
     put_keys(keys_ref, prev[:, :width], 0, [jnp.where(me > 0, 0.0, MASKED)] * blocks)
     put_keys(keys_ref, pair_ref[:, :width], BLOCK, ())
     put_keys(keys_ref, follow[:, :width], BLOCK + rows, [jnp.where(me < devices - 1, 0.0, MASKED)] * blocks)
     put_values(values_ref, jnp.concatenate([prev[:, width:], pair_ref[:, width:], follow[:, width:]], axis=0))
-    fetches[0].wait()
-    lane = lax.broadcasted_iota(jnp.int32, (BLOCK, HEAD_DIM), 1)
-    for group in range(KV_HEADS):
-        fetches[1 + group].wait()
-        part = jnp.dot(tokens_ref[...], wq_ref[group], preferred_element_type=F32)
-        part = part.astype(BF16) * (1.0 / math.sqrt(HEAD_DIM))
-        for block in range(blocks):
-            extra = jnp.where(lane == block, 1.0, 0.0).astype(BF16)
-            for head in range(SHARE):
-                to = slice(head * BLOCK, (head + 1) * BLOCK)
-                piece = part[block * BLOCK : (block + 1) * BLOCK, head * HEAD_DIM : (head + 1) * HEAD_DIM]
-                q_ref[group, block, to, :HEAD_DIM] = piece
-                q_ref[group, block, to, HEAD_DIM:] = extra
-    keep = pltpu.make_async_copy(q_ref, q_hbm, sems.at[KV_HEADS + 1])
-    keep.start()
+    fetch.wait()
 
     def scores(group, block):
         at = slice(block * BLOCK, block * BLOCK + BLOCK + rows)
         return lax.dot_general(keys_ref[group, at], q_ref[group, block], NT, preferred_element_type=F32), None
 
     def kept(group):
-        return pltpu.make_async_copy(acc_ref.at[group], acc_hbm.at[group], sems.at[KV_HEADS + 2])
+        return pltpu.make_async_copy(acc_ref.at[group], acc_hbm.at[group], sems.at[1])
 
     def finish(group, block, highest, total):
         acc_ref[group, block] = total
@@ -174,8 +189,7 @@
     run_units(scores, finish, values, ((sa, ta), (sb, tb)))
     keep_top = pltpu.make_async_copy(top_ref, top_hbm, sems.at[0])
     keep_top.start()
-    keep.wait()
-    pltpu.make_async_copy(acc_ref, acc_hbm, sems.at[KV_HEADS + 2]).wait()
+    pltpu.make_async_copy(acc_ref, acc_hbm, sems.at[1]).wait()
     keep_top.wait()
 
 
@@ -216,9 +230,8 @@
         at = swapped if start == 0 else mid_rows + start - per_device
         put_keys(keys_ref, coarse_ref[start : start + per_device, :width], at, bias)
     put_values(values_ref, rows_ref[:, width:])
-    fetches[0].wait()
-    fetches[1].wait()
-    fetches[2].wait()
+    for fetch in fetches[:3]:
+        fetch.wait()
 
     def scores(group, block):
         return lax.dot_general(keys_ref[group], q_ref[group, block], NT, preferred_element_type=F32), top_ref[group, block]
@@ -275,12 +288,14 @@
         [shape((rows, 2 * width), BF16), shape((per_device, 2 * width), BF16), shape((blocks, 2 * width), BF16), half, half],
         [HBM] * 3,
         [VMEM] * 5,
-        [pltpu.VMEM((rows, model), BF16)] + [pltpu.VMEM((model, width), BF16)] * 2 + [dma((3,))],
+        [pltpu.VMEM((rows, model), BF16), pltpu.VMEM((model, 2 * width), BF16), dma((2 + blocks,))],
         2 * 10**9,
         "pair",
         54000,
     )(tokens, w_key, w_value)
 
+    state = [shape((KV_HEADS, blocks, stack, WIDE), BF16), shape((KV_HEADS, blocks, VROWS, stack), F32), shape((KV_HEADS, blocks, 1, stack), F32)]
+    held = [pltpu.VMEM(part.shape, part.dtype) for part in state]
     spread = coarse
     level = GROUP
     while level < devices:
@@ -288,27 +303,35 @@
         level *= 2
     spread = spread[blocks:]
     inner = swap(inner, 1)
+    q = call(
+        query,
+        state[0],
+        [HBM, HBM, VMEM],
+        HBM,
+        [pltpu.VMEM((rows, model), BF16), pltpu.VMEM((KV_HEADS, model, SHARE * HEAD_DIM), BF16), held[0], dma((2 * KV_HEADS + 1,))],
+        2 * 10**9,
+        "query",
+        55000,
+    )(tokens, w_query, coarse)
+    spread = tied(spread, q)
     links = [(i, i + 1) for i in range(1, devices - 1, 2)]
-    outer = lax.ppermute(outer, "seq", links + [(b, a) for a, b in links])
+    outer = lax.ppermute(tied(outer, spread), "seq", links + [(b, a) for a, b in links])
     payload = jnp.concatenate([mid, spread], axis=0)
     payload = jnp.broadcast_to(payload[None], (GROUP, *payload.shape))
     members = [list(range(at, at + GROUP)) for at in range(0, devices, GROUP)]
     arrived = lax.all_to_all(payload, "seq", 0, 0, axis_index_groups=members)
 
-    state = [shape((KV_HEADS, blocks, stack, WIDE), BF16), shape((KV_HEADS, blocks, VROWS, stack), F32), shape((KV_HEADS, blocks, 1, stack), F32)]
-    held = [pltpu.VMEM(part.shape, part.dtype) for part in state]
-    q, acc, top = call(
+    acc, top = call(
         near,
-        state,
-        [HBM, HBM, VMEM, VMEM, VMEM],
-        [HBM] * 3,
-        [pltpu.VMEM((rows, model), BF16), pltpu.VMEM((KV_HEADS, model, SHARE * HEAD_DIM), BF16)]
-        + held
-        + [dma((KV_HEADS + 3,)), pltpu.VMEM((KV_HEADS, rows + 2 * BLOCK, WIDE), BF16), pltpu.VMEM((KV_HEADS, VROWS, rows + 2 * BLOCK), BF16)]
+        state[1:],
+        [HBM, VMEM, VMEM, VMEM],
+        [HBM] * 2,
+        held
+        + [dma((2,)), pltpu.VMEM((KV_HEADS, rows + 2 * BLOCK, WIDE), BF16), pltpu.VMEM((KV_HEADS, VROWS, rows + 2 * BLOCK), BF16)]
         + slots(rows + BLOCK),
         10**10,
         "near",
-    )(tokens, w_query, tied(pair, payload), inner, outer)
+    )(q, tied(pair, payload), inner, outer)
 
     coarse_far = arrived[:, per_device:].reshape(-1, 2 * width)
     keys = (GROUP - 1) * per_device + coarse_far.shape[0]

time: 43.8 us -> 42.8 us (0.977); the launches traced: 43.5 us -> 42 us
  waiting for transfers between devices: 4.34 us -> 1.53 us
  Pallas kernels: 26.1 us -> 27.9 us
  starting transfers between devices: 12.1 us -> 11.5 us
    ppermute x2, waiting for transfers between devices: 4.33 us -> 0.01 us  [swap(): return lax.ppermute(rows, 'seq', [(i, i ^ apart) for i in range(count)])]
    ppermute x2, starting transfers between devices: 7.85 us -> 4.1 us  [swap(): return lax.ppermute(rows, 'seq', [(i, i ^ apart) for i in range(count)])]
    all_to_all x1, starting transfers between devices: 3.59 us -> 6.72 us  [body(): arrived = lax.all_to_all(payload, 'seq', 0, 0, axis_index_groups=members)]
    pallas_call x1 -> x2, Pallas kernels: 13.1 us -> 15.7 us  [the longest x1 10.4 us: body(): call(near, state[1:], [HBM, VMEM, VMEM, VMEM], [HBM] * 2, held + [dma((2,...]
    all_to_all x1, waiting for transfers between devices: 0.01 us -> 1.52 us  [body(): arrived = lax.all_to_all(payload, 'seq', 0, 0, axis_index_groups=members)]
    pallas_call x1, Pallas kernels: 3.28 us -> 2.52 us  [body(): call(project_pair, [shape((rows, 2 * width), BF16), shape((per_device, 2...]
  transfers between devices with their start and end apart: 4 -> 4, of which waited for: 1 -> 1; matrix products, arithmetic and copies ran while one was open for 2% -> 2% of each run, Pallas kernels for 30% -> 37%
where the time goes in v4:
time: 42.8 us; the launch traced here: 42 us
  Pallas kernels  27.9 us (65%)
  starting transfers between devices  11.5 us (27%)
  waiting for transfers between devices  1.53 us (4%)
  local copies, waits for them, and re-layouts  0.92 us (2%)
    pallas_call x1, Pallas kernels, body(): call(near, state[1:], [HBM, VMEM, VMEM, VMEM], [HBM] * 2, held + [dma((2,...  10.4 us
    pallas_call x1, Pallas kernels, body(): call(far, shape((rows, w_out.shape[1]), BF16), [HBM] * 3 + [VMEM, VMEM, H...  9.7 us
    all_to_all x1, starting transfers between devices, body(): arrived = lax.all_to_all(payload, 'seq', 0, 0, axis_index_groups=members)  6.72 us
    pallas_call x1, Pallas kernels, body(): call(query, state[0], [HBM, HBM, VMEM], HBM, [pltpu.VMEM((rows, model), B...  5.3 us
    ppermute x2, starting transfers between devices, swap(): return lax.ppermute(rows, 'seq', [(i, i ^ apart) for i in range(count)])  4.1 us
    pallas_call x1, Pallas kernels, body(): call(project_pair, [shape((rows, 2 * width), BF16), shape((per_device, 2...  2.52 us
    all_to_all x1, waiting for transfers between devices, body(): arrived = lax.all_to_all(payload, 'seq', 0, 0, axis_index_groups=members)  1.52 us
    broadcast_in_dim x1, local copies, waits for them, and re-layouts, body(): payload = jnp.broadcast_to(payload[None], (GROUP, *payload.shape))  0.88 us
  transfers between devices with their start and end apart: 4, of which 1 were waited for; matrix products, arithmetic and copies ran while one was open for 2% of the time, Pallas kernels for 37%

profile of v4, /device:TPU:0, one launch (start us, length us, event | category | flops | bytes accessed | tf_op | source)
XLA Modules:
  0.0 42.0 jit_solution(1193996967525824855)
XLA Ops:
  0.0 2.5 %pair.1 = (bf16[512,512]{1,0:T(8,128)(2,1)S(1)}, bf16[32,512]{1,0:T(8,128)(2,1)S(1)}, bf16[2,512]{1,0:T(2,128)(2,1)S(1)}, bf16[256,512]{1,0:T(8,128)(2,1)S(1)}, bf16[256,512]{1,0:T(8,128)(2,1)S(1)}) custom-call(bf16[512,1024]{1,0:T(8,128)(2,1)} %tokens_hbm.3, bf16[1024,256]{1,0:T(8,128)(2,1)} %wk_hbm.1, bf16[1024,256]{1,0:T(8,128)(2,1)} %wv_hbm.1), custom_call_target="tpu_custom_call" | custom-call | flops 2000000000 | bytes 1048576 | tf_op jit(solution)/shard_map/pair/pallas_call | solution.py:286
  2.5 4.1 %collective-permute-start = (bf16[2,512]{1,0:T(2,128)(2,1)S(1)}, bf16[2,512]{1,0:T(2,128)(2,1)S(1)}, u32[]{:S(2)}, u32[]{:S(2)}) collective-permute-start(bf16[2,512]{1,0:T(2,128)(2,1)S(1)} %get-tuple-element.15.order_ref), channel_id=1, source_target_pairs={{0,16},{1,17},{2,18},{3,19},{4,20},{5,21},{6,22},{7,23},{8,24},{9,... | collective-permute-start | bytes 6152 | tf_op jit(solution)/shard_map/ppermute | solution.py:30
  6.6 0.0 collective-permute-start.1
  6.6 5.3 %query.1.q_hbm = bf16[4,2,1024,128]{3,2,1,0:T(8,128)(2,1)} custom-call(bf16[512,1024]{1,0:T(8,128)(2,1)} %tokens_hbm.3, bf16[1024,1024]{1,0:T(8,128)(2,1)} %wq_hbm.1, bf16[2,512]{1,0:T(2,128)(2,1)S(1)} %get-tuple-element.15.order_ref), custom_call_target="tpu_custom_call" | custom-call | flops 2000000000 | bytes 1048576 | tf_op jit(solution)/shard_map/query/pallas_call | solution.py:306
  11.9 0.0 collective-permute-done
  12.0 0.7 %collective-permute-start.2 = (bf16[256,512]{1,0:T(8,128)(2,1)S(1)}, bf16[256,512]{1,0:T(8,128)(2,1)S(1)}, u32[]{:S(2)}, u32[]{:S(2)}) collective-permute-start(bf16[256,512]{1,0:T(8,128)(2,1)S(1)} %get-tuple-element.22), channel_id=1, source_target_pairs={{1,2},{3,4},{5,6},{7,8},{9,10},{11,12},{13,14},{15,16},{17,18},{19... | collective-permute-start | bytes 786440 | tf_op jit(solution)/shard_map/ppermute | solution.py:318
  12.7 0.9 %broadcast_in_dim.2 = bf16[16,34,512]{2,1,0:T(8,128)(2,1)} broadcast(bf16[34,512]{1,0:T(8,128)(2,1)S(1)} %pad_maximum_fusion), dimensions={1,2} | broadcast | bytes 591872 | tf_op jit(solution)/shard_map/broadcast_in_dim | solution.py:320
  13.5 6.7 %all-to-all-start = ((bf16[16,34,512]{2,1,0:T(8,128)(2,1)}), bf16[16,34,512]{2,1,0:T(8,128)(2,1)S(1)}, u32[]{:S(2)}, u32[]{:S(2)}) async-start(bf16[16,34,512]{2,1,0:T(8,128)(2,1)} %broadcast_in_dim.2), calls=%async_computation | async-start | bytes 1310720 | tf_op jit(solution)/shard_map/all_to_all | solution.py:322
  20.3 0.0 collective-permute-done.1.inner_ref
  20.3 0.0 collective-permute-done.2.outer_ref
  20.3 10.4 %near.1 = (f32[4,2,80,1024]{3,2,1,0:T(8,128)}, f32[4,2,1,1024]{3,2,1,0:T(1,128)S(1)}) custom-call(bf16[4,2,1024,128]{3,2,1,0:T(8,128)(2,1)} %query.1.q_hbm, bf16[512,512]{1,0:T(8,128)(2,1)S(1)} %get-tuple-element.19.pair_ref, bf16[256,512]{1,0:T(8,128)(2,1)S(1)} %collective-permute-done.1.inner_ref, bf16[256,512]{1,0:T(8,128)(2,1)S(1)} %collective-permute-done.2.outer_ref), custom_call_target="tpu_custom_call" | custom-call | flops 10000000000 | bytes 1048576 | tf_op jit(solution)/shard_map/near/pallas_call | solution.py:324
  30.7 1.5 %all-to-all-done.mids_ref = bf16[16,34,512]{2,1,0:T(8,128)(2,1)S(1)} async-done(((bf16[16,34,512]{2,1,0:T(8,128)(2,1)}), bf16[16,34,512]{2,1,0:T(8,128)(2,1)S(1)}, u32[]{:S(2)}, u32[]{:S(2)}) %all-to-all-start) | async-done | bytes 557088 | tf_op jit(solution)/shard_map/all_to_all | solution.py:322
  32.3 9.7 %far.1 = bf16[512,1024]{1,0:T(8,128)(2,1)} custom-call(bf16[4,2,1024,128]{3,2,1,0:T(8,128)(2,1)} %query.1.q_hbm, f32[4,2,80,1024]{3,2,1,0:T(8,128)} %get-tuple-element.23.acc_hbm, f32[4,2,1,1024]{3,2,1,0:T(1,128)S(1)} %get-tuple-element.24.top_hbm, bf16[16,34,512]{2,1,0:T(8,128)(2,1)S(1)} %all-to-all-done.mids_ref, bf16[32,512]{1,0:T(8,128)(2,1)S(1)} %reshape.4.coarse_ref, ...), custom_call_target="tpu_custom_call" | custom-call | flops 8000000000 | bytes 1048576 | tf_op jit(solution)/shard_map/far/pallas_call | solution.py:338
  (3 shorter events, 0.0 us)
Async XLA Ops:
  2.5 9.4 %collective-permute-start = (bf16[2,512]{1,0:T(2,128)(2,1)S(1)}, bf16[2,512]{1,0:T(2,128)(2,1)S(1)}, u32[]{:S(2)}, u32[]{:S(2)}) collective-permute-start(bf16[2,512]{1,0:T(2,128)(2,1)S(1)} %get-tuple-element.15.order_ref), channel_id=1, source_target_pairs={{0,16},{1,17},{2,18},{3,19},{4,20},{5,21},{6,22},{7,23},{8,24},{9,... | collective-permute-start | bytes 6152 | tf_op jit(solution)/shard_map/ppermute | solution.py:30
  6.6 13.6 %collective-permute-start.1 = (bf16[256,512]{1,0:T(8,128)(2,1)S(1)}, bf16[256,512]{1,0:T(8,128)(2,1)S(1)}, u32[]{:S(2)}, u32[]{:S(2)}) collective-permute-start(bf16[256,512]{1,0:T(8,128)(2,1)S(1)} %get-tuple-element.20), channel_id=1, source_target_pairs={{0,1},{1,0},{2,3},{3,2},{4,5},{5,4},{6,7},{7,6},{8,9},{9,8},{10,11... | collective-permute-start | bytes 786440 | tf_op jit(solution)/shard_map/ppermute | solution.py:30
  12.0 8.3 %collective-permute-start.2 = (bf16[256,512]{1,0:T(8,128)(2,1)S(1)}, bf16[256,512]{1,0:T(8,128)(2,1)S(1)}, u32[]{:S(2)}, u32[]{:S(2)}) collective-permute-start(bf16[256,512]{1,0:T(8,128)(2,1)S(1)} %get-tuple-element.22), channel_id=1, source_target_pairs={{1,2},{3,4},{5,6},{7,8},{9,10},{11,12},{13,14},{15,16},{17,18},{19... | collective-permute-start | bytes 786440 | tf_op jit(solution)/shard_map/ppermute | solution.py:318
  13.5 18.7 %all-to-all-start = ((bf16[16,34,512]{2,1,0:T(8,128)(2,1)}), bf16[16,34,512]{2,1,0:T(8,128)(2,1)S(1)}, u32[]{:S(2)}, u32[]{:S(2)}) async-start(bf16[16,34,512]{2,1,0:T(8,128)(2,1)} %broadcast_in_dim.2), calls=%async_computation | async-start | bytes 1310720 | tf_op jit(solution)/shard_map/all_to_all | solution.py:322

commit v5 on v4

--- a/solution.py
+++ b/solution.py
@@ -68,35 +68,6 @@
     outer_ref[...] = jnp.where(even, kept[0], kept[-1])
 
 
-def query(tokens_hbm, wq_hbm, order_ref, q_hbm, tokens_ref, wq_ref, q_ref, sems):
-    rows = tokens_ref.shape[0]
-    blocks = rows // BLOCK
-    span = SHARE * HEAD_DIM
-    fetches = [pltpu.make_async_copy(tokens_hbm, tokens_ref, sems.at[KV_HEADS])]
-    for group in range(KV_HEADS):
-        fetches.append(pltpu.make_async_copy(wq_hbm.at[:, pl.ds(group * span, span)], wq_ref.at[group], sems.at[group]))
-    for fetch in fetches:
-        fetch.start()
-    lane = lax.broadcasted_iota(jnp.int32, (BLOCK, HEAD_DIM), 1)
-    fetches[0].wait()
-    keeps = []
-    for group in range(KV_HEADS):
-        fetches[1 + group].wait()
-        part = jnp.dot(tokens_ref[...], wq_ref[group], preferred_element_type=F32)
-        part = part.astype(BF16) * (1.0 / math.sqrt(HEAD_DIM))
-        for block in range(blocks):
-            extra = jnp.where(lane == block, 1.0, 0.0).astype(BF16)
-            for head in range(SHARE):
-                to = slice(head * BLOCK, (head + 1) * BLOCK)
-                piece = part[block * BLOCK : (block + 1) * BLOCK, head * HEAD_DIM : (head + 1) * HEAD_DIM]
-                q_ref[group, block, to, :HEAD_DIM] = piece
-                q_ref[group, block, to, HEAD_DIM:] = extra
-        keeps.append(pltpu.make_async_copy(q_ref.at[group], q_hbm.at[group], sems.at[KV_HEADS + 1 + group]))
-        keeps[-1].start()
-    for keep in keeps:
-        keep.wait()
-
-
 def put_keys(keys_ref, rows, at, biases):
     count = rows.shape[0]
     lane = lax.broadcasted_iota(jnp.int32, (count, HEAD_DIM), 1)
@@ -122,7 +93,7 @@
     values_ref[...] = jnp.where(counting, 1.0, turned).astype(BF16).reshape(KV_HEADS, VROWS, count)
 
 
-def run_units(scores, finish, values, buffers):
+def run_units(before, scores, finish, values, buffers):
     def first(group, block):
         held, top = buffers[block]
         x, floor = scores(group, block)
@@ -136,9 +107,11 @@
         weights = jnp.exp(held[...] - highest).astype(BF16)
         finish(group, block, highest, jnp.dot(values(group, block), weights, preferred_element_type=F32))
 
+    before(0)
     first(0, 0)
 
     def step(group, carry):
+        before(group + 1)
         first(group, 1)
         second(group, 0)
         first(group + 1, 0)
@@ -152,57 +125,79 @@
     second(last, 1)
 
 
-def near(q_hbm, pair_ref, inner_ref, outer_ref, acc_hbm, top_hbm,
-         q_ref, acc_ref, top_ref, sems, keys_ref, values_ref, sa, ta, sb, tb):
-    fetch = pltpu.make_async_copy(q_hbm, q_ref, sems.at[0])
-    fetch.start()
-    rows = pair_ref.shape[0]
+def near(tokens_ref, wq_hbm, pair_ref, inner_ref, outer_ref, q_hbm, acc_hbm, top_hbm,
+         wq_ref, q_ref, acc_ref, top_ref, sems, keys_ref, values_ref, sa, ta, sb, tb):
+    rows = tokens_ref.shape[0]
     blocks = rows // BLOCK
     width = KV_HEADS * HEAD_DIM
+    span = SHARE * HEAD_DIM
     me = lax.axis_index("seq")
     devices = lax.axis_size("seq")
     even = me % 2 == 0
+    fetches = [
+        pltpu.make_async_copy(wq_hbm.at[:, pl.ds(group * span, span)], wq_ref.at[group], sems.at[group])
+        for group in range(KV_HEADS)
+    ]
+    for fetch in fetches:
+        fetch.start()
     prev = jnp.where(even, outer_ref[...], inner_ref[...])
     follow = jnp.where(even, inner_ref[...], outer_ref[...])
     put_keys(keys_ref, prev[:, :width], 0, [jnp.where(me > 0, 0.0, MASKED)] * blocks)
     put_keys(keys_ref, pair_ref[:, :width], BLOCK, ())
     put_keys(keys_ref, follow[:, :width], BLOCK + rows, [jnp.where(me < devices - 1, 0.0, MASKED)] * blocks)
     put_values(values_ref, jnp.concatenate([prev[:, width:], pair_ref[:, width:], follow[:, width:]], axis=0))
-    fetch.wait()
+    lane = lax.broadcasted_iota(jnp.int32, (BLOCK, HEAD_DIM), 1)
+
+    def keep(group, source, target, order):
+        return pltpu.make_async_copy(source.at[group], target.at[group], sems.at[order * KV_HEADS + group])
+
+    def before(group):
+        pltpu.make_async_copy(wq_hbm.at[:, pl.ds(0, span)], wq_ref.at[group], sems.at[group]).wait()
+        part = jnp.dot(tokens_ref[...], wq_ref[group], preferred_element_type=F32)
+        part = part.astype(BF16) * (1.0 / math.sqrt(HEAD_DIM))
+        for block in range(blocks):
+            extra = jnp.where(lane == block, 1.0, 0.0).astype(BF16)
+            for head in range(SHARE):
+                to = slice(head * BLOCK, (head + 1) * BLOCK)
+                piece = part[block * BLOCK : (block + 1) * BLOCK, head * HEAD_DIM : (head + 1) * HEAD_DIM]
+                q_ref[group, block, to, :HEAD_DIM] = piece
+                q_ref[group, block, to, HEAD_DIM:] = extra
+        keep(group, q_ref, q_hbm, 1).start()
 
     def scores(group, block):
         at = slice(block * BLOCK, block * BLOCK + BLOCK + rows)
         return lax.dot_general(keys_ref[group, at], q_ref[group, block], NT, preferred_element_type=F32), None
-
-    def kept(group):
-        return pltpu.make_async_copy(acc_ref.at[group], acc_hbm.at[group], sems.at[1])
 
     def finish(group, block, highest, total):
         acc_ref[group, block] = total
         top_ref[group, block] = highest
         if block == blocks - 1:
-            kept(group).start()
+            keep(group, acc_ref, acc_hbm, 2).start()
 
     def values(group, block):
         return values_ref[group, :, block * BLOCK : block * BLOCK + BLOCK + rows]
 
-    run_units(scores, finish, values, ((sa, ta), (sb, tb)))
-    keep_top = pltpu.make_async_copy(top_ref, top_hbm, sems.at[0])
+    run_units(before, scores, finish, values, ((sa, ta), (sb, tb)))
+    keep_top = pltpu.make_async_copy(top_ref, top_hbm, sems.at[3 * KV_HEADS])
     keep_top.start()
-    pltpu.make_async_copy(acc_ref, acc_hbm, sems.at[1]).wait()
+    for group in range(KV_HEADS):
+        keep(group, q_ref, q_hbm, 1).wait()
+        keep(group, acc_ref, acc_hbm, 2).wait()
     keep_top.wait()
 
 
 def far(q_hbm, acc_hbm, top_hbm, mids_ref, coarse_ref, wout_hbm, out_hbm,
         q_ref, acc_ref, top_ref, wout_ref, out_ref, sems, rows_ref, keys_ref, values_ref, mixed_ref, sa, ta, sb, tb):
-    fetches = [
-        pltpu.make_async_copy(source, target, sems.at[at])
-        for at, (source, target) in enumerate(
-            ((q_hbm, q_ref), (top_hbm, top_ref), (acc_hbm, acc_ref), (wout_hbm, wout_ref))
-        )
-    ]
-    for fetch in fetches:
-        fetch.start()
+    def fetch(group, source, target, order):
+        return pltpu.make_async_copy(source.at[group], target.at[group], sems.at[order * KV_HEADS + group])
+
+    fetch_top = pltpu.make_async_copy(top_hbm, top_ref, sems.at[2 * KV_HEADS])
+    fetch_wout = pltpu.make_async_copy(wout_hbm, wout_ref, sems.at[2 * KV_HEADS + 1])
+    fetch_top.start()
+    for group in range(KV_HEADS):
+        fetch(group, q_hbm, q_ref, 0).start()
+        fetch(group, acc_hbm, acc_ref, 1).start()
+    fetch_wout.start()
     blocks = mixed_ref.shape[0]
     width = KV_HEADS * HEAD_DIM
     me = lax.axis_index("seq")
@@ -230,8 +225,11 @@
         at = swapped if start == 0 else mid_rows + start - per_device
         put_keys(keys_ref, coarse_ref[start : start + per_device, :width], at, bias)
     put_values(values_ref, rows_ref[:, width:])
-    for fetch in fetches[:3]:
-        fetch.wait()
+    fetch_top.wait()
+
+    def before(group):
+        fetch(group, q_hbm, q_ref, 0).wait()
+        fetch(group, acc_hbm, acc_ref, 1).wait()
 
     def scores(group, block):
         return lax.dot_general(keys_ref[group], q_ref[group, block], NT, preferred_element_type=F32), top_ref[group, block]
@@ -244,13 +242,13 @@
             to = pl.multiple_of((group * SHARE + head) * HEAD_DIM, HEAD_DIM)
             mixed_ref[block, pl.ds(to, HEAD_DIM), :] = share[:, head * BLOCK : (head + 1) * BLOCK]
 
-    run_units(scores, finish, lambda group, block: values_ref[group], ((sa, ta), (sb, tb)))
-    fetches[3].wait()
+    run_units(before, scores, finish, lambda group, block: values_ref[group], ((sa, ta), (sb, tb)))
+    fetch_wout.wait()
     stores = []
     for block in range(blocks):
         at = pl.ds(block * BLOCK, BLOCK)
         out_ref[at] = lax.dot_general(mixed_ref[block], wout_ref[...], TN, preferred_element_type=F32).astype(BF16)
-        store = pltpu.make_async_copy(out_ref.at[at], out_hbm.at[at], sems.at[4 + block])
+        store = pltpu.make_async_copy(out_ref.at[at], out_hbm.at[at], sems.at[2 * KV_HEADS + 2 + block])
         store.start()
         stores.append(store)
     for store in stores:
@@ -303,17 +301,6 @@
         level *= 2
     spread = spread[blocks:]
     inner = swap(inner, 1)
-    q = call(
-        query,
-        state[0],
-        [HBM, HBM, VMEM],
-        HBM,
-        [pltpu.VMEM((rows, model), BF16), pltpu.VMEM((KV_HEADS, model, SHARE * HEAD_DIM), BF16), held[0], dma((2 * KV_HEADS + 1,))],
-        2 * 10**9,
-        "query",
-        55000,
-    )(tokens, w_query, coarse)
-    spread = tied(spread, q)
     links = [(i, i + 1) for i in range(1, devices - 1, 2)]
     outer = lax.ppermute(tied(outer, spread), "seq", links + [(b, a) for a, b in links])
     payload = jnp.concatenate([mid, spread], axis=0)
@@ -321,17 +308,18 @@
     members = [list(range(at, at + GROUP)) for at in range(0, devices, GROUP)]
     arrived = lax.all_to_all(payload, "seq", 0, 0, axis_index_groups=members)
 
-    acc, top = call(
+    q, acc, top = call(
         near,
-        state[1:],
-        [HBM, VMEM, VMEM, VMEM],
-        [HBM] * 2,
-        held
-        + [dma((2,)), pltpu.VMEM((KV_HEADS, rows + 2 * BLOCK, WIDE), BF16), pltpu.VMEM((KV_HEADS, VROWS, rows + 2 * BLOCK), BF16)]
+        state,
+        [VMEM, HBM, VMEM, VMEM, VMEM],
+        [HBM] * 3,
+        [pltpu.VMEM((KV_HEADS, model, SHARE * HEAD_DIM), BF16)]
+        + held
+        + [dma((3 * KV_HEADS + 1,)), pltpu.VMEM((KV_HEADS, rows + 2 * BLOCK, WIDE), BF16), pltpu.VMEM((KV_HEADS, VROWS, rows + 2 * BLOCK), BF16)]
         + slots(rows + BLOCK),
         10**10,
         "near",
-    )(q, tied(pair, payload), inner, outer)
+    )(tokens, w_query, tied(pair, payload), inner, outer)
 
     coarse_far = arrived[:, per_device:].reshape(-1, 2 * width)
     keys = (GROUP - 1) * per_device + coarse_far.shape[0]
@@ -344,7 +332,7 @@
         + [
             pltpu.VMEM(w_out.shape, BF16),
             pltpu.VMEM((rows, w_out.shape[1]), BF16),
-            dma((4 + blocks,)),
+            dma((2 * KV_HEADS + 2 + blocks,)),
             pltpu.VMEM((keys, 2 * width), BF16),
             pltpu.VMEM((KV_HEADS, keys, WIDE), BF16),
             pltpu.VMEM((KV_HEADS, VROWS, keys), BF16),

time: 42.8 us -> 38.7 us (0.904); the launches traced: 42 us -> 38.4 us
  Pallas kernels: 27.9 us -> 23 us
  starting transfers between devices: 11.5 us -> 12.4 us
  waiting for transfers between devices: 1.53 us -> 2 us
    pallas_call x2 -> x1, Pallas kernels: 15.7 us -> 11.5 us  [body(): call(near, state, [VMEM, HBM, VMEM, VMEM, VMEM], [HBM] * 3, [pltpu.VMEM((...]
    ppermute x2, waiting for transfers between devices: 0.01 us -> 1.56 us  [swap(): return lax.ppermute(rows, 'seq', [(i, i ^ apart) for i in range(count)])]
    all_to_all x1, waiting for transfers between devices: 1.52 us -> 0.44 us  [body(): arrived = lax.all_to_all(payload, 'seq', 0, 0, axis_index_groups=members)]
    all_to_all x1, starting transfers between devices: 6.72 us -> 7.61 us  [body(): arrived = lax.all_to_all(payload, 'seq', 0, 0, axis_index_groups=members)]
    pallas_call x1, Pallas kernels: 9.7 us -> 8.94 us  [body(): call(far, shape((rows, w_out.shape[1]), BF16), [HBM] * 3 + [VMEM, VMEM, H...]
  transfers between devices with their start and end apart: 4 -> 4, of which waited for: 1 -> 2; matrix products, arithmetic and copies ran while one was open for 2% -> 2% of each run, Pallas kernels for 37% -> 30%
where the time goes in v5:
time: 38.7 us; the launch traced here: 38.4 us
  Pallas kernels  23 us (59%)
  starting transfers between devices  12.4 us (32%)
  waiting for transfers between devices  2 us (5%)
  local copies, waits for them, and re-layouts  0.92 us (2%)
    pallas_call x1, Pallas kernels, body(): call(near, state, [VMEM, HBM, VMEM, VMEM, VMEM], [HBM] * 3, [pltpu.VMEM((...  11.5 us
    pallas_call x1, Pallas kernels, body(): call(far, shape((rows, w_out.shape[1]), BF16), [HBM] * 3 + [VMEM, VMEM, H...  8.94 us
    all_to_all x1, starting transfers between devices, body(): arrived = lax.all_to_all(payload, 'seq', 0, 0, axis_index_groups=members)  7.61 us
    ppermute x2, starting transfers between devices, swap(): return lax.ppermute(rows, 'seq', [(i, i ^ apart) for i in range(count)])  4.1 us
    pallas_call x1, Pallas kernels, body(): call(project_pair, [shape((rows, 2 * width), BF16), shape((per_device, 2...  2.61 us
    ppermute x2, waiting for transfers between devices, swap(): return lax.ppermute(rows, 'seq', [(i, i ^ apart) for i in range(count)])  1.56 us
    broadcast_in_dim x1, local copies, waits for them, and re-layouts, body(): payload = jnp.broadcast_to(payload[None], (GROUP, *payload.shape))  0.88 us
  transfers between devices with their start and end apart: 4, of which 2 were waited for; matrix products, arithmetic and copies ran while one was open for 2% of the time, Pallas kernels for 30%

profile of v5, /device:TPU:0, one launch (start us, length us, event | category | flops | bytes accessed | tf_op | source)
XLA Modules:
  0.0 38.4 jit_solution(1212714655048885803)
XLA Ops:
  0.0 0.0 copy-start
  0.0 2.6 %pair.1 = (bf16[512,512]{1,0:T(8,128)(2,1)S(1)}, bf16[32,512]{1,0:T(8,128)(2,1)S(1)}, bf16[2,512]{1,0:T(2,128)(2,1)S(1)}, bf16[256,512]{1,0:T(8,128)(2,1)S(1)}, bf16[256,512]{1,0:T(8,128)(2,1)S(1)}) custom-call(bf16[512,1024]{1,0:T(8,128)(2,1)} %tokens_ref.1, bf16[1024,256]{1,0:T(8,128)(2,1)} %wk_hbm.1, bf16[1024,256]{1,0:T(8,128)(2,1)} %wv_hbm.1), custom_call_target="tpu_custom_call" | custom-call | flops 2000000000 | bytes 1048576 | tf_op jit(solution)/shard_map/pair/pallas_call | solution.py:284
  2.6 4.1 %collective-permute-start = (bf16[2,512]{1,0:T(2,128)(2,1)S(1)}, bf16[2,512]{1,0:T(2,128)(2,1)S(1)}, u32[]{:S(2)}, u32[]{:S(2)}) collective-permute-start(bf16[2,512]{1,0:T(2,128)(2,1)S(1)} %get-tuple-element.17), channel_id=1, source_target_pairs={{0,16},{1,17},{2,18},{3,19},{4,20},{5,21},{6,22},{7,23},{8,24},{9,... | collective-permute-start | bytes 6152 | tf_op jit(solution)/shard_map/ppermute | solution.py:30
  6.7 0.0 collective-permute-start.1
  6.7 1.6 %collective-permute-done = bf16[2,512]{1,0:T(2,128)(2,1)S(1)} collective-permute-done((bf16[2,512]{1,0:T(2,128)(2,1)S(1)}, bf16[2,512]{1,0:T(2,128)(2,1)S(1)}, u32[]{:S(2)}, u32[]{:S(2)}) %collective-permute-start) | collective-permute-done | bytes 2080 | tf_op jit(solution)/shard_map/ppermute | solution.py:30
  8.3 0.7 %collective-permute-start.2 = (bf16[256,512]{1,0:T(8,128)(2,1)S(1)}, bf16[256,512]{1,0:T(8,128)(2,1)S(1)}, u32[]{:S(2)}, u32[]{:S(2)}) collective-permute-start(bf16[256,512]{1,0:T(8,128)(2,1)S(1)} %get-tuple-element.21), channel_id=1, source_target_pairs={{1,2},{3,4},{5,6},{7,8},{9,10},{11,12},{13,14},{15,16},{17,18},{19... | collective-permute-start | bytes 786440 | tf_op jit(solution)/shard_map/ppermute | solution.py:305
  9.0 0.9 %broadcast_in_dim.2 = bf16[16,34,512]{2,1,0:T(8,128)(2,1)} broadcast(bf16[34,512]{1,0:T(8,128)(2,1)S(1)} %pad_maximum_fusion), dimensions={1,2} | broadcast | bytes 591872 | tf_op jit(solution)/shard_map/broadcast_in_dim | solution.py:307
  9.9 7.6 %all-to-all-start = ((bf16[16,34,512]{2,1,0:T(8,128)(2,1)}), bf16[16,34,512]{2,1,0:T(8,128)(2,1)S(1)}, u32[]{:S(2)}, u32[]{:S(2)}) async-start(bf16[16,34,512]{2,1,0:T(8,128)(2,1)} %broadcast_in_dim.2), calls=%async_computation | async-start | bytes 1310720 | tf_op jit(solution)/shard_map/all_to_all | solution.py:309
  17.5 0.0 collective-permute-done.1.inner_ref
  17.5 0.0 collective-permute-done.2.outer_ref
  17.5 0.0 copy-done
  17.5 11.5 %near.1 = (bf16[4,2,1024,128]{3,2,1,0:T(8,128)(2,1)}, f32[4,2,80,1024]{3,2,1,0:T(8,128)}, f32[4,2,1,1024]{3,2,1,0:T(1,128)S(1)}) custom-call(bf16[512,1024]{1,0:T(8,128)(2,1)S(1)} %copy-done, bf16[1024,1024]{1,0:T(8,128)(2,1)} %wq_hbm.1, bf16[512,512]{1,0:T(8,128)(2,1)S(1)} %get-tuple-element.18.pair_ref, ...), custom_call_target="tpu_custom_call" | custom-call | flops 10000000000 | bytes 1048576 | tf_op jit(solution)/shard_map/near/pallas_call | solution.py:311
  29.0 0.4 %all-to-all-done.mids_ref = bf16[16,34,512]{2,1,0:T(8,128)(2,1)S(1)} async-done(((bf16[16,34,512]{2,1,0:T(8,128)(2,1)}), bf16[16,34,512]{2,1,0:T(8,128)(2,1)S(1)}, u32[]{:S(2)}, u32[]{:S(2)}) %all-to-all-start) | async-done | bytes 557088 | tf_op jit(solution)/shard_map/all_to_all | solution.py:309
  29.5 8.9 %far.1 = bf16[512,1024]{1,0:T(8,128)(2,1)} custom-call(bf16[4,2,1024,128]{3,2,1,0:T(8,128)(2,1)} %get-tuple-element.22.q_hbm, f32[4,2,80,1024]{3,2,1,0:T(8,128)} %get-tuple-element.23.acc_hbm, f32[4,2,1,1024]{3,2,1,0:T(1,128)S(1)} %get-tuple-element.24.top_hbm, bf16[16,34,512]{2,1,0:T(8,128)(2,1)S(1)} %all-to-all-done.mids_ref, ...), custom_call_target="tpu_custom_call" | custom-call | flops 8000000000 | bytes 1048576 | tf_op jit(solution)/shard_map/far/pallas_call | solution.py:326
  (3 shorter events, 0.0 us)
Async XLA Ops:
  0.0 17.5 %copy-start = (bf16[512,1024]{1,0:T(8,128)(2,1)S(1)}, bf16[512,1024]{1,0:T(8,128)(2,1)}, u32[]{:S(2)}) copy-start(bf16[512,1024]{1,0:T(8,128)(2,1)} %tokens_ref.1) | copy-start | bytes 3145732
  2.6 5.7 %collective-permute-start = (bf16[2,512]{1,0:T(2,128)(2,1)S(1)}, bf16[2,512]{1,0:T(2,128)(2,1)S(1)}, u32[]{:S(2)}, u32[]{:S(2)}) collective-permute-start(bf16[2,512]{1,0:T(2,128)(2,1)S(1)} %get-tuple-element.17), channel_id=1, source_target_pairs={{0,16},{1,17},{2,18},{3,19},{4,20},{5,21},{6,22},{7,23},{8,24},{9,... | collective-permute-start | bytes 6152 | tf_op jit(solution)/shard_map/ppermute | solution.py:30
  6.7 10.8 %collective-permute-start.1 = (bf16[256,512]{1,0:T(8,128)(2,1)S(1)}, bf16[256,512]{1,0:T(8,128)(2,1)S(1)}, u32[]{:S(2)}, u32[]{:S(2)}) collective-permute-start(bf16[256,512]{1,0:T(8,128)(2,1)S(1)} %get-tuple-element.19), channel_id=1, source_target_pairs={{0,1},{1,0},{2,3},{3,2},{4,5},{5,4},{6,7},{7,6},{8,9},{9,8},{10,11... | collective-permute-start | bytes 786440 | tf_op jit(solution)/shard_map/ppermute | solution.py:30
  8.3 9.2 %collective-permute-start.2 = (bf16[256,512]{1,0:T(8,128)(2,1)S(1)}, bf16[256,512]{1,0:T(8,128)(2,1)S(1)}, u32[]{:S(2)}, u32[]{:S(2)}) collective-permute-start(bf16[256,512]{1,0:T(8,128)(2,1)S(1)} %get-tuple-element.21), channel_id=1, source_target_pairs={{1,2},{3,4},{5,6},{7,8},{9,10},{11,12},{13,14},{15,16},{17,18},{19... | collective-permute-start | bytes 786440 | tf_op jit(solution)/shard_map/ppermute | solution.py:305
  9.9 19.6 %all-to-all-start = ((bf16[16,34,512]{2,1,0:T(8,128)(2,1)}), bf16[16,34,512]{2,1,0:T(8,128)(2,1)S(1)}, u32[]{:S(2)}, u32[]{:S(2)}) async-start(bf16[16,34,512]{2,1,0:T(8,128)(2,1)} %broadcast_in_dim.2), calls=%async_computation | async-start | bytes 1310720 | tf_op jit(solution)/shard_map/all_to_all | solution.py:309

commit v6 on v5

--- a/solution.py
+++ b/solution.py
@@ -93,7 +93,7 @@
     values_ref[...] = jnp.where(counting, 1.0, turned).astype(BF16).reshape(KV_HEADS, VROWS, count)
 
 
-def run_units(before, scores, finish, values, buffers):
+def run_units(before, scores, finish, values, buffers, closing=None, between=None):
     def first(group, block):
         held, top = buffers[block]
         x, floor = scores(group, block)
@@ -119,9 +119,13 @@
         return carry
 
     lax.fori_loop(0, KV_HEADS - 1, step, 0)
+    if closing is not None:
+        closing()
     last = KV_HEADS - 1
     first(last, 1)
     second(last, 0)
+    if between is not None:
+        between()
     second(last, 1)
 
 
@@ -151,8 +155,24 @@
     def keep(group, source, target, order):
         return pltpu.make_async_copy(source.at[group], target.at[group], sems.at[order * KV_HEADS + group])
 
+    def leave(group, block):
+        return pltpu.make_async_copy(acc_ref.at[group, block], acc_hbm.at[group, block], sems.at[2 * KV_HEADS + 1 + group * blocks + block])
+
+    def send(group):
+        for block in range(blocks):
+            leave(group, block).start()
+
     def before(group):
         pltpu.make_async_copy(wq_hbm.at[:, pl.ds(0, span)], wq_ref.at[group], sems.at[group]).wait()
+
+        @pl.when(group >= 1)
+        def _():
+            keep(group - 1, q_ref, q_hbm, 1).start()
+
+        @pl.when(group >= 2)
+        def _():
+            send(group - 2)
+
         part = jnp.dot(tokens_ref[...], wq_ref[group], preferred_element_type=F32)
         part = part.astype(BF16) * (1.0 / math.sqrt(HEAD_DIM))
         for block in range(blocks):
@@ -162,7 +182,10 @@
                 piece = part[block * BLOCK : (block + 1) * BLOCK, head * HEAD_DIM : (head + 1) * HEAD_DIM]
                 q_ref[group, block, to, :HEAD_DIM] = piece
                 q_ref[group, block, to, HEAD_DIM:] = extra
-        keep(group, q_ref, q_hbm, 1).start()
+
+    def closing():
+        keep(KV_HEADS - 1, q_ref, q_hbm, 1).start()
+        send(KV_HEADS - 2)
 
     def scores(group, block):
         at = slice(block * BLOCK, block * BLOCK + BLOCK + rows)
@@ -171,18 +194,18 @@
     def finish(group, block, highest, total):
         acc_ref[group, block] = total
         top_ref[group, block] = highest
-        if block == blocks - 1:
-            keep(group, acc_ref, acc_hbm, 2).start()
 
     def values(group, block):
         return values_ref[group, :, block * BLOCK : block * BLOCK + BLOCK + rows]
 
-    run_units(before, scores, finish, values, ((sa, ta), (sb, tb)))
-    keep_top = pltpu.make_async_copy(top_ref, top_hbm, sems.at[3 * KV_HEADS])
+    run_units(before, scores, finish, values, ((sa, ta), (sb, tb)), closing)
+    send(KV_HEADS - 1)
+    keep_top = pltpu.make_async_copy(top_ref, top_hbm, sems.at[2 * KV_HEADS])
     keep_top.start()
     for group in range(KV_HEADS):
         keep(group, q_ref, q_hbm, 1).wait()
-        keep(group, acc_ref, acc_hbm, 2).wait()
+        for block in range(blocks):
+            leave(group, block).wait()
     keep_top.wait()
 
 
@@ -242,17 +265,21 @@
             to = pl.multiple_of((group * SHARE + head) * HEAD_DIM, HEAD_DIM)
             mixed_ref[block, pl.ds(to, HEAD_DIM), :] = share[:, head * BLOCK : (head + 1) * BLOCK]
 
-    run_units(before, scores, finish, lambda group, block: values_ref[group], ((sa, ta), (sb, tb)))
-    fetch_wout.wait()
-    stores = []
-    for block in range(blocks):
+    def store(block):
+        at = pl.ds(block * BLOCK, BLOCK)
+        return pltpu.make_async_copy(out_ref.at[at], out_hbm.at[at], sems.at[2 * KV_HEADS + 2 + block])
+
+    def project(block):
         at = pl.ds(block * BLOCK, BLOCK)
         out_ref[at] = lax.dot_general(mixed_ref[block], wout_ref[...], TN, preferred_element_type=F32).astype(BF16)
-        store = pltpu.make_async_copy(out_ref.at[at], out_hbm.at[at], sems.at[2 * KV_HEADS + 2 + block])
-        store.start()
-        stores.append(store)
-    for store in stores:
-        store.wait()
+
+    run_units(before, scores, finish, lambda group, block: values_ref[group], ((sa, ta), (sb, tb)), fetch_wout.wait, lambda: project(0))
+    store(0).start()
+    for block in range(1, blocks):
+        project(block)
+        store(block).start()
+    for block in range(blocks):
+        store(block).wait()
 
 
 def body(tokens, w_query, w_key, w_value, w_out):
@@ -315,7 +342,7 @@
         [HBM] * 3,
         [pltpu.VMEM((KV_HEADS, model, SHARE * HEAD_DIM), BF16)]
         + held
-        + [dma((3 * KV_HEADS + 1,)), pltpu.VMEM((KV_HEADS, rows + 2 * BLOCK, WIDE), BF16), pltpu.VMEM((KV_HEADS, VROWS, rows + 2 * BLOCK), BF16)]
+        + [dma((2 * KV_HEADS + 1 + KV_HEADS * blocks,)), pltpu.VMEM((KV_HEADS, rows + 2 * BLOCK, WIDE), BF16), pltpu.VMEM((KV_HEADS, VROWS, rows + 2 * BLOCK), BF16)]
         + slots(rows + BLOCK),
         10**10,
         "near",

time: 38.7 us -> 38.4 us (level)
  no operation moved by 1% of the time
where the time goes in v6:
time: 38.4 us; the launch traced here: 38.1 us
  Pallas kernels  22.7 us (59%)
  starting transfers between devices  12.4 us (32%)
  waiting for transfers between devices  1.98 us (5%)
  local copies, waits for them, and re-layouts  0.92 us (2%)
    pallas_call x1, Pallas kernels, body(): call(near, state, [VMEM, HBM, VMEM, VMEM, VMEM], [HBM] * 3, [pltpu.VMEM((...  11.5 us
    pallas_call x1, Pallas kernels, body(): call(far, shape((rows, w_out.shape[1]), BF16), [HBM] * 3 + [VMEM, VMEM, H...  8.63 us
    all_to_all x1, starting transfers between devices, body(): arrived = lax.all_to_all(payload, 'seq', 0, 0, axis_index_groups=members)  7.61 us
    ppermute x2, starting transfers between devices, swap(): return lax.ppermute(rows, 'seq', [(i, i ^ apart) for i in range(count)])  4.1 us
    pallas_call x1, Pallas kernels, body(): call(project_pair, [shape((rows, 2 * width), BF16), shape((per_device, 2...  2.61 us
    ppermute x2, waiting for transfers between devices, swap(): return lax.ppermute(rows, 'seq', [(i, i ^ apart) for i in range(count)])  1.56 us
    broadcast_in_dim x1, local copies, waits for them, and re-layouts, body(): payload = jnp.broadcast_to(payload[None], (GROUP, *payload.shape))  0.88 us
  transfers between devices with their start and end apart: 4, of which 2 were waited for; matrix products, arithmetic and copies ran while one was open for 2% of the time, Pallas kernels for 30%

profile of v6, /device:TPU:0, one launch (start us, length us, event | category | flops | bytes accessed | tf_op | source)
XLA Modules:
  0.0 38.1 jit_solution(453553911448144309)
XLA Ops:
  0.0 0.0 copy-start
  0.0 2.6 %pair.1 = (bf16[512,512]{1,0:T(8,128)(2,1)S(1)}, bf16[32,512]{1,0:T(8,128)(2,1)S(1)}, bf16[2,512]{1,0:T(2,128)(2,1)S(1)}, bf16[256,512]{1,0:T(8,128)(2,1)S(1)}, bf16[256,512]{1,0:T(8,128)(2,1)S(1)}) custom-call(bf16[512,1024]{1,0:T(8,128)(2,1)} %tokens_ref.1, bf16[1024,256]{1,0:T(8,128)(2,1)} %wk_hbm.1, bf16[1024,256]{1,0:T(8,128)(2,1)} %wv_hbm.1), custom_call_target="tpu_custom_call" | custom-call | flops 2000000000 | bytes 1048576 | tf_op jit(solution)/shard_map/pair/pallas_call | solution.py:311
  2.6 4.1 %collective-permute-start = (bf16[2,512]{1,0:T(2,128)(2,1)S(1)}, bf16[2,512]{1,0:T(2,128)(2,1)S(1)}, u32[]{:S(2)}, u32[]{:S(2)}) collective-permute-start(bf16[2,512]{1,0:T(2,128)(2,1)S(1)} %get-tuple-element.17), channel_id=1, source_target_pairs={{0,16},{1,17},{2,18},{3,19},{4,20},{5,21},{6,22},{7,23},{8,24},{9,... | collective-permute-start | bytes 6152 | tf_op jit(solution)/shard_map/ppermute | solution.py:30
  6.7 0.0 collective-permute-start.1
  6.7 1.6 %collective-permute-done = bf16[2,512]{1,0:T(2,128)(2,1)S(1)} collective-permute-done((bf16[2,512]{1,0:T(2,128)(2,1)S(1)}, bf16[2,512]{1,0:T(2,128)(2,1)S(1)}, u32[]{:S(2)}, u32[]{:S(2)}) %collective-permute-start) | collective-permute-done | bytes 2080 | tf_op jit(solution)/shard_map/ppermute | solution.py:30
  8.3 0.7 %collective-permute-start.2 = (bf16[256,512]{1,0:T(8,128)(2,1)S(1)}, bf16[256,512]{1,0:T(8,128)(2,1)S(1)}, u32[]{:S(2)}, u32[]{:S(2)}) collective-permute-start(bf16[256,512]{1,0:T(8,128)(2,1)S(1)} %get-tuple-element.21), channel_id=1, source_target_pairs={{1,2},{3,4},{5,6},{7,8},{9,10},{11,12},{13,14},{15,16},{17,18},{19... | collective-permute-start | bytes 786440 | tf_op jit(solution)/shard_map/ppermute | solution.py:332
  9.0 0.9 %broadcast_in_dim.2 = bf16[16,34,512]{2,1,0:T(8,128)(2,1)} broadcast(bf16[34,512]{1,0:T(8,128)(2,1)S(1)} %pad_maximum_fusion), dimensions={1,2} | broadcast | bytes 591872 | tf_op jit(solution)/shard_map/broadcast_in_dim | solution.py:334
  9.9 7.6 %all-to-all-start = ((bf16[16,34,512]{2,1,0:T(8,128)(2,1)}), bf16[16,34,512]{2,1,0:T(8,128)(2,1)S(1)}, u32[]{:S(2)}, u32[]{:S(2)}) async-start(bf16[16,34,512]{2,1,0:T(8,128)(2,1)} %broadcast_in_dim.2), calls=%async_computation | async-start | bytes 1310720 | tf_op jit(solution)/shard_map/all_to_all | solution.py:336
  17.5 0.0 collective-permute-done.1.inner_ref
  17.5 0.0 collective-permute-done.2.outer_ref
  17.5 0.0 copy-done
  17.5 11.5 %near.1 = (bf16[4,2,1024,128]{3,2,1,0:T(8,128)(2,1)}, f32[4,2,80,1024]{3,2,1,0:T(8,128)}, f32[4,2,1,1024]{3,2,1,0:T(1,128)S(1)}) custom-call(bf16[512,1024]{1,0:T(8,128)(2,1)S(1)} %copy-done, bf16[1024,1024]{1,0:T(8,128)(2,1)} %wq_hbm.1, bf16[512,512]{1,0:T(8,128)(2,1)S(1)} %get-tuple-element.18.pair_ref, ...), custom_call_target="tpu_custom_call" | custom-call | flops 10000000000 | bytes 1048576 | tf_op jit(solution)/shard_map/near/pallas_call | solution.py:338
  29.0 0.4 %all-to-all-done.mids_ref = bf16[16,34,512]{2,1,0:T(8,128)(2,1)S(1)} async-done(((bf16[16,34,512]{2,1,0:T(8,128)(2,1)}), bf16[16,34,512]{2,1,0:T(8,128)(2,1)S(1)}, u32[]{:S(2)}, u32[]{:S(2)}) %all-to-all-start) | async-done | bytes 557088 | tf_op jit(solution)/shard_map/all_to_all | solution.py:336
  29.5 8.6 %far.1 = bf16[512,1024]{1,0:T(8,128)(2,1)} custom-call(bf16[4,2,1024,128]{3,2,1,0:T(8,128)(2,1)} %get-tuple-element.22.q_hbm, f32[4,2,80,1024]{3,2,1,0:T(8,128)} %get-tuple-element.23.acc_hbm, f32[4,2,1,1024]{3,2,1,0:T(1,128)S(1)} %get-tuple-element.24.top_hbm, bf16[16,34,512]{2,1,0:T(8,128)(2,1)S(1)} %all-to-all-done.mids_ref, ...), custom_call_target="tpu_custom_call" | custom-call | flops 8000000000 | bytes 1048576 | tf_op jit(solution)/shard_map/far/pallas_call | solution.py:353
  (3 shorter events, 0.0 us)
Async XLA Ops:
  0.0 17.5 %copy-start = (bf16[512,1024]{1,0:T(8,128)(2,1)S(1)}, bf16[512,1024]{1,0:T(8,128)(2,1)}, u32[]{:S(2)}) copy-start(bf16[512,1024]{1,0:T(8,128)(2,1)} %tokens_ref.1) | copy-start | bytes 3145732
  2.6 5.7 %collective-permute-start = (bf16[2,512]{1,0:T(2,128)(2,1)S(1)}, bf16[2,512]{1,0:T(2,128)(2,1)S(1)}, u32[]{:S(2)}, u32[]{:S(2)}) collective-permute-start(bf16[2,512]{1,0:T(2,128)(2,1)S(1)} %get-tuple-element.17), channel_id=1, source_target_pairs={{0,16},{1,17},{2,18},{3,19},{4,20},{5,21},{6,22},{7,23},{8,24},{9,... | collective-permute-start | bytes 6152 | tf_op jit(solution)/shard_map/ppermute | solution.py:30
  6.7 10.8 %collective-permute-start.1 = (bf16[256,512]{1,0:T(8,128)(2,1)S(1)}, bf16[256,512]{1,0:T(8,128)(2,1)S(1)}, u32[]{:S(2)}, u32[]{:S(2)}) collective-permute-start(bf16[256,512]{1,0:T(8,128)(2,1)S(1)} %get-tuple-element.19), channel_id=1, source_target_pairs={{0,1},{1,0},{2,3},{3,2},{4,5},{5,4},{6,7},{7,6},{8,9},{9,8},{10,11... | collective-permute-start | bytes 786440 | tf_op jit(solution)/shard_map/ppermute | solution.py:30
  8.3 9.2 %collective-permute-start.2 = (bf16[256,512]{1,0:T(8,128)(2,1)S(1)}, bf16[256,512]{1,0:T(8,128)(2,1)S(1)}, u32[]{:S(2)}, u32[]{:S(2)}) collective-permute-start(bf16[256,512]{1,0:T(8,128)(2,1)S(1)} %get-tuple-element.21), channel_id=1, source_target_pairs={{1,2},{3,4},{5,6},{7,8},{9,10},{11,12},{13,14},{15,16},{17,18},{19... | collective-permute-start | bytes 786440 | tf_op jit(solution)/shard_map/ppermute | solution.py:332
  9.9 19.6 %all-to-all-start = ((bf16[16,34,512]{2,1,0:T(8,128)(2,1)}), bf16[16,34,512]{2,1,0:T(8,128)(2,1)S(1)}, u32[]{:S(2)}, u32[]{:S(2)}) async-start(bf16[16,34,512]{2,1,0:T(8,128)(2,1)} %broadcast_in_dim.2), calls=%async_computation | async-start | bytes 1310720 | tf_op jit(solution)/shard_map/all_to_all | solution.py:336

commit v7 on v6

--- a/solution.py
+++ b/solution.py
@@ -328,10 +328,12 @@
         level *= 2
     spread = spread[blocks:]
     inner = swap(inner, 1)
+    payload = jnp.pad(mid, ((0, spread.shape[0]), (0, 0)))
+    payload = lax.optimization_barrier(jnp.broadcast_to(payload[None], (GROUP, *payload.shape)))
     links = [(i, i + 1) for i in range(1, devices - 1, 2)]
-    outer = lax.ppermute(tied(outer, spread), "seq", links + [(b, a) for a, b in links])
-    payload = jnp.concatenate([mid, spread], axis=0)
-    payload = jnp.broadcast_to(payload[None], (GROUP, *payload.shape))
+    outer = lax.ppermute(tied(outer, payload), "seq", links + [(b, a) for a, b in links])
+    late = jnp.broadcast_to(spread[None], (GROUP, *spread.shape))
+    payload = lax.dynamic_update_slice(payload, late, (0, per_device, 0))
     members = [list(range(at, at + GROUP)) for at in range(0, devices, GROUP)]
     arrived = lax.all_to_all(payload, "seq", 0, 0, axis_index_groups=members)
 

time: 38.4 us -> 37.3 us (0.971)
  the two profiles are of different devices: /device:TPU:0 before, /device:TPU:11 now
where the time goes in v7:
time: 37.3 us; the launch traced here: 37.1 us
  Pallas kernels  22.6 us (61%)
  starting transfers between devices  10.8 us (29%)
  waiting for transfers between devices  2.01 us (5%)
  local copies, waits for them, and re-layouts  1.57 us (4%)
    pallas_call x1, Pallas kernels, body(): call(near, state, [VMEM, HBM, VMEM, VMEM, VMEM], [HBM] * 3, [pltpu.VMEM((...  11.5 us
    pallas_call x1, Pallas kernels, body(): call(far, shape((rows, w_out.shape[1]), BF16), [HBM] * 3 + [VMEM, VMEM, H...  8.63 us
    all_to_all x1, starting transfers between devices, body(): arrived = lax.all_to_all(payload, 'seq', 0, 0, axis_index_groups=members)  4.37 us
    ppermute x1, starting transfers between devices, body(): lax.ppermute(tied(outer, payload), 'seq', links + [(b, a) for a, b in lin...  3.95 us
    pallas_call x1, Pallas kernels, body(): call(project_pair, [shape((rows, 2 * width), BF16), shape((per_device, 2...  2.52 us
    ppermute x2, starting transfers between devices, swap(): return lax.ppermute(rows, 'seq', [(i, i ^ apart) for i in range(count)])  2.45 us
    ppermute x1, waiting for transfers between devices, body(): lax.ppermute(tied(outer, payload), 'seq', links + [(b, a) for a, b in lin...  2 us
    broadcast_in_dim x1, local copies, waits for them, and re-layouts, body(): jnp.broadcast_to(payload[None], (GROUP, *payload.shape))  0.88 us
  transfers between devices with their start and end apart: 4, of which 1 were waited for; matrix products, arithmetic and copies ran while one was open for 4% of the time, Pallas kernels for 31%

profile of v7, /device:TPU:11, one launch (start us, length us, event | category | flops | bytes accessed | tf_op | source)
XLA Modules:
  0.0 37.1 jit_solution(11480560445003260307)
XLA Ops:
  0.0 2.5 %pair.1 = (bf16[512,512]{1,0:T(8,128)(2,1)S(1)}, bf16[32,512]{1,0:T(8,128)(2,1)S(1)}, bf16[2,512]{1,0:T(2,128)(2,1)S(1)}, bf16[256,512]{1,0:T(8,128)(2,1)S(1)}, bf16[256,512]{1,0:T(8,128)(2,1)S(1)}) custom-call(bf16[512,1024]{1,0:T(8,128)(2,1)} %tokens_ref.1, bf16[1024,256]{1,0:T(8,128)(2,1)} %wk_hbm.1, bf16[1024,256]{1,0:T(8,128)(2,1)} %wv_hbm.1), custom_call_target="tpu_custom_call" | custom-call | flops 2000000000 | bytes 1048576 | tf_op jit(solution)/shard_map/pair/pallas_call | solution.py:311
  2.5 0.0 copy-start
  2.5 2.4 %collective-permute-start = (bf16[2,512]{1,0:T(2,128)(2,1)S(1)}, bf16[2,512]{1,0:T(2,128)(2,1)S(1)}, u32[]{:S(2)}, u32[]{:S(2)}) collective-permute-start(bf16[2,512]{1,0:T(2,128)(2,1)S(1)} %get-tuple-element.17), channel_id=1, source_target_pairs={{0,16},{1,17},{2,18},{3,19},{4,20},{5,21},{6,22},{7,23},{8,24},{9,... | collective-permute-start | bytes 6152 | tf_op jit(solution)/shard_map/ppermute | solution.py:30
  4.9 0.9 %broadcast_in_dim.4 = bf16[16,34,512]{2,1,0:T(8,128)(2,1)} broadcast(bf16[34,512]{1,0:T(8,128)(2,1)S(1)} %pad.4), dimensions={1,2} | broadcast | bytes 591872 | tf_op jit(solution)/shard_map/broadcast_in_dim | solution.py:332
  5.8 3.9 %collective-permute-start.2 = (bf16[256,512]{1,0:T(8,128)(2,1)S(1)}, bf16[256,512]{1,0:T(8,128)(2,1)S(1)}, u32[]{:S(2)}, u32[]{:S(2)}) collective-permute-start(bf16[256,512]{1,0:T(8,128)(2,1)S(1)} %get-tuple-element.21), channel_id=1, source_target_pairs={{1,2},{3,4},{5,6},{7,8},{9,10},{11,12},{13,14},{15,16},{17,18},{19... | collective-permute-start | bytes 786440 | tf_op jit(solution)/shard_map/ppermute | solution.py:334
  9.8 0.1 collective-permute-start.1
  9.8 0.0 collective-permute-done
  9.8 0.6 %broadcast_dynamic-update-slice_fusion = bf16[16,34,512]{2,1,0:T(8,128)(2,1)} fusion(bf16[16,34,512]{2,1,0:T(8,128)(2,1)} %broadcast_in_dim.4, bf16[2,512]{1,0:T(2,128)(2,1)S(1)} %collective-permute-done), kind=kLoop, calls=%fused_computation | loop fusion | bytes 34816 | tf_op jit(solution)/shard_map/dynamic_update_slice | solution.py:336
  10.5 4.4 %all-to-all-start = ((bf16[16,34,512]{2,1,0:T(8,128)(2,1)}), bf16[16,34,512]{2,1,0:T(8,128)(2,1)S(1)}, u32[]{:S(2)}, u32[]{:S(2)}) async-start(bf16[16,34,512]{2,1,0:T(8,128)(2,1)} %broadcast_dynamic-update-slice_fusion), calls=%async_computation | async-start | bytes 1310720 | tf_op jit(solution)/shard_map/all_to_all | solution.py:338
  14.9 2.0 %collective-permute-done.2.outer_ref = bf16[256,512]{1,0:T(8,128)(2,1)S(1)} collective-permute-done((bf16[256,512]{1,0:T(8,128)(2,1)S(1)}, bf16[256,512]{1,0:T(8,128)(2,1)S(1)}, u32[]{:S(2)}, u32[]{:S(2)}) %collective-permute-start.2) | collective-permute-done | bytes 262176 | tf_op jit(solution)/shard_map/ppermute | solution.py:334
  16.9 0.0 collective-permute-done.1.inner_ref
  16.9 0.0 copy-done
  16.9 11.5 %near.1 = (bf16[4,2,1024,128]{3,2,1,0:T(8,128)(2,1)}, f32[4,2,80,1024]{3,2,1,0:T(8,128)}, f32[4,2,1,1024]{3,2,1,0:T(1,128)S(1)}) custom-call(bf16[512,1024]{1,0:T(8,128)(2,1)S(1)} %copy-done, bf16[1024,1024]{1,0:T(8,128)(2,1)} %wq_hbm.1, bf16[512,512]{1,0:T(8,128)(2,1)S(1)} %get-tuple-element.18.pair_ref, ...), custom_call_target="tpu_custom_call" | custom-call | flops 10000000000 | bytes 1048576 | tf_op jit(solution)/shard_map/near/pallas_call | solution.py:340
  28.4 0.0 all-to-all-done.mids_ref
  28.4 8.6 %far.1 = bf16[512,1024]{1,0:T(8,128)(2,1)} custom-call(bf16[4,2,1024,128]{3,2,1,0:T(8,128)(2,1)} %get-tuple-element.22.q_hbm, f32[4,2,80,1024]{3,2,1,0:T(8,128)} %get-tuple-element.23.acc_hbm, f32[4,2,1,1024]{3,2,1,0:T(1,128)S(1)} %get-tuple-element.24.top_hbm, bf16[16,34,512]{2,1,0:T(8,128)(2,1)S(1)} %all-to-all-done.mids_ref, ...), custom_call_target="tpu_custom_call" | custom-call | flops 8000000000 | bytes 1048576 | tf_op jit(solution)/shard_map/far/pallas_call | solution.py:355
  (3 shorter events, 0.0 us)
Async XLA Ops:
  2.5 14.3 %copy-start = (bf16[512,1024]{1,0:T(8,128)(2,1)S(1)}, bf16[512,1024]{1,0:T(8,128)(2,1)}, u32[]{:S(2)}) copy-start(bf16[512,1024]{1,0:T(8,128)(2,1)} %tokens_ref.1) | copy-start | bytes 3145732
  2.5 7.3 %collective-permute-start = (bf16[2,512]{1,0:T(2,128)(2,1)S(1)}, bf16[2,512]{1,0:T(2,128)(2,1)S(1)}, u32[]{:S(2)}, u32[]{:S(2)}) collective-permute-start(bf16[2,512]{1,0:T(2,128)(2,1)S(1)} %get-tuple-element.17), channel_id=1, source_target_pairs={{0,16},{1,17},{2,18},{3,19},{4,20},{5,21},{6,22},{7,23},{8,24},{9,... | collective-permute-start | bytes 6152 | tf_op jit(solution)/shard_map/ppermute | solution.py:30
  5.8 11.1 %collective-permute-start.2 = (bf16[256,512]{1,0:T(8,128)(2,1)S(1)}, bf16[256,512]{1,0:T(8,128)(2,1)S(1)}, u32[]{:S(2)}, u32[]{:S(2)}) collective-permute-start(bf16[256,512]{1,0:T(8,128)(2,1)S(1)} %get-tuple-element.21), channel_id=1, source_target_pairs={{1,2},{3,4},{5,6},{7,8},{9,10},{11,12},{13,14},{15,16},{17,18},{19... | collective-permute-start | bytes 786440 | tf_op jit(solution)/shard_map/ppermute | solution.py:334
  9.8 7.1 %collective-permute-start.1 = (bf16[256,512]{1,0:T(8,128)(2,1)S(1)}, bf16[256,512]{1,0:T(8,128)(2,1)S(1)}, u32[]{:S(2)}, u32[]{:S(2)}) collective-permute-start(bf16[256,512]{1,0:T(8,128)(2,1)S(1)} %get-tuple-element.19), channel_id=1, source_target_pairs={{0,1},{1,0},{2,3},{3,2},{4,5},{5,4},{6,7},{7,6},{8,9},{9,8},{10,11... | collective-permute-start | bytes 786440 | tf_op jit(solution)/shard_map/ppermute | solution.py:30
  10.5 17.9 %all-to-all-start = ((bf16[16,34,512]{2,1,0:T(8,128)(2,1)}), bf16[16,34,512]{2,1,0:T(8,128)(2,1)S(1)}, u32[]{:S(2)}, u32[]{:S(2)}) async-start(bf16[16,34,512]{2,1,0:T(8,128)(2,1)} %broadcast_dynamic-update-slice_fusion), calls=%async_computation | async-start | bytes 1310720 | tf_op jit(solution)/shard_map/all_to_all | solution.py:338

commit v8 on v7

--- a/solution.py
+++ b/solution.py
@@ -327,13 +327,13 @@
         spread = jnp.concatenate([spread, swap(spread, level)], axis=0)
         level *= 2
     spread = spread[blocks:]
-    inner = swap(inner, 1)
     payload = jnp.pad(mid, ((0, spread.shape[0]), (0, 0)))
     payload = lax.optimization_barrier(jnp.broadcast_to(payload[None], (GROUP, *payload.shape)))
     links = [(i, i + 1) for i in range(1, devices - 1, 2)]
     outer = lax.ppermute(tied(outer, payload), "seq", links + [(b, a) for a, b in links])
     late = jnp.broadcast_to(spread[None], (GROUP, *spread.shape))
     payload = lax.dynamic_update_slice(payload, late, (0, per_device, 0))
+    inner = swap(tied(inner, payload), 1)
     members = [list(range(at, at + GROUP)) for at in range(0, devices, GROUP)]
     arrived = lax.all_to_all(payload, "seq", 0, 0, axis_index_groups=members)
 

time: 37.3 us -> 36.5 us (0.979)
  local copies, waits for them, and re-layouts: 1.57 us -> 0.97 us
    broadcast_in_dim x1, local copies, waits for them, and re-layouts: 0.88 us -> 0.05 us  [body(): jnp.broadcast_to(payload[None], (GROUP, *payload.shape))]
    unnamed x2 -> x4, local copies, waits for them, and re-layouts: 0.01 us -> 0.84 us
    dynamic_update_slice x1, local copies, waits for them, and re-layouts: 0.64 us -> 0.05 us  [body(): payload = lax.dynamic_update_slice(payload, late, (0, per_device, 0))]
  transfers between devices with their start and end apart: 4 -> 4, of which waited for: 1 -> 1; matrix products, arithmetic and copies ran while one was open for 4% -> 0% of each run, Pallas kernels for 31% -> 32%
where the time goes in v8:
time: 36.5 us; the launch traced here: 36.2 us
  Pallas kernels  22.6 us (62%)
  starting transfers between devices  10.7 us (29%)
  waiting for transfers between devices  1.81 us (5%)
  local copies, waits for them, and re-layouts  0.97 us (3%)
    pallas_call x1, Pallas kernels, body(): call(near, state, [VMEM, HBM, VMEM, VMEM, VMEM], [HBM] * 3, [pltpu.VMEM((...  11.5 us
    pallas_call x1, Pallas kernels, body(): call(far, shape((rows, w_out.shape[1]), BF16), [HBM] * 3 + [VMEM, VMEM, H...  8.62 us
    all_to_all x1, starting transfers between devices, body(): arrived = lax.all_to_all(payload, 'seq', 0, 0, axis_index_groups=members)  4.39 us
    ppermute x1, starting transfers between devices, body(): lax.ppermute(tied(outer, payload), 'seq', links + [(b, a) for a, b in lin...  3.96 us
    pallas_call x1, Pallas kernels, body(): call(project_pair, [shape((rows, 2 * width), BF16), shape((per_device, 2...  2.52 us
    ppermute x2, starting transfers between devices, swap(): return lax.ppermute(rows, 'seq', [(i, i ^ apart) for i in range(count)])  2.38 us
    ppermute x1, waiting for transfers between devices, body(): lax.ppermute(tied(outer, payload), 'seq', links + [(b, a) for a, b in lin...  1.81 us
    unnamed x4, local copies, waits for them, and re-layouts  0.84 us
  transfers between devices with their start and end apart: 4, of which 1 were waited for; matrix products, arithmetic and copies ran while one was open for 0% of the time, Pallas kernels for 32%

profile of v8, /device:TPU:11, one launch (start us, length us, event | category | flops | bytes accessed | tf_op | source)
XLA Modules:
  0.0 36.2 jit_solution(4311938953746770521)
XLA Ops:
  0.0 2.5 %pair.1 = (bf16[512,512]{1,0:T(8,128)(2,1)S(1)}, bf16[32,512]{1,0:T(8,128)(2,1)S(1)}, bf16[2,512]{1,0:T(2,128)(2,1)S(1)}, bf16[256,512]{1,0:T(8,128)(2,1)S(1)}, bf16[256,512]{1,0:T(8,128)(2,1)S(1)}) custom-call(bf16[512,1024]{1,0:T(8,128)(2,1)} %tokens_ref.1, bf16[1024,256]{1,0:T(8,128)(2,1)} %wk_hbm.1, bf16[1024,256]{1,0:T(8,128)(2,1)} %wv_hbm.1), custom_call_target="tpu_custom_call" | custom-call | flops 2000000000 | bytes 1048576 | tf_op jit(solution)/shard_map/pair/pallas_call | solution.py:311
  2.5 0.0 copy-start
  2.5 2.4 %collective-permute-start = (bf16[2,512]{1,0:T(2,128)(2,1)S(1)}, bf16[2,512]{1,0:T(2,128)(2,1)S(1)}, u32[]{:S(2)}, u32[]{:S(2)}) collective-permute-start(bf16[2,512]{1,0:T(2,128)(2,1)S(1)} %get-tuple-element.18), channel_id=1, source_target_pairs={{0,16},{1,17},{2,18},{3,19},{4,20},{5,21},{6,22},{7,23},{8,24},{9,... | collective-permute-start | bytes 6152 | tf_op jit(solution)/shard_map/ppermute | solution.py:30
  5.0 4.0 %collective-permute-start.2 = (bf16[256,512]{1,0:T(8,128)(2,1)S(1)}, bf16[256,512]{1,0:T(8,128)(2,1)S(1)}, u32[]{:S(2)}, u32[]{:S(2)}) collective-permute-start(bf16[256,512]{1,0:T(8,128)(2,1)S(1)} %get-tuple-element.23), channel_id=1, source_target_pairs={{1,2},{3,4},{5,6},{7,8},{9,10},{11,12},{13,14},{15,16},{17,18},{19... | collective-permute-start | bytes 786440 | tf_op jit(solution)/shard_map/ppermute | solution.py:333
  8.9 0.0 collective-permute-done
  9.0 0.0 copy-start.1
  9.0 0.8 %copy-done.1 = bf16[16,34,512]{2,1,0:T(8,128)(2,1)} copy-done((bf16[16,34,512]{2,1,0:T(8,128)(2,1)}, bf16[16,34,512]{2,1,0:T(8,128)(2,1)S(1)}, u32[]{:S(2)}) %copy-start.1) | copy-done | bytes 557080
  9.8 0.0 collective-permute-start.1
  9.8 4.4 %all-to-all-start = ((bf16[16,34,512]{2,1,0:T(8,128)(2,1)}), bf16[16,34,512]{2,1,0:T(8,128)(2,1)S(1)}, u32[]{:S(2)}, u32[]{:S(2)}) async-start(bf16[16,34,512]{2,1,0:T(8,128)(2,1)} %copy-done.1), calls=%async_computation | async-start | bytes 1310720 | tf_op jit(solution)/shard_map/all_to_all | solution.py:338
  14.2 1.8 %collective-permute-done.2.outer_ref = bf16[256,512]{1,0:T(8,128)(2,1)S(1)} collective-permute-done((bf16[256,512]{1,0:T(8,128)(2,1)S(1)}, bf16[256,512]{1,0:T(8,128)(2,1)S(1)}, u32[]{:S(2)}, u32[]{:S(2)}) %collective-permute-start.2) | collective-permute-done | bytes 262176 | tf_op jit(solution)/shard_map/ppermute | solution.py:333
  16.0 0.0 collective-permute-done.1.inner_ref
  16.0 0.0 copy-done
  16.0 11.5 %near.1 = (bf16[4,2,1024,128]{3,2,1,0:T(8,128)(2,1)}, f32[4,2,80,1024]{3,2,1,0:T(8,128)}, f32[4,2,1,1024]{3,2,1,0:T(1,128)S(1)}) custom-call(bf16[512,1024]{1,0:T(8,128)(2,1)S(1)} %copy-done, bf16[1024,1024]{1,0:T(8,128)(2,1)} %wq_hbm.1, bf16[512,512]{1,0:T(8,128)(2,1)S(1)} %get-tuple-element.19.pair_ref, ...), custom_call_target="tpu_custom_call" | custom-call | flops 10000000000 | bytes 1048576 | tf_op jit(solution)/shard_map/near/pallas_call | solution.py:340
  27.6 0.0 all-to-all-done.mids_ref
  27.6 8.6 %far.1 = bf16[512,1024]{1,0:T(8,128)(2,1)} custom-call(bf16[4,2,1024,128]{3,2,1,0:T(8,128)(2,1)} %get-tuple-element.24.q_hbm, f32[4,2,80,1024]{3,2,1,0:T(8,128)} %get-tuple-element.25.acc_hbm, f32[4,2,1,1024]{3,2,1,0:T(1,128)S(1)} %get-tuple-element.26.top_hbm, bf16[16,34,512]{2,1,0:T(8,128)(2,1)S(1)} %all-to-all-done.mids_ref, ...), custom_call_target="tpu_custom_call" | custom-call | flops 8000000000 | bytes 1048576 | tf_op jit(solution)/shard_map/far/pallas_call | solution.py:355
  (5 shorter events, 0.1 us)
Async XLA Ops:
  2.5 13.5 %copy-start = (bf16[512,1024]{1,0:T(8,128)(2,1)S(1)}, bf16[512,1024]{1,0:T(8,128)(2,1)}, u32[]{:S(2)}) copy-start(bf16[512,1024]{1,0:T(8,128)(2,1)} %tokens_ref.1) | copy-start | bytes 3145732
  2.5 6.4 %collective-permute-start = (bf16[2,512]{1,0:T(2,128)(2,1)S(1)}, bf16[2,512]{1,0:T(2,128)(2,1)S(1)}, u32[]{:S(2)}, u32[]{:S(2)}) collective-permute-start(bf16[2,512]{1,0:T(2,128)(2,1)S(1)} %get-tuple-element.18), channel_id=1, source_target_pairs={{0,16},{1,17},{2,18},{3,19},{4,20},{5,21},{6,22},{7,23},{8,24},{9,... | collective-permute-start | bytes 6152 | tf_op jit(solution)/shard_map/ppermute | solution.py:30
  5.0 11.1 %collective-permute-start.2 = (bf16[256,512]{1,0:T(8,128)(2,1)S(1)}, bf16[256,512]{1,0:T(8,128)(2,1)S(1)}, u32[]{:S(2)}, u32[]{:S(2)}) collective-permute-start(bf16[256,512]{1,0:T(8,128)(2,1)S(1)} %get-tuple-element.23), channel_id=1, source_target_pairs={{1,2},{3,4},{5,6},{7,8},{9,10},{11,12},{13,14},{15,16},{17,18},{19... | collective-permute-start | bytes 786440 | tf_op jit(solution)/shard_map/ppermute | solution.py:333
  9.0 0.8 %copy-start.1 = (bf16[16,34,512]{2,1,0:T(8,128)(2,1)}, bf16[16,34,512]{2,1,0:T(8,128)(2,1)S(1)}, u32[]{:S(2)}) copy-start(bf16[16,34,512]{2,1,0:T(8,128)(2,1)S(1)} %broadcast_dynamic-update-slice_fusion) | copy-start | bytes 1671172
  9.8 6.2 %collective-permute-start.1 = (bf16[256,512]{1,0:T(8,128)(2,1)S(1)}, bf16[256,512]{1,0:T(8,128)(2,1)S(1)}, u32[]{:S(2)}, u32[]{:S(2)}) collective-permute-start(bf16[256,512]{1,0:T(8,128)(2,1)S(1)} %get-tuple-element.21), channel_id=1, source_target_pairs={{0,1},{1,0},{2,3},{3,2},{4,5},{5,4},{6,7},{7,6},{8,9},{9,8},{10,11... | collective-permute-start | bytes 786440 | tf_op jit(solution)/shard_map/ppermute | solution.py:30
  9.8 17.7 %all-to-all-start = ((bf16[16,34,512]{2,1,0:T(8,128)(2,1)}), bf16[16,34,512]{2,1,0:T(8,128)(2,1)S(1)}, u32[]{:S(2)}, u32[]{:S(2)}) async-start(bf16[16,34,512]{2,1,0:T(8,128)(2,1)} %copy-done.1), calls=%async_computation | async-start | bytes 1310720 | tf_op jit(solution)/shard_map/all_to_all | solution.py:338

commit v9 on v8

--- a/solution.py
+++ b/solution.py
@@ -38,11 +38,13 @@
     rows = tokens_ref.shape[0]
     width = wk_hbm.shape[1]
     blocks = rows // BLOCK
-    fetches = [pltpu.make_async_copy(wk_hbm, weight_ref.at[:, pl.ds(0, width)], sems.at[0])]
-    fetches.append(pltpu.make_async_copy(wv_hbm, weight_ref.at[:, pl.ds(width, width)], sems.at[1]))
-    for block in range(blocks):
-        at = pl.ds(block * BLOCK, BLOCK)
-        fetches.append(pltpu.make_async_copy(tokens_hbm.at[at], tokens_ref.at[at], sems.at[2 + block]))
+    depth = tokens_ref.shape[1] // 2
+    fetches = []
+    for part in range(2):
+        at = pl.ds(part * depth, depth)
+        fetches.append(pltpu.make_async_copy(wk_hbm.at[at], weight_ref.at[at, pl.ds(0, width)], sems.at[3 * part]))
+        fetches.append(pltpu.make_async_copy(wv_hbm.at[at], weight_ref.at[at, pl.ds(width, width)], sems.at[3 * part + 1]))
+        fetches.append(pltpu.make_async_copy(tokens_hbm.at[:, at], tokens_ref.at[:, at], sems.at[3 * part + 2]))
     for fetch in fetches:
         fetch.start()
     even = lax.axis_index("seq") % 2 == 0
@@ -52,13 +54,17 @@
     column = lax.broadcasted_iota(jnp.int32, (tall, BLOCK), 1)
     share = jnp.where(row < runs, jnp.where(column // POOL == row, 1.0 / POOL, 0.0), jnp.where(row == runs, 1.0 / BLOCK, 0.0))
     share = share.astype(BF16)
-    fetches[0].wait()
-    fetches[1].wait()
+    total = None
+    for part in range(2):
+        for fetch in fetches[3 * part : 3 * part + 3]:
+            fetch.wait()
+        at = slice(part * depth, (part + 1) * depth)
+        product = jnp.dot(tokens_ref[:, at], weight_ref[at], preferred_element_type=F32)
+        total = product if total is None else total + product
     kept = []
     for block in range(blocks):
         at = slice(block * BLOCK, (block + 1) * BLOCK)
-        fetches[2 + block].wait()
-        held = jnp.dot(tokens_ref[at], weight_ref[...], preferred_element_type=F32).astype(BF16)
+        held = total[at].astype(BF16)
         pair_ref[at] = held
         kept.append(held)
         mean = jnp.dot(share, held, preferred_element_type=F32)
@@ -313,7 +319,7 @@
         [shape((rows, 2 * width), BF16), shape((per_device, 2 * width), BF16), shape((blocks, 2 * width), BF16), half, half],
         [HBM] * 3,
         [VMEM] * 5,
-        [pltpu.VMEM((rows, model), BF16), pltpu.VMEM((model, 2 * width), BF16), dma((2 + blocks,))],
+        [pltpu.VMEM((rows, model), BF16), pltpu.VMEM((model, 2 * width), BF16), dma((6,))],
         2 * 10**9,
         "pair",
         54000,

time: 36.5 us -> 36.4 us (level)
  the two profiles are of different devices: /device:TPU:11 before, /device:TPU:3 now
where the time goes in v9:
time: 36.4 us; the launch traced here: 36.2 us
  Pallas kernels  22.5 us (62%)
  starting transfers between devices  10.8 us (30%)
  waiting for transfers between devices  1.71 us (5%)
  local copies, waits for them, and re-layouts  0.97 us (3%)
    pallas_call x1, Pallas kernels, body(): call(near, state, [VMEM, HBM, VMEM, VMEM, VMEM], [HBM] * 3, [pltpu.VMEM((...  11.5 us
    pallas_call x1, Pallas kernels, body(): call(far, shape((rows, w_out.shape[1]), BF16), [HBM] * 3 + [VMEM, VMEM, H...  8.62 us
    all_to_all x1, starting transfers between devices, body(): arrived = lax.all_to_all(payload, 'seq', 0, 0, axis_index_groups=members)  4.5 us
    ppermute x1, starting transfers between devices, body(): lax.ppermute(tied(outer, payload), 'seq', links + [(b, a) for a, b in lin...  3.96 us
    pallas_call x1, Pallas kernels, body(): call(project_pair, [shape((rows, 2 * width), BF16), shape((per_device, 2...  2.42 us
    ppermute x2, starting transfers between devices, swap(): return lax.ppermute(rows, 'seq', [(i, i ^ apart) for i in range(count)])  2.38 us
    ppermute x1, waiting for transfers between devices, body(): lax.ppermute(tied(outer, payload), 'seq', links + [(b, a) for a, b in lin...  1.7 us
    unnamed x4, local copies, waits for them, and re-layouts  0.84 us
  transfers between devices with their start and end apart: 4, of which 1 were waited for; matrix products, arithmetic and copies ran while one was open for 0% of the time, Pallas kernels for 32%

profile of v9, /device:TPU:3, one launch (start us, length us, event | category | flops | bytes accessed | tf_op | source)
XLA Modules:
  0.0 36.2 jit_solution(16982744021210466629)
XLA Ops:
  0.0 2.4 %pair.1 = (bf16[512,512]{1,0:T(8,128)(2,1)S(1)}, bf16[32,512]{1,0:T(8,128)(2,1)S(1)}, bf16[2,512]{1,0:T(2,128)(2,1)S(1)}, bf16[256,512]{1,0:T(8,128)(2,1)S(1)}, bf16[256,512]{1,0:T(8,128)(2,1)S(1)}) custom-call(bf16[512,1024]{1,0:T(8,128)(2,1)} %tokens_ref.1, bf16[1024,256]{1,0:T(8,128)(2,1)} %wk_hbm.1, bf16[1024,256]{1,0:T(8,128)(2,1)} %wv_hbm.1), custom_call_target="tpu_custom_call" | custom-call | flops 2000000000 | bytes 1048576 | tf_op jit(solution)/shard_map/pair/pallas_call | solution.py:317
  2.4 0.0 copy-start
  2.4 2.4 %collective-permute-start = (bf16[2,512]{1,0:T(2,128)(2,1)S(1)}, bf16[2,512]{1,0:T(2,128)(2,1)S(1)}, u32[]{:S(2)}, u32[]{:S(2)}) collective-permute-start(bf16[2,512]{1,0:T(2,128)(2,1)S(1)} %get-tuple-element.18), channel_id=1, source_target_pairs={{0,16},{1,17},{2,18},{3,19},{4,20},{5,21},{6,22},{7,23},{8,24},{9,... | collective-permute-start | bytes 6152 | tf_op jit(solution)/shard_map/ppermute | solution.py:30
  4.9 4.0 %collective-permute-start.2 = (bf16[256,512]{1,0:T(8,128)(2,1)S(1)}, bf16[256,512]{1,0:T(8,128)(2,1)S(1)}, u32[]{:S(2)}, u32[]{:S(2)}) collective-permute-start(bf16[256,512]{1,0:T(8,128)(2,1)S(1)} %get-tuple-element.23), channel_id=1, source_target_pairs={{1,2},{3,4},{5,6},{7,8},{9,10},{11,12},{13,14},{15,16},{17,18},{19... | collective-permute-start | bytes 786440 | tf_op jit(solution)/shard_map/ppermute | solution.py:339
  8.8 0.0 collective-permute-done
  8.9 0.0 copy-start.1
  8.9 0.8 %copy-done.1 = bf16[16,34,512]{2,1,0:T(8,128)(2,1)} copy-done((bf16[16,34,512]{2,1,0:T(8,128)(2,1)}, bf16[16,34,512]{2,1,0:T(8,128)(2,1)S(1)}, u32[]{:S(2)}) %copy-start.1) | copy-done | bytes 557080
  9.7 0.0 collective-permute-start.1
  9.7 4.5 %all-to-all-start = ((bf16[16,34,512]{2,1,0:T(8,128)(2,1)}), bf16[16,34,512]{2,1,0:T(8,128)(2,1)S(1)}, u32[]{:S(2)}, u32[]{:S(2)}) async-start(bf16[16,34,512]{2,1,0:T(8,128)(2,1)} %copy-done.1), calls=%async_computation | async-start | bytes 1310720 | tf_op jit(solution)/shard_map/all_to_all | solution.py:344
  14.2 1.7 %collective-permute-done.2.outer_ref = bf16[256,512]{1,0:T(8,128)(2,1)S(1)} collective-permute-done((bf16[256,512]{1,0:T(8,128)(2,1)S(1)}, bf16[256,512]{1,0:T(8,128)(2,1)S(1)}, u32[]{:S(2)}, u32[]{:S(2)}) %collective-permute-start.2) | collective-permute-done | bytes 262176 | tf_op jit(solution)/shard_map/ppermute | solution.py:339
  15.9 0.0 collective-permute-done.1.inner_ref
  15.9 0.0 copy-done
  15.9 11.5 %near.1 = (bf16[4,2,1024,128]{3,2,1,0:T(8,128)(2,1)}, f32[4,2,80,1024]{3,2,1,0:T(8,128)}, f32[4,2,1,1024]{3,2,1,0:T(1,128)S(1)}) custom-call(bf16[512,1024]{1,0:T(8,128)(2,1)S(1)} %copy-done, bf16[1024,1024]{1,0:T(8,128)(2,1)} %wq_hbm.1, bf16[512,512]{1,0:T(8,128)(2,1)S(1)} %get-tuple-element.19.pair_ref, ...), custom_call_target="tpu_custom_call" | custom-call | flops 10000000000 | bytes 1048576 | tf_op jit(solution)/shard_map/near/pallas_call | solution.py:346
  27.5 0.0 all-to-all-done.mids_ref
  27.5 8.6 %far.1 = bf16[512,1024]{1,0:T(8,128)(2,1)} custom-call(bf16[4,2,1024,128]{3,2,1,0:T(8,128)(2,1)} %get-tuple-element.24.q_hbm, f32[4,2,80,1024]{3,2,1,0:T(8,128)} %get-tuple-element.25.acc_hbm, f32[4,2,1,1024]{3,2,1,0:T(1,128)S(1)} %get-tuple-element.26.top_hbm, bf16[16,34,512]{2,1,0:T(8,128)(2,1)S(1)} %all-to-all-done.mids_ref, ...), custom_call_target="tpu_custom_call" | custom-call | flops 8000000000 | bytes 1048576 | tf_op jit(solution)/shard_map/far/pallas_call | solution.py:361
  (5 shorter events, 0.1 us)
Async XLA Ops:
  2.4 13.5 %copy-start = (bf16[512,1024]{1,0:T(8,128)(2,1)S(1)}, bf16[512,1024]{1,0:T(8,128)(2,1)}, u32[]{:S(2)}) copy-start(bf16[512,1024]{1,0:T(8,128)(2,1)} %tokens_ref.1) | copy-start | bytes 3145732
  2.4 6.4 %collective-permute-start = (bf16[2,512]{1,0:T(2,128)(2,1)S(1)}, bf16[2,512]{1,0:T(2,128)(2,1)S(1)}, u32[]{:S(2)}, u32[]{:S(2)}) collective-permute-start(bf16[2,512]{1,0:T(2,128)(2,1)S(1)} %get-tuple-element.18), channel_id=1, source_target_pairs={{0,16},{1,17},{2,18},{3,19},{4,20},{5,21},{6,22},{7,23},{8,24},{9,... | collective-permute-start | bytes 6152 | tf_op jit(solution)/shard_map/ppermute | solution.py:30
  4.9 11.1 %collective-permute-start.2 = (bf16[256,512]{1,0:T(8,128)(2,1)S(1)}, bf16[256,512]{1,0:T(8,128)(2,1)S(1)}, u32[]{:S(2)}, u32[]{:S(2)}) collective-permute-start(bf16[256,512]{1,0:T(8,128)(2,1)S(1)} %get-tuple-element.23), channel_id=1, source_target_pairs={{1,2},{3,4},{5,6},{7,8},{9,10},{11,12},{13,14},{15,16},{17,18},{19... | collective-permute-start | bytes 786440 | tf_op jit(solution)/shard_map/ppermute | solution.py:339
  8.9 0.8 %copy-start.1 = (bf16[16,34,512]{2,1,0:T(8,128)(2,1)}, bf16[16,34,512]{2,1,0:T(8,128)(2,1)S(1)}, u32[]{:S(2)}) copy-start(bf16[16,34,512]{2,1,0:T(8,128)(2,1)S(1)} %broadcast_dynamic-update-slice_fusion) | copy-start | bytes 1671172
  9.7 6.2 %collective-permute-start.1 = (bf16[256,512]{1,0:T(8,128)(2,1)S(1)}, bf16[256,512]{1,0:T(8,128)(2,1)S(1)}, u32[]{:S(2)}, u32[]{:S(2)}) collective-permute-start(bf16[256,512]{1,0:T(8,128)(2,1)S(1)} %get-tuple-element.21), channel_id=1, source_target_pairs={{0,1},{1,0},{2,3},{3,2},{4,5},{5,4},{6,7},{7,6},{8,9},{9,8},{10,11... | collective-permute-start | bytes 786440 | tf_op jit(solution)/shard_map/ppermute | solution.py:30
  9.7 17.7 %all-to-all-start = ((bf16[16,34,512]{2,1,0:T(8,128)(2,1)}), bf16[16,34,512]{2,1,0:T(8,128)(2,1)S(1)}, u32[]{:S(2)}, u32[]{:S(2)}) async-start(bf16[16,34,512]{2,1,0:T(8,128)(2,1)} %copy-done.1), calls=%async_computation | async-start | bytes 1310720 | tf_op jit(solution)/shard_map/all_to_all | solution.py:344

commit v10 on v9

--- a/solution.py
+++ b/solution.py
@@ -38,9 +38,9 @@
     rows = tokens_ref.shape[0]
     width = wk_hbm.shape[1]
     blocks = rows // BLOCK
-    depth = tokens_ref.shape[1] // 2
+    depth = tokens_ref.shape[1] // 4
     fetches = []
-    for part in range(2):
+    for part in range(4):
         at = pl.ds(part * depth, depth)
         fetches.append(pltpu.make_async_copy(wk_hbm.at[at], weight_ref.at[at, pl.ds(0, width)], sems.at[3 * part]))
         fetches.append(pltpu.make_async_copy(wv_hbm.at[at], weight_ref.at[at, pl.ds(width, width)], sems.at[3 * part + 1]))
@@ -55,7 +55,7 @@
     share = jnp.where(row < runs, jnp.where(column // POOL == row, 1.0 / POOL, 0.0), jnp.where(row == runs, 1.0 / BLOCK, 0.0))
     share = share.astype(BF16)
     total = None
-    for part in range(2):
+    for part in range(4):
         for fetch in fetches[3 * part : 3 * part + 3]:
             fetch.wait()
         at = slice(part * depth, (part + 1) * depth)
@@ -319,7 +319,7 @@
         [shape((rows, 2 * width), BF16), shape((per_device, 2 * width), BF16), shape((blocks, 2 * width), BF16), half, half],
         [HBM] * 3,
         [VMEM] * 5,
-        [pltpu.VMEM((rows, model), BF16), pltpu.VMEM((model, 2 * width), BF16), dma((6,))],
+        [pltpu.VMEM((rows, model), BF16), pltpu.VMEM((model, 2 * width), BF16), dma((12,))],
         2 * 10**9,
         "pair",
         54000,

time: 36.4 us -> 36.3 us (level)
  the two profiles are of different devices: /device:TPU:3 before, /device:TPU:11 now
where the time goes in v10:
time: 36.3 us; the launch traced here: 36 us
  Pallas kernels  22.4 us (62%)
  starting transfers between devices  10.7 us (29%)
  waiting for transfers between devices  1.81 us (5%)
  local copies, waits for them, and re-layouts  0.97 us (3%)
    pallas_call x1, Pallas kernels, body(): call(near, state, [VMEM, HBM, VMEM, VMEM, VMEM], [HBM] * 3, [pltpu.VMEM((...  11.5 us
    pallas_call x1, Pallas kernels, body(): call(far, shape((rows, w_out.shape[1]), BF16), [HBM] * 3 + [VMEM, VMEM, H...  8.63 us
    all_to_all x1, starting transfers between devices, body(): arrived = lax.all_to_all(payload, 'seq', 0, 0, axis_index_groups=members)  4.4 us
    ppermute x1, starting transfers between devices, body(): lax.ppermute(tied(outer, payload), 'seq', links + [(b, a) for a, b in lin...  3.96 us
    ppermute x2, starting transfers between devices, swap(): return lax.ppermute(rows, 'seq', [(i, i ^ apart) for i in range(count)])  2.37 us
    pallas_call x1, Pallas kernels, body(): call(project_pair, [shape((rows, 2 * width), BF16), shape((per_device, 2...  2.29 us
    ppermute x1, waiting for transfers between devices, body(): lax.ppermute(tied(outer, payload), 'seq', links + [(b, a) for a, b in lin...  1.8 us
    unnamed x4, local copies, waits for them, and re-layouts  0.84 us
  transfers between devices with their start and end apart: 4, of which 1 were waited for; matrix products, arithmetic and copies ran while one was open for 0% of the time, Pallas kernels for 32%

profile of v10, /device:TPU:11, one launch (start us, length us, event | category | flops | bytes accessed | tf_op | source)
XLA Modules:
  0.0 36.0 jit_solution(6179194314497130912)
XLA Ops:
  0.0 2.3 %pair.1 = (bf16[512,512]{1,0:T(8,128)(2,1)S(1)}, bf16[32,512]{1,0:T(8,128)(2,1)S(1)}, bf16[2,512]{1,0:T(2,128)(2,1)S(1)}, bf16[256,512]{1,0:T(8,128)(2,1)S(1)}, bf16[256,512]{1,0:T(8,128)(2,1)S(1)}) custom-call(bf16[512,1024]{1,0:T(8,128)(2,1)} %tokens_ref.1, bf16[1024,256]{1,0:T(8,128)(2,1)} %wk_hbm.1, bf16[1024,256]{1,0:T(8,128)(2,1)} %wv_hbm.1), custom_call_target="tpu_custom_call" | custom-call | flops 2000000000 | bytes 1048576 | tf_op jit(solution)/shard_map/pair/pallas_call | solution.py:317
  2.3 0.0 copy-start
  2.3 2.4 %collective-permute-start = (bf16[2,512]{1,0:T(2,128)(2,1)S(1)}, bf16[2,512]{1,0:T(2,128)(2,1)S(1)}, u32[]{:S(2)}, u32[]{:S(2)}) collective-permute-start(bf16[2,512]{1,0:T(2,128)(2,1)S(1)} %get-tuple-element.18), channel_id=1, source_target_pairs={{0,16},{1,17},{2,18},{3,19},{4,20},{5,21},{6,22},{7,23},{8,24},{9,... | collective-permute-start | bytes 6152 | tf_op jit(solution)/shard_map/ppermute | solution.py:30
  4.7 4.0 %collective-permute-start.2 = (bf16[256,512]{1,0:T(8,128)(2,1)S(1)}, bf16[256,512]{1,0:T(8,128)(2,1)S(1)}, u32[]{:S(2)}, u32[]{:S(2)}) collective-permute-start(bf16[256,512]{1,0:T(8,128)(2,1)S(1)} %get-tuple-element.23), channel_id=1, source_target_pairs={{1,2},{3,4},{5,6},{7,8},{9,10},{11,12},{13,14},{15,16},{17,18},{19... | collective-permute-start | bytes 786440 | tf_op jit(solution)/shard_map/ppermute | solution.py:339
  8.7 0.0 collective-permute-done
  8.8 0.0 copy-start.1
  8.8 0.8 %copy-done.1 = bf16[16,34,512]{2,1,0:T(8,128)(2,1)} copy-done((bf16[16,34,512]{2,1,0:T(8,128)(2,1)}, bf16[16,34,512]{2,1,0:T(8,128)(2,1)S(1)}, u32[]{:S(2)}) %copy-start.1) | copy-done | bytes 557080
  9.6 0.0 collective-permute-start.1
  9.6 4.4 %all-to-all-start = ((bf16[16,34,512]{2,1,0:T(8,128)(2,1)}), bf16[16,34,512]{2,1,0:T(8,128)(2,1)S(1)}, u32[]{:S(2)}, u32[]{:S(2)}) async-start(bf16[16,34,512]{2,1,0:T(8,128)(2,1)} %copy-done.1), calls=%async_computation | async-start | bytes 1310720 | tf_op jit(solution)/shard_map/all_to_all | solution.py:344
  14.0 1.8 %collective-permute-done.2.outer_ref = bf16[256,512]{1,0:T(8,128)(2,1)S(1)} collective-permute-done((bf16[256,512]{1,0:T(8,128)(2,1)S(1)}, bf16[256,512]{1,0:T(8,128)(2,1)S(1)}, u32[]{:S(2)}, u32[]{:S(2)}) %collective-permute-start.2) | collective-permute-done | bytes 262176 | tf_op jit(solution)/shard_map/ppermute | solution.py:339
  15.8 0.0 collective-permute-done.1.inner_ref
  15.8 0.0 copy-done
  15.8 11.5 %near.1 = (bf16[4,2,1024,128]{3,2,1,0:T(8,128)(2,1)}, f32[4,2,80,1024]{3,2,1,0:T(8,128)}, f32[4,2,1,1024]{3,2,1,0:T(1,128)S(1)}) custom-call(bf16[512,1024]{1,0:T(8,128)(2,1)S(1)} %copy-done, bf16[1024,1024]{1,0:T(8,128)(2,1)} %wq_hbm.1, bf16[512,512]{1,0:T(8,128)(2,1)S(1)} %get-tuple-element.19.pair_ref, ...), custom_call_target="tpu_custom_call" | custom-call | flops 10000000000 | bytes 1048576 | tf_op jit(solution)/shard_map/near/pallas_call | solution.py:346
  27.3 0.0 all-to-all-done.mids_ref
  27.4 8.6 %far.1 = bf16[512,1024]{1,0:T(8,128)(2,1)} custom-call(bf16[4,2,1024,128]{3,2,1,0:T(8,128)(2,1)} %get-tuple-element.24.q_hbm, f32[4,2,80,1024]{3,2,1,0:T(8,128)} %get-tuple-element.25.acc_hbm, f32[4,2,1,1024]{3,2,1,0:T(1,128)S(1)} %get-tuple-element.26.top_hbm, bf16[16,34,512]{2,1,0:T(8,128)(2,1)S(1)} %all-to-all-done.mids_ref, ...), custom_call_target="tpu_custom_call" | custom-call | flops 8000000000 | bytes 1048576 | tf_op jit(solution)/shard_map/far/pallas_call | solution.py:361
  (5 shorter events, 0.1 us)
Async XLA Ops:
  2.3 13.5 %copy-start = (bf16[512,1024]{1,0:T(8,128)(2,1)S(1)}, bf16[512,1024]{1,0:T(8,128)(2,1)}, u32[]{:S(2)}) copy-start(bf16[512,1024]{1,0:T(8,128)(2,1)} %tokens_ref.1) | copy-start | bytes 3145732
  2.3 6.4 %collective-permute-start = (bf16[2,512]{1,0:T(2,128)(2,1)S(1)}, bf16[2,512]{1,0:T(2,128)(2,1)S(1)}, u32[]{:S(2)}, u32[]{:S(2)}) collective-permute-start(bf16[2,512]{1,0:T(2,128)(2,1)S(1)} %get-tuple-element.18), channel_id=1, source_target_pairs={{0,16},{1,17},{2,18},{3,19},{4,20},{5,21},{6,22},{7,23},{8,24},{9,... | collective-permute-start | bytes 6152 | tf_op jit(solution)/shard_map/ppermute | solution.py:30
  4.7 11.1 %collective-permute-start.2 = (bf16[256,512]{1,0:T(8,128)(2,1)S(1)}, bf16[256,512]{1,0:T(8,128)(2,1)S(1)}, u32[]{:S(2)}, u32[]{:S(2)}) collective-permute-start(bf16[256,512]{1,0:T(8,128)(2,1)S(1)} %get-tuple-element.23), channel_id=1, source_target_pairs={{1,2},{3,4},{5,6},{7,8},{9,10},{11,12},{13,14},{15,16},{17,18},{19... | collective-permute-start | bytes 786440 | tf_op jit(solution)/shard_map/ppermute | solution.py:339
  8.8 0.8 %copy-start.1 = (bf16[16,34,512]{2,1,0:T(8,128)(2,1)}, bf16[16,34,512]{2,1,0:T(8,128)(2,1)S(1)}, u32[]{:S(2)}) copy-start(bf16[16,34,512]{2,1,0:T(8,128)(2,1)S(1)} %broadcast_dynamic-update-slice_fusion) | copy-start | bytes 1671172
  9.6 6.2 %collective-permute-start.1 = (bf16[256,512]{1,0:T(8,128)(2,1)S(1)}, bf16[256,512]{1,0:T(8,128)(2,1)S(1)}, u32[]{:S(2)}, u32[]{:S(2)}) collective-permute-start(bf16[256,512]{1,0:T(8,128)(2,1)S(1)} %get-tuple-element.21), channel_id=1, source_target_pairs={{0,1},{1,0},{2,3},{3,2},{4,5},{5,4},{6,7},{7,6},{8,9},{9,8},{10,11... | collective-permute-start | bytes 786440 | tf_op jit(solution)/shard_map/ppermute | solution.py:30
  9.6 17.7 %all-to-all-start = ((bf16[16,34,512]{2,1,0:T(8,128)(2,1)}), bf16[16,34,512]{2,1,0:T(8,128)(2,1)S(1)}, u32[]{:S(2)}, u32[]{:S(2)}) async-start(bf16[16,34,512]{2,1,0:T(8,128)(2,1)} %copy-done.1), calls=%async_computation | async-start | bytes 1310720 | tf_op jit(solution)/shard_map/all_to_all | solution.py:344
